TPU v7x, 256 devices: a whole 4x4x8 slice. The times are simulated.
256 devices in a mesh: grp: 8 (over y, core), spl: 32 (over x, z).
Axes of the slice: x: 4, y: 4, z: 8, core: 2. Of those that a mesh axis runs over, the one named last changes fastest.
Arguments:
- slater: float32 [80, 5, 128, 128], P('grp', None, 'spl'), may hold values from -6 to 6
- couple_type: int32 [16384, 8], P('grp'), may hold values from 0 to 79
- couple_multipole: int32 [16384, 8], P('grp'), may hold values from 0 to 4
- couple_angle: int32 [16384, 8], P('grp'), may hold values from 0 to 63
- angular: float32 [64], replicated, may hold values from -1 to 1
- owner_map: int32 [16384], P('grp'), may hold values from 0 to 31, as said below
Outputs:
- hamiltonian: float32 [32768, 128, 128], P(('grp', 'spl'))
Inputs may be any that keep to these rules, and one draw needn't show every extreme that they name: `owner_map`: within each group of 2048 consecutive pairs, a quarter of the 32 owners are named by exactly 128 pairs, a quarter by exactly 64, and the other half by exactly 32; which owners and which pairs vary.
All inputs are finite; a program needn't handle non-finite values.
Results may differ from a plain program's by a relative error of at most 0.0003.
Values sent between devices are 32-bit elements; how exact they have to be, the bound alone decides.
No kernel may reach another device: no remote copies, remote signals or barrier semaphores. Data moves between devices by JAX's collectives and lax.ppermute only.
A program may use at most 128 MiB of HBM per device.

v0:
```python
import functools

import jax
import jax.numpy as jnp
from jax import lax
from jax.experimental import pallas as pl
from jax.experimental.pallas import tpu as pltpu
from jax.sharding import Mesh
from jax.sharding import PartitionSpec as P

NY, NC, NX, NZ = 4, 2, 4, 8
ROWS = 4
COLS = 50
CUTS = (10, 20, 20)
FLAT = tuple(ROWS * cut for cut in CUTS)
K = NY * NC * COLS
SLOTS = 128
NS = 128
F32, BF16 = jnp.float32, jnp.bfloat16


def shift(value, axis, step):
    n = lax.axis_size(axis)
    return lax.ppermute(value, axis, [(i, (i + step) % n) for i in range(n)])


def turn(value, axis, step):
    n = lax.axis_size(axis)
    pairs = []
    for c in range(NC):
        for i in range(n):
            j = (i + (step if c == 0 else -step)) % n
            pairs.append((i * NC + c, j * NC + c) if axis == "y" else (c * n + i, c * n + j))
    return lax.ppermute(value, ("y", "core") if axis == "y" else ("core", axis), pairs)


def trade(value, axis, bit):
    n = lax.axis_size(axis)
    return lax.ppermute(value, axis, [(i, i ^ bit) for i in range(n)])


def swap_halves(flat):
    pairs = []
    for c in range(NC):
        for z in range(NZ):
            high = (z >> 1) & 1
            if c == high:
                pairs.append((c * NZ + z, c * NZ + z))
            else:
                pairs.append((c * NZ + z, high * NZ + (z ^ 2)))
    return lax.ppermute(flat, ("core", "z"), pairs)


def together(*values):
    return lax.optimization_barrier(values)


def global_columns(y):
    place = lax.broadcasted_iota(jnp.int32, (K, 1), 0)
    ids, start, offset, first = place, 0, 0, 0
    for part, cut in enumerate(CUTS):
        for half in range(NC):
            for step in range(NY):
                source = y ^ step if part == 0 else lax.rem(y + NY - step, NY)
                now = 100 * source + COLS * half + first - start
                ids = ids + jnp.where(place >= start, now - offset, 0)
                offset, start = now, start + cut
        first += cut
    return ids


def mixing_kernel(owner_ref, kind_ref, pole_ref, angle_ref, angular_ref, out_ref):
    me = lax.axis_index("x") * NZ + lax.axis_index("z")
    pairs = owner_ref.shape[0] * owner_ref.shape[1]
    groups = pairs // 128
    mine = (owner_ref[...] == me).astype(F32)
    low = lax.broadcasted_iota(jnp.int32, (128, 128), 0)
    high = lax.broadcasted_iota(jnp.int32, (128, 128), 1)
    upper = (low <= high).astype(BF16)
    within = jnp.dot(mine.astype(BF16), upper, preferred_element_type=F32)
    totals = jnp.sum(mine, axis=1, keepdims=True)
    before = jnp.zeros((groups, 1), F32)
    row = lax.broadcasted_iota(jnp.int32, (groups, 1), 0)
    for j in range(groups - 1):
        before = before + jnp.where(row > j, totals[j : j + 1, :], 0.0)
    rank = jnp.where(mine > 0.0, within + before - 1.0, -1.0).astype(jnp.int32)
    slot = lax.broadcasted_iota(jnp.int32, (SLOTS, 128), 0)
    chosen = jnp.zeros((24, SLOTS), F32)
    for j in range(groups):
        span = pl.ds(j * 128, 128)
        listed = jnp.concatenate([kind_ref[:, span], pole_ref[:, span], angle_ref[:, span]], axis=0)
        selected = (rank[j : j + 1, :] == slot).astype(BF16)
        chosen = chosen + lax.dot_general(
            listed.astype(F32).astype(BF16),
            selected,
            (((1,), (1,)), ((), ())),
            preferred_element_type=F32,
        )
    count = jnp.sum(totals, axis=0, keepdims=True)
    filled = lax.broadcasted_iota(jnp.int32, (1, SLOTS), 1).astype(F32) < count
    chosen = chosen.astype(jnp.int32)
    column = global_columns(lax.axis_index("y"))
    size = angular_ref.shape[1]
    table = lax.broadcasted_iota(jnp.int32, (size, SLOTS), 0)
    down, across = (lax.broadcasted_iota(jnp.int32, (size, size), d) for d in range(2))
    angular = jnp.sum(jnp.where(down == across, angular_ref[...], 0.0), axis=1, keepdims=True)
    total = jnp.zeros((K, SLOTS), F32)
    for entry in range(8):
        wanted = chosen[entry : entry + 1, :] * 5 + chosen[8 + entry : 9 + entry, :]
        angle = chosen[16 + entry : 17 + entry, :]
        value = jnp.sum(jnp.where(table == angle, angular, 0.0), axis=0, keepdims=True)
        value = jnp.where(filled, value, 0.0)
        total = total + jnp.where(column == wanted, value, 0.0)
    pad = jnp.zeros((512 - K, SLOTS), F32)
    out_ref[...] = jnp.concatenate([total, pad], axis=0).T


def mixing(owner_map, kinds, poles, angles, angular):
    vmem = pl.BlockSpec(memory_space=pltpu.VMEM)
    return pl.pallas_call(
        mixing_kernel,
        out_shape=jax.ShapeDtypeStruct((SLOTS, 512), F32),
        in_specs=[vmem] * 5,
        out_specs=vmem,
        compiler_params=pltpu.CompilerParams(vmem_limit_bytes=16 << 20),
        cost_estimate=pl.CostEstimate(flops=100 << 20, bytes_accessed=1 << 20, transcendentals=0),
    )(owner_map.reshape(-1, 128), kinds.T, poles.T, angles.T, angular[None, :])


def before(x, core, step):
    return lax.rem(x + jnp.where(core == 0, NX - step, step), NX)


def product_kernel(steps, fresh, *refs):
    count = len(steps)
    own_ref, other_ref = refs[:2]
    a_ref, b_refs, c_refs = refs[2], refs[3:8], refs[8:13]
    refs = refs[13 + (0 if fresh else 1) :]
    out_ref, send_refs = refs[0], refs[1 : 1 + count]
    a_all, b_all, c_all, left_all, kept, given, sems, out_sems = refs[1 + count :]
    core, x, z = (lax.axis_index(name) for name in ("core", "x", "z"))

    def arrive(n):
        step = steps[n]
        copies = []

        def add(source, target):
            copies.append(pltpu.make_async_copy(source, target, sems.at[n, len(copies)]))

        add(a_ref.at[:, x ^ before(x, core, step)], a_all.at[n])
        add(b_refs[0].at[step], b_all.at[n, 0])
        add(b_refs[1].at[step], b_all.at[n, 1])
        add(b_refs[2 + step // 2].at[step % 2], b_all.at[n, 2])
        add(b_refs[4].at[step], b_all.at[n, 3])
        if step == 2:
            for half in range(2):
                add(c_refs[2 + half], c_all.at[n, pl.ds(4 * half, 4)])
        else:
            add(c_refs[(0, 1, None, 4)[step]], c_all.at[n])
        return copies

    def leave(n, q):
        rows = pl.ds(pl.multiple_of(8 * (4 * before(x, core, steps[n]) + core + 2 * q), 8), 8)
        return (
            pltpu.make_async_copy(
                kept.at[n, q].reshape(SLOTS, 8, NS), out_ref.at[:, rows, :], out_sems.at[n, q]
            ),
            pltpu.make_async_copy(given.at[n, q], send_refs[n].at[q], out_sems.at[n, 2 + q]),
        )

    for copy in arrive(0):
        copy.start()
    mix = jnp.concatenate([own_ref[...], other_ref[...]], axis=0)
    mix_high = mix.astype(BF16)
    left_all[: 2 * SLOTS, :] = mix_high
    left_all[2 * SLOTS :, :] = (mix - mix_high.astype(F32)).astype(BF16)
    a_run, b_run, c_run = NY * CUTS[0], CUTS[1], NY * CUTS[2]
    pad = jnp.zeros((512 - K, NS), F32)

    for n in range(count):
        for copy in arrive(n):
            copy.wait()
        if n + 1 < count:
            for copy in arrive(n + 1):
                copy.start()

        def one_tile(q, carry, n=n):
            for b in range(2):
                places = [4 * q + 2 * half + b for half in range(2)]
                spots = [lax.rem(place - z + NZ + 3, NZ) for place in places]
                for first in (0, 2):
                    highs, lows = [], []
                    for r in (first, first + 1):
                        pieces = [a_all[n, s, pl.ds(r, a_run, stride=ROWS), :] for s in places]
                        pieces += [
                            b_all[n, y, s, pl.ds(r, b_run, stride=ROWS), :] for s in spots for y in range(NY)
                        ]
                        pieces += [c_all[n, s, pl.ds(r, c_run, stride=ROWS), :] for s in spots]
                        value = jnp.concatenate(pieces + [pad], axis=0)
                        high = value.astype(BF16)
                        highs.append(high)
                        lows.append((value - high.astype(F32)).astype(BF16))
                    right_high = jnp.concatenate(highs, axis=1)
                    right_low = jnp.concatenate(lows, axis=1)
                    full = jnp.dot(left_all[...], right_high, preferred_element_type=F32)
                    rest = jnp.dot(left_all[: 2 * SLOTS, :], right_low, preferred_element_type=F32)
                    total = full[: 2 * SLOTS] + (full[2 * SLOTS :] + rest)
                    for m in range(2):
                        lanes = slice(m * NS, (m + 1) * NS)
                        row = pl.ds(4 * b + first + m, SLOTS, stride=8)
                        kept[n, q, row, :] = total[:SLOTS, lanes]
                        given[n, q, row, :] = total[SLOTS:, lanes]
            for copy in leave(n, q):
                copy.start()
            return carry

        lax.fori_loop(0, 2, one_tile, 0)
    for n in range(count):
        for q in range(2):
            for copy in leave(n, q):
                copy.wait()


def product(steps, own, other, a_part, b_parts, c_parts, out):
    vmem = pl.BlockSpec(memory_space=pltpu.VMEM)
    anywhere = pl.BlockSpec(memory_space=pl.ANY)
    hbm = pl.BlockSpec(memory_space=pltpu.HBM)
    fresh, count = out is None, len(steps)
    operands = [own, other, a_part, *b_parts, *c_parts] + ([] if fresh else [out])
    flops = 2 * 8 * 768 * 512 * 256
    return pl.pallas_call(
        functools.partial(product_kernel, steps, fresh),
        out_shape=(
            jax.ShapeDtypeStruct((SLOTS, NS, NS), F32),
            *[jax.ShapeDtypeStruct((2, SLOTS * 8, NS), F32)] * count,
        ),
        in_specs=[vmem, vmem, hbm] + [anywhere] * (len(operands) - 3),
        out_specs=(anywhere,) * (1 + count),
        scratch_shapes=[
            pltpu.VMEM((count, NZ, NY * FLAT[0], NS), F32),
            pltpu.VMEM((count, NY, NZ, FLAT[1], NS), F32),
            pltpu.VMEM((count, NZ, NY * FLAT[2], NS), F32),
            pltpu.VMEM((4 * SLOTS, 512), BF16),
            pltpu.VMEM((count, 2, SLOTS * 8, NS), F32),
            pltpu.VMEM((count, 2, SLOTS * 8, NS), F32),
            pltpu.SemaphoreType.DMA((count, 7)),
            pltpu.SemaphoreType.DMA((count, 4)),
        ],
        input_output_aliases={} if fresh else {len(operands) - 1: 0},
        compiler_params=pltpu.CompilerParams(vmem_limit_bytes=60 << 20),
        cost_estimate=pl.CostEstimate(flops=count * flops, bytes_accessed=count << 23, transcendentals=0),
    )(*operands)


def place_kernel(steps, *refs):
    count = len(steps)
    blocks, out_ref, sems = refs[:count], refs[-2], refs[-1]
    core, x = lax.axis_index("core"), lax.axis_index("x")
    copies = []
    for n, step in enumerate(steps):
        tile = 4 * before(x, 1 - core, step) + 1 - core
        for q in range(2):
            rows = pl.ds(pl.multiple_of(8 * (tile + 2 * q), 8), 8)
            source = blocks[n].at[q].reshape(SLOTS, 8, NS)
            copies.append(pltpu.make_async_copy(source, out_ref.at[:, rows, :], sems.at[2 * n + q]))
    for copy in copies:
        copy.start()
    for copy in copies:
        copy.wait()


def place(steps, blocks, out):
    anywhere = pl.BlockSpec(memory_space=pl.ANY)
    vmem = pl.BlockSpec(memory_space=pltpu.VMEM)
    count = len(blocks)
    return pl.pallas_call(
        functools.partial(place_kernel, steps),
        out_shape=jax.ShapeDtypeStruct(out.shape, F32),
        in_specs=[vmem] * count + [anywhere],
        out_specs=anywhere,
        scratch_shapes=[pltpu.SemaphoreType.DMA((2 * count,))],
        input_output_aliases={count: 0},
        compiler_params=pltpu.CompilerParams(vmem_limit_bytes=8 << 20),
        cost_estimate=pl.CostEstimate(flops=0, bytes_accessed=count << 21, transcendentals=0),
    )(*blocks, out)


def body(slater, couple_type, couple_multipole, couple_angle, angular, owner_map):
    flat = swap_halves(slater.reshape(COLS * ROWS, NS))
    part_a, part_bc = flat[: FLAT[0]], flat[FLAT[0] :]

    p1, m1, p2, m2 = (shift(part_bc, "z", n) for n in (1, -1, 2, -2))
    a_y = jnp.concatenate([part_a, trade(part_a, "y", 1)], axis=0)
    p1, m1, p2, m2, a_y = together(p1, m1, p2, m2, a_y)
    p3, m3, p4 = shift(p2, "z", 1), shift(m2, "z", -1), shift(p2, "z", 2)
    a_y = jnp.concatenate([a_y, trade(a_y, "y", 2)], axis=0)
    p3, m3, p4, a_y = together(p3, m3, p4, a_y)
    bc = jnp.stack([p3, p2, p1, part_bc, m1, m2, m3, p4])

    b_0, c_0 = bc[:, : FLAT[1]], bc[:, FLAT[1] :]
    b_1, b_3 = turn(b_0, "x", 1), turn(b_0, "x", -1)
    c_1, c_3 = shift(c_0, "y", 1), shift(c_0, "y", -1)
    a_x = jnp.stack([a_y, trade(a_y, "x", 1)])
    b_1, b_3, c_1, c_3, a_x = together(b_1, b_3, c_1, c_3, a_x)
    b_2 = turn(b_1[:4], "x", 1), turn(b_3[4:], "x", -1)
    c_2 = shift(c_1[:4], "y", 1), shift(c_3[4:], "y", -1)
    a_x = jnp.concatenate([a_x, trade(a_x, "x", 2)], axis=0)
    *b_2, c_20, c_21, a_x = together(*b_2, *c_2, a_x)
    b_x = jnp.stack([b_0, b_1, jnp.concatenate(b_2, axis=0), b_3])
    c_y = jnp.concatenate([c_0, c_1, jnp.concatenate([c_20, c_21], axis=0), c_3], axis=1)

    own = mixing(owner_map, couple_type, couple_multipole, couple_angle, angular)

    a_z = lax.all_gather(a_x, "z", axis=0, tiled=False)
    y_1, y_3 = shift(b_x, "y", 1), shift(b_x, "y", -1)
    x_1, x_3 = turn(c_y, "x", 1), turn(c_y, "x", -1)
    other = lax.ppermute(own, "core", [(0, 1), (1, 0)])
    y_1, y_3, x_1, x_3, other = together(y_1, y_3, x_1, x_3, other)
    y_2 = shift(y_1[:2], "y", 1), shift(y_3[2:], "y", -1)
    x_2 = turn(x_1[:4], "x", 1), turn(x_3[4:], "x", -1)

    b_parts, c_parts = [b_x, y_1, *y_2, y_3], [c_y, x_1, *x_2, x_3]
    out, received = None, []
    for steps in ((0, 1, 2), (3,)):
        out, *given = product(steps, own, other, a_z, b_parts, c_parts, out)
        received += [lax.ppermute(block, "core", [(0, 1), (1, 0)]) for block in given]
    out = place((0, 1, 2), received[:3], out)
    return place((3,), received[3:], out)


def solution(mesh):
    fine = Mesh(mesh.devices.reshape(NY, NC, NX, NZ), ("y", "core", "x", "z"))
    groups = ("y", "core")
    return jax.shard_map(
        body,
        mesh=fine,
        in_specs=(
            P(groups, None, ("x", "z"), None),
            P(groups, None),
            P(groups, None),
            P(groups, None),
            P(),
            P(groups),
        ),
        out_specs=P(("y", "core", "x", "z"), None, None),
        check_vma=False,
    )
```

profile of v0, /device:TPU:1, one launch (start us, length us, event | category | flops | bytes accessed | tf_op | source)
XLA Modules:
  0.0 142.6 jit_solution(10168927581551955498)
XLA Ops:
  6.5 6.3 %collective-permute-start = (f32[200,128]{1,0:T(8,128)}, f32[200,128]{1,0:T(8,128)S(1)}, u32[]{:S(2)}, u32[]{:S(2)}) collective-permute-start(f32[200,128]{1,0:T(8,128)} %bitcast.42), channel_id=1, source_target_pairs={{0,0},{1,1},{2,32},{3,33},{4,4},{5,5},{6,36},{7,37},{32,2},{33,3},... | collective-permute-start | bytes 307208 | tf_op jit(solution)/shard_map/ppermute | solution.py:51
  12.8 2.5 %collective-permute-done = f32[200,128]{1,0:T(8,128)S(1)} collective-permute-done((f32[200,128]{1,0:T(8,128)}, f32[200,128]{1,0:T(8,128)S(1)}, u32[]{:S(2)}, u32[]{:S(2)}) %collective-permute-start) | collective-permute-done | bytes 102432 | tf_op jit(solution)/shard_map/ppermute | solution.py:51
  15.4 1.3 collective-permute-start.5
  16.7 2.4 %collective-permute-start.3 = (f32[160,128]{1,0:T(8,128)S(1)}, f32[160,128]{1,0:T(8,128)S(1)}, u32[]{:S(2)}, u32[]{:S(2)}) collective-permute-start(f32[160,128]{1,0:T(8,128)S(1)} %slice.48), channel_id=1, source_target_pairs={{0,2},{1,3},{2,4},{3,5},{4,6},{5,7},{6,0},{7,1},{8,10},{9,11},{10,... | collective-permute-start | bytes 245768 | tf_op jit(solution)/shard_map/ppermute | solution.py:24
  19.0 3.6 %collective-permute-start.2 = (f32[160,128]{1,0:T(8,128)S(1)}, f32[160,128]{1,0:T(8,128)S(1)}, u32[]{:S(2)}, u32[]{:S(2)}) collective-permute-start(f32[160,128]{1,0:T(8,128)S(1)} %slice.48), channel_id=1, source_target_pairs={{0,7},{1,0},{2,1},{3,2},{4,3},{5,4},{6,5},{7,6},{8,15},{9,8},{10,9... | collective-permute-start | bytes 245768 | tf_op jit(solution)/shard_map/ppermute | solution.py:24
  22.6 4.2 %collective-permute-done.3 = f32[160,128]{1,0:T(8,128)S(1)} collective-permute-done((f32[160,128]{1,0:T(8,128)S(1)}, f32[160,128]{1,0:T(8,128)S(1)}, u32[]{:S(2)}, u32[]{:S(2)}) %collective-permute-start.3) | collective-permute-done | bytes 81952 | tf_op jit(solution)/shard_map/ppermute | solution.py:24
  26.9 0.4 collective-permute-done.1
  27.2 2.6 %collective-permute-start.9 = (f32[80,128]{1,0:T(8,128)S(1)}, f32[80,128]{1,0:T(8,128)S(1)}, u32[]{:S(2)}, u32[]{:S(2)}) collective-permute-start(f32[80,128]{1,0:T(8,128)S(1)} %pad_maximum_fusion.5), channel_id=1, source_target_pairs={{0,128},{64,192},{128,0},{192,64},{1,129},{65,193},{129,1},{193,65... | collective-permute-start | bytes 122888 | tf_op jit(solution)/shard_map/ppermute | solution.py:39
  29.9 1.9 %collective-permute-start.8 = (f32[160,128]{1,0:T(8,128)S(1)}, f32[160,128]{1,0:T(8,128)S(1)}, u32[]{:S(2)}, u32[]{:S(2)}) collective-permute-start(f32[160,128]{1,0:T(8,128)S(1)} %collective-permute-done.3), channel_id=1, source_target_pairs={{0,2},{1,3},{2,4},{3,5},{4,6},{5,7},{6,0},{7,1},{8,10},{9,11},{10,... | collective-permute-start | bytes 245768 | tf_op jit(solution)/shard_map/ppermute | solution.py:24
  31.8 0.9 collective-permute-start.6
  32.7 1.8 %collective-permute-start.7 = (f32[160,128]{1,0:T(8,128)S(1)}, f32[160,128]{1,0:T(8,128)S(1)}, u32[]{:S(2)}, u32[]{:S(2)}) collective-permute-start(f32[160,128]{1,0:T(8,128)S(1)} %collective-permute-done.4), channel_id=1, source_target_pairs={{0,7},{1,0},{2,1},{3,2},{4,3},{5,4},{6,5},{7,6},{8,15},{9,8},{10,9... | collective-permute-start | bytes 245768 | tf_op jit(solution)/shard_map/ppermute | solution.py:24
  34.4 2.4 %collective-permute-done.7 = f32[160,128]{1,0:T(8,128)S(1)} collective-permute-done((f32[160,128]{1,0:T(8,128)S(1)}, f32[160,128]{1,0:T(8,128)S(1)}, u32[]{:S(2)}, u32[]{:S(2)}) %collective-permute-start.7) | collective-permute-done | bytes 81952 | tf_op jit(solution)/shard_map/ppermute | solution.py:24
  37.1 2.6 %collective-permute-start.10 = (f32[8,80,128]{2,1,0:T(8,128)S(1)}, f32[8,80,128]{2,1,0:T(8,128)S(1)}, u32[]{:S(2)}, u32[]{:S(2)}) collective-permute-start(f32[8,80,128]{2,1,0:T(8,128)S(1)} %get-tuple-element.67), channel_id=1, source_target_pairs={{0,8},{8,16},{16,24},{24,0},{32,56},{40,32},{48,40},{56,48},{1,9},... | collective-permute-start | bytes 983048 | tf_op jit(solution)/shard_map/ppermute | solution.py:34
  39.6 1.5 %collective-permute-start.12 = (f32[8,80,128]{2,1,0:T(8,128)S(1)}, f32[8,80,128]{2,1,0:T(8,128)S(1)}, u32[]{:S(2)}, u32[]{:S(2)}) collective-permute-start(f32[8,80,128]{2,1,0:T(8,128)S(1)} %get-tuple-element.66), channel_id=1, source_target_pairs={{0,64},{64,128},{128,192},{192,0},{1,65},{65,129},{129,193},{193,1... | collective-permute-start | bytes 983048 | tf_op jit(solution)/shard_map/ppermute | solution.py:24
  41.1 0.2 collective-permute-start.14
  41.3 3.2 %collective-permute-done.14 = f32[160,128]{1,0:T(8,128)S(1)} collective-permute-done((f32[160,128]{1,0:T(8,128)S(1)}, f32[160,128]{1,0:T(8,128)S(1)}, u32[]{:S(2)}, u32[]{:S(2)}) %collective-permute-start.14) | collective-permute-done | bytes 81952 | tf_op jit(solution)/shard_map/ppermute | solution.py:39
  44.5 2.2 %collective-permute-done.11 = f32[8,80,128]{2,1,0:T(8,128)S(1)} collective-permute-done((f32[8,80,128]{2,1,0:T(8,128)S(1)}, f32[8,80,128]{2,1,0:T(8,128)S(1)}, u32[]{:S(2)}, u32[]{:S(2)}) %collective-permute-start.11) | collective-permute-done | bytes 327712 | tf_op jit(solution)/shard_map/ppermute | solution.py:34
  46.8 1.7 %collective-permute-start.19 = (f32[2,160,128]{2,1,0:T(8,128)S(1)}, f32[2,160,128]{2,1,0:T(8,128)S(1)}, u32[]{:S(2)}, u32[]{:S(2)}) collective-permute-start(f32[2,160,128]{2,1,0:T(8,128)S(1)} %pad_maximum_fusion.3), channel_id=1, source_target_pairs={{0,16},{8,24},{16,0},{24,8},{1,17},{9,25},{17,1},{25,9},{2,18},{10... | collective-permute-start | bytes 491528 | tf_op jit(solution)/shard_map/ppermute | solution.py:39
  48.7 1.5 %collective-permute-start.17 = (f32[4,80,128]{2,1,0:T(8,128)S(1)}, f32[4,80,128]{2,1,0:T(8,128)S(1)}, u32[]{:S(2)}, u32[]{:S(2)}) collective-permute-start(f32[4,80,128]{2,1,0:T(8,128)S(1)} %slice.42), channel_id=1, source_target_pairs={{0,64},{64,128},{128,192},{192,0},{1,65},{65,129},{129,193},{193,1... | collective-permute-start | bytes 491528 | tf_op jit(solution)/shard_map/ppermute | solution.py:24
  50.1 1.5 %collective-permute-start.16 = (f32[4,80,128]{2,1,0:T(8,128)S(1)}, f32[4,80,128]{2,1,0:T(8,128)S(1)}, u32[]{:S(2)}, u32[]{:S(2)}) collective-permute-start(f32[4,80,128]{2,1,0:T(8,128)S(1)} %slice.41), channel_id=1, source_target_pairs={{0,24},{8,0},{16,8},{24,16},{32,40},{40,48},{48,56},{56,32},{1,25}... | collective-permute-start | bytes 491528 | tf_op jit(solution)/shard_map/ppermute | solution.py:34
  51.6 1.2 collective-permute-start.15
  52.8 1.5 %collective-permute-done.19 = f32[2,160,128]{2,1,0:T(8,128)S(1)} collective-permute-done((f32[2,160,128]{2,1,0:T(8,128)S(1)}, f32[2,160,128]{2,1,0:T(8,128)S(1)}, u32[]{:S(2)}, u32[]{:S(2)}) %collective-permute-start.19) | collective-permute-done | bytes 163872 | tf_op jit(solution)/shard_map/ppermute | solution.py:39
  54.2 0.7 pad_maximum_fusion.2
  55.0 1.4 collective-permute-done.17
  56.6 2.7 %collective-permute-start.22 = (f32[8,320,128]{2,1,0:T(8,128)S(1)}, f32[8,320,128]{2,1,0:T(8,128)S(1)}, u32[]{:S(2)}, u32[]{:S(2)}) collective-permute-start(f32[8,320,128]{2,1,0:T(8,128)S(1)} %pad_maximum_fusion.1.refs_8_), channel_id=1, source_target_pairs={{0,8},{8,16},{16,24},{24,0},{32,56},{40,32},{48,40},{56,48},{1,9},... | collective-permute-start | bytes 3932168 | tf_op jit(solution)/shard_map/ppermute | solution.py:34
  59.5 0.9 collective-permute-start.21
  60.5 0.6 collective-permute-start.20
  61.1 0.9 shard_map.64.refs_0_
  62.0 13.3 %collective-permute-start.24 = (f32[128,512]{1,0:T(8,128)S(1)}, f32[128,512]{1,0:T(8,128)S(1)}, u32[]{:S(2)}, u32[]{:S(2)}) collective-permute-start(f32[128,512]{1,0:T(8,128)S(1)} %shard_map.64.refs_0_), channel_id=1, source_target_pairs={{0,32},{32,0},{1,33},{33,1},{2,34},{34,2},{3,35},{35,3},{4,36},{36... | collective-permute-start | bytes 786440 | tf_op jit(solution)/shard_map/ppermute | solution.py:317
  75.2 1.2 collective-permute-done.24.refs_1_
  76.4 4.9 %collective-permute-done.23.refs_12_ = f32[8,320,128]{2,1,0:T(8,128)S(1)} collective-permute-done((f32[8,320,128]{2,1,0:T(8,128)S(1)}, f32[8,320,128]{2,1,0:T(8,128)S(1)}, u32[]{:S(2)}, u32[]{:S(2)}) %collective-permute-start.23) | collective-permute-done | bytes 1310752 | tf_op jit(solution)/shard_map/ppermute | solution.py:34
  81.3 1.7 %collective-permute-done.22.refs_9_ = f32[8,320,128]{2,1,0:T(8,128)S(1)} collective-permute-done((f32[8,320,128]{2,1,0:T(8,128)S(1)}, f32[8,320,128]{2,1,0:T(8,128)S(1)}, u32[]{:S(2)}, u32[]{:S(2)}) %collective-permute-start.22) | collective-permute-done | bytes 1310752 | tf_op jit(solution)/shard_map/ppermute | solution.py:34
  83.3 0.9 copy-done.9
  84.2 0.4 copy-done.10
  84.6 3.4 %collective-permute-start.27 = (f32[4,320,128]{2,1,0:T(8,128)S(1)}, f32[4,320,128]{2,1,0:T(8,128)S(1)}, u32[]{:S(2)}, u32[]{:S(2)}) collective-permute-start(f32[4,320,128]{2,1,0:T(8,128)S(1)} %slice.46), channel_id=1, source_target_pairs={{0,8},{8,16},{16,24},{24,0},{32,56},{40,32},{48,40},{56,48},{1,9},... | collective-permute-start | bytes 1966088 | tf_op jit(solution)/shard_map/ppermute | solution.py:34
  88.0 1.5 %collective-permute-start.25 = (f32[2,8,80,128]{3,2,1,0:T(8,128)S(1)}, f32[2,8,80,128]{3,2,1,0:T(8,128)S(1)}, u32[]{:S(2)}, u32[]{:S(2)}) collective-permute-start(f32[2,8,80,128]{3,2,1,0:T(8,128)S(1)} %slice.44), channel_id=1, source_target_pairs={{0,64},{64,128},{128,192},{192,0},{1,65},{65,129},{129,193},{193,1... | collective-permute-start | bytes 1966088 | tf_op jit(solution)/shard_map/ppermute | solution.py:24
  89.5 9.8 %collective-permute-done.28.refs_11_ = f32[4,320,128]{2,1,0:T(8,128)S(1)} collective-permute-done((f32[4,320,128]{2,1,0:T(8,128)S(1)}, f32[4,320,128]{2,1,0:T(8,128)S(1)}, u32[]{:S(2)}, u32[]{:S(2)}) %collective-permute-start.28) | collective-permute-done | bytes 655392 | tf_op jit(solution)/shard_map/ppermute | solution.py:34
  99.3 1.2 collective-permute-done.25.refs_5_
  100.5 3.6 %all-gather.3.cloned.1.call-done = f32[32,160,128]{2,1,0:T(8,128)} async-done(((f32[4,160,128]{2,1,0:T(8,128)}), f32[32,160,128]{2,1,0:T(8,128)}) %all-gather.3.cloned.1.call-update) | async-done | bytes 2621456 | tf_op jit(solution)/shard_map/all_gather | solution.py:314
  104.2 11.0 %shard_map.65 = (f32[128,128,128]{2,1,0:T(8,128)}, f32[2,1024,128]{2,1,0:T(8,128)}, f32[2,1024,128]{2,1,0:T(8,128)}, f32[2,1024,128]{2,1,0:T(8,128)}) custom-call(f32[128,512]{1,0:T(8,128)} %copy-done, f32[128,512]{1,0:T(8,128)} %copy-done.16, f32[8,4,160,128]{3,2,1,0:T(8,128)} %bitcast.36, f32[4,8,80,128]{3,2,1,0:T(8,128)} %copy-done.7, ...), custom_call_target="tpu_custom_call" | custom-call | flops 4831838208 | bytes 25165824 | tf_op jit(solution)/shard_map/pallas_call | solution.py:231
  115.1 10.1 %collective-permute-start.30 = (f32[2,1024,128]{2,1,0:T(8,128)}, f32[2,1024,128]{2,1,0:T(8,128)S(1)}, u32[]{:S(2)}, u32[]{:S(2)}) collective-permute-start(f32[2,1024,128]{2,1,0:T(8,128)} %get-tuple-element.61), channel_id=1, source_target_pairs={{0,32},{32,0},{1,33},{33,1},{2,34},{34,2},{3,35},{35,3},{4,36},{36... | collective-permute-start | bytes 3145736 | tf_op jit(solution)/shard_map/ppermute | solution.py:326
  125.2 0.1 collective-permute-start.31
  125.3 0.4 collective-permute-start.32
  125.7 6.1 %shard_map.66 = (f32[128,128,128]{2,1,0:T(8,128)}, f32[2,1024,128]{2,1,0:T(8,128)}) custom-call(f32[128,512]{1,0:T(8,128)} %copy-done, f32[128,512]{1,0:T(8,128)} %copy-done.16, f32[8,4,160,128]{3,2,1,0:T(8,128)} %bitcast.37, f32[4,8,80,128]{3,2,1,0:T(8,128)} %copy-done.7, f32[4,8,80,128]{3,2,1,0:T(8,128)} %copy-done.11, ...), custom_call_target="tpu_custom_call", output_to_operand_aliasing={{0}: (13, {})} | custom-call | flops 1610612736 | bytes 8388608 | tf_op jit(solution)/shard_map/pallas_call | solution.py:231
  131.8 0.2 collective-permute-start.29
  132.0 1.7 %shard_map.67.refs_1_ = f32[128,128,128]{2,1,0:T(8,128)} custom-call(f32[2,1024,128]{2,1,0:T(8,128)S(1)} %collective-permute-done.30.refs_0_, f32[2,1024,128]{2,1,0:T(8,128)S(1)} %collective-permute-done.31.refs_1_, f32[2,1024,128]{2,1,0:T(8,128)S(1)} %collective-permute-done.32.refs_2_, ...), custom_call_target="tpu_custom_call", output_to_operand_aliasing={{}: (3, {})} | custom-call | bytes 6291456 | tf_op jit(solution)/shard_map/pallas_call | solution.py:276
  133.8 1.0 collective-permute-done.29.refs_0_
  134.8 1.0 shard_map.68
  (86 shorter events, 0.9 us)
Async XLA Ops:
  6.5 97.6 %all-gather.3.cloned.1.call-start = ((), (), s32[]{:S(2)}) async-start(), calls=%async_computation | async-start | bytes 2949120 | tf_op jit(solution)/shard_map/all_gather | solution.py:314
  6.5 8.8 %collective-permute-start = (f32[200,128]{1,0:T(8,128)}, f32[200,128]{1,0:T(8,128)S(1)}, u32[]{:S(2)}, u32[]{:S(2)}) collective-permute-start(f32[200,128]{1,0:T(8,128)} %bitcast.42), channel_id=1, source_target_pairs={{0,0},{1,1},{2,32},{3,33},{4,4},{5,5},{6,36},{7,37},{32,2},{33,3},... | collective-permute-start | bytes 307208 | tf_op jit(solution)/shard_map/ppermute | solution.py:51
  15.4 7.2 %collective-permute-start.5 = (f32[40,128]{1,0:T(8,128)S(1)}, f32[40,128]{1,0:T(8,128)S(1)}, u32[]{:S(2)}, u32[]{:S(2)}) collective-permute-start(f32[40,128]{1,0:T(8,128)S(1)} %slice.49), channel_id=1, source_target_pairs={{0,64},{64,0},{128,192},{192,128},{1,65},{65,1},{129,193},{193,129... | collective-permute-start | bytes 61448 | tf_op jit(solution)/shard_map/ppermute | solution.py:39
  16.7 5.9 %collective-permute-start.4 = (f32[160,128]{1,0:T(8,128)S(1)}, f32[160,128]{1,0:T(8,128)S(1)}, u32[]{:S(2)}, u32[]{:S(2)}) collective-permute-start(f32[160,128]{1,0:T(8,128)S(1)} %slice.48), channel_id=1, source_target_pairs={{0,6},{1,7},{2,0},{3,1},{4,2},{5,3},{6,4},{7,5},{8,14},{9,15},{10,... | collective-permute-start | bytes 245768 | tf_op jit(solution)/shard_map/ppermute | solution.py:24
  16.7 10.2 %collective-permute-start.3 = (f32[160,128]{1,0:T(8,128)S(1)}, f32[160,128]{1,0:T(8,128)S(1)}, u32[]{:S(2)}, u32[]{:S(2)}) collective-permute-start(f32[160,128]{1,0:T(8,128)S(1)} %slice.48), channel_id=1, source_target_pairs={{0,2},{1,3},{2,4},{3,5},{4,6},{5,7},{6,0},{7,1},{8,10},{9,11},{10,... | collective-permute-start | bytes 245768 | tf_op jit(solution)/shard_map/ppermute | solution.py:24
  19.0 7.8 %collective-permute-start.2 = (f32[160,128]{1,0:T(8,128)S(1)}, f32[160,128]{1,0:T(8,128)S(1)}, u32[]{:S(2)}, u32[]{:S(2)}) collective-permute-start(f32[160,128]{1,0:T(8,128)S(1)} %slice.48), channel_id=1, source_target_pairs={{0,7},{1,0},{2,1},{3,2},{4,3},{5,4},{6,5},{7,6},{8,15},{9,8},{10,9... | collective-permute-start | bytes 245768 | tf_op jit(solution)/shard_map/ppermute | solution.py:24
  22.6 4.6 %collective-permute-start.1 = (f32[160,128]{1,0:T(8,128)S(1)}, f32[160,128]{1,0:T(8,128)S(1)}, u32[]{:S(2)}, u32[]{:S(2)}) collective-permute-start(f32[160,128]{1,0:T(8,128)S(1)} %slice.48), channel_id=1, source_target_pairs={{0,1},{1,2},{2,3},{3,4},{4,5},{5,6},{6,7},{7,0},{8,9},{9,10},{10,1... | collective-permute-start | bytes 245768 | tf_op jit(solution)/shard_map/ppermute | solution.py:24
  27.2 7.2 %collective-permute-start.9 = (f32[80,128]{1,0:T(8,128)S(1)}, f32[80,128]{1,0:T(8,128)S(1)}, u32[]{:S(2)}, u32[]{:S(2)}) collective-permute-start(f32[80,128]{1,0:T(8,128)S(1)} %pad_maximum_fusion.5), channel_id=1, source_target_pairs={{0,128},{64,192},{128,0},{192,64},{1,129},{65,193},{129,1},{193,65... | collective-permute-start | bytes 122888 | tf_op jit(solution)/shard_map/ppermute | solution.py:39
  29.9 7.0 %collective-permute-start.8 = (f32[160,128]{1,0:T(8,128)S(1)}, f32[160,128]{1,0:T(8,128)S(1)}, u32[]{:S(2)}, u32[]{:S(2)}) collective-permute-start(f32[160,128]{1,0:T(8,128)S(1)} %collective-permute-done.3), channel_id=1, source_target_pairs={{0,2},{1,3},{2,4},{3,5},{4,6},{5,7},{6,0},{7,1},{8,10},{9,11},{10,... | collective-permute-start | bytes 245768 | tf_op jit(solution)/shard_map/ppermute | solution.py:24
  31.8 5.1 %collective-permute-start.6 = (f32[160,128]{1,0:T(8,128)S(1)}, f32[160,128]{1,0:T(8,128)S(1)}, u32[]{:S(2)}, u32[]{:S(2)}) collective-permute-start(f32[160,128]{1,0:T(8,128)S(1)} %collective-permute-done.3), channel_id=1, source_target_pairs={{0,1},{1,2},{2,3},{3,4},{4,5},{5,6},{6,7},{7,0},{8,9},{9,10},{10,1... | collective-permute-start | bytes 245768 | tf_op jit(solution)/shard_map/ppermute | solution.py:24
  32.7 4.2 %collective-permute-start.7 = (f32[160,128]{1,0:T(8,128)S(1)}, f32[160,128]{1,0:T(8,128)S(1)}, u32[]{:S(2)}, u32[]{:S(2)}) collective-permute-start(f32[160,128]{1,0:T(8,128)S(1)} %collective-permute-done.4), channel_id=1, source_target_pairs={{0,7},{1,0},{2,1},{3,2},{4,3},{5,4},{6,5},{7,6},{8,15},{9,8},{10,9... | collective-permute-start | bytes 245768 | tf_op jit(solution)/shard_map/ppermute | solution.py:24
  37.1 7.5 %collective-permute-start.10 = (f32[8,80,128]{2,1,0:T(8,128)S(1)}, f32[8,80,128]{2,1,0:T(8,128)S(1)}, u32[]{:S(2)}, u32[]{:S(2)}) collective-permute-start(f32[8,80,128]{2,1,0:T(8,128)S(1)} %get-tuple-element.67), channel_id=1, source_target_pairs={{0,8},{8,16},{16,24},{24,0},{32,56},{40,32},{48,40},{56,48},{1,9},... | collective-permute-start | bytes 983048 | tf_op jit(solution)/shard_map/ppermute | solution.py:34
  39.6 7.1 %collective-permute-start.11 = (f32[8,80,128]{2,1,0:T(8,128)S(1)}, f32[8,80,128]{2,1,0:T(8,128)S(1)}, u32[]{:S(2)}, u32[]{:S(2)}) collective-permute-start(f32[8,80,128]{2,1,0:T(8,128)S(1)} %get-tuple-element.67), channel_id=1, source_target_pairs={{0,24},{8,0},{16,8},{24,16},{32,40},{40,48},{48,56},{56,32},{1,25}... | collective-permute-start | bytes 983048 | tf_op jit(solution)/shard_map/ppermute | solution.py:34
  39.6 7.1 %collective-permute-start.13 = (f32[8,80,128]{2,1,0:T(8,128)S(1)}, f32[8,80,128]{2,1,0:T(8,128)S(1)}, u32[]{:S(2)}, u32[]{:S(2)}) collective-permute-start(f32[8,80,128]{2,1,0:T(8,128)S(1)} %get-tuple-element.66), channel_id=1, source_target_pairs={{0,192},{64,0},{128,64},{192,128},{1,193},{65,1},{129,65},{193,129... | collective-permute-start | bytes 983048 | tf_op jit(solution)/shard_map/ppermute | solution.py:24
  39.6 7.1 %collective-permute-start.12 = (f32[8,80,128]{2,1,0:T(8,128)S(1)}, f32[8,80,128]{2,1,0:T(8,128)S(1)}, u32[]{:S(2)}, u32[]{:S(2)}) collective-permute-start(f32[8,80,128]{2,1,0:T(8,128)S(1)} %get-tuple-element.66), channel_id=1, source_target_pairs={{0,64},{64,128},{128,192},{192,0},{1,65},{65,129},{129,193},{193,1... | collective-permute-start | bytes 983048 | tf_op jit(solution)/shard_map/ppermute | solution.py:24
  41.1 3.4 %collective-permute-start.14 = (f32[160,128]{1,0:T(8,128)S(1)}, f32[160,128]{1,0:T(8,128)S(1)}, u32[]{:S(2)}, u32[]{:S(2)}) collective-permute-start(f32[160,128]{1,0:T(8,128)S(1)} %pad_maximum_fusion.4), channel_id=1, source_target_pairs={{0,8},{8,0},{16,24},{24,16},{1,9},{9,1},{17,25},{25,17},{2,10},{10... | collective-permute-start | bytes 245768 | tf_op jit(solution)/shard_map/ppermute | solution.py:39
  46.8 7.5 %collective-permute-start.19 = (f32[2,160,128]{2,1,0:T(8,128)S(1)}, f32[2,160,128]{2,1,0:T(8,128)S(1)}, u32[]{:S(2)}, u32[]{:S(2)}) collective-permute-start(f32[2,160,128]{2,1,0:T(8,128)S(1)} %pad_maximum_fusion.3), channel_id=1, source_target_pairs={{0,16},{8,24},{16,0},{24,8},{1,17},{9,25},{17,1},{25,9},{2,18},{10... | collective-permute-start | bytes 491528 | tf_op jit(solution)/shard_map/ppermute | solution.py:39
  48.6 6.4 %collective-permute-start.18 = (f32[4,80,128]{2,1,0:T(8,128)S(1)}, f32[4,80,128]{2,1,0:T(8,128)S(1)}, u32[]{:S(2)}, u32[]{:S(2)}) collective-permute-start(f32[4,80,128]{2,1,0:T(8,128)S(1)} %slice.43), channel_id=1, source_target_pairs={{0,192},{64,0},{128,64},{192,128},{1,193},{65,1},{129,65},{193,129... | collective-permute-start | bytes 491528 | tf_op jit(solution)/shard_map/ppermute | solution.py:24
  48.7 7.8 %collective-permute-start.17 = (f32[4,80,128]{2,1,0:T(8,128)S(1)}, f32[4,80,128]{2,1,0:T(8,128)S(1)}, u32[]{:S(2)}, u32[]{:S(2)}) collective-permute-start(f32[4,80,128]{2,1,0:T(8,128)S(1)} %slice.42), channel_id=1, source_target_pairs={{0,64},{64,128},{128,192},{192,0},{1,65},{65,129},{129,193},{193,1... | collective-permute-start | bytes 491528 | tf_op jit(solution)/shard_map/ppermute | solution.py:24
  50.1 6.3 %collective-permute-start.16 = (f32[4,80,128]{2,1,0:T(8,128)S(1)}, f32[4,80,128]{2,1,0:T(8,128)S(1)}, u32[]{:S(2)}, u32[]{:S(2)}) collective-permute-start(f32[4,80,128]{2,1,0:T(8,128)S(1)} %slice.41), channel_id=1, source_target_pairs={{0,24},{8,0},{16,8},{24,16},{32,40},{40,48},{48,56},{56,32},{1,25}... | collective-permute-start | bytes 491528 | tf_op jit(solution)/shard_map/ppermute | solution.py:34
  51.6 4.8 %collective-permute-start.15 = (f32[4,80,128]{2,1,0:T(8,128)S(1)}, f32[4,80,128]{2,1,0:T(8,128)S(1)}, u32[]{:S(2)}, u32[]{:S(2)}) collective-permute-start(f32[4,80,128]{2,1,0:T(8,128)S(1)} %slice.40), channel_id=1, source_target_pairs={{0,8},{8,16},{16,24},{24,0},{32,56},{40,32},{48,40},{56,48},{1,9},... | collective-permute-start | bytes 491528 | tf_op jit(solution)/shard_map/ppermute | solution.py:34
  56.5 3.0 %copy-start.6 = (f32[8,320,128]{2,1,0:T(8,128)}, f32[8,320,128]{2,1,0:T(8,128)S(1)}, u32[]{:S(2)}) copy-start(f32[8,320,128]{2,1,0:T(8,128)S(1)} %pad_maximum_fusion.1.refs_8_) | copy-start | bytes 3932164
  56.5 24.8 %collective-permute-start.23 = (f32[8,320,128]{2,1,0:T(8,128)S(1)}, f32[8,320,128]{2,1,0:T(8,128)S(1)}, u32[]{:S(2)}, u32[]{:S(2)}) collective-permute-start(f32[8,320,128]{2,1,0:T(8,128)S(1)} %pad_maximum_fusion.1.refs_8_), channel_id=1, source_target_pairs={{0,24},{8,0},{16,8},{24,16},{32,40},{40,48},{48,56},{56,32},{1,25}... | collective-permute-start | bytes 3932168 | tf_op jit(solution)/shard_map/ppermute | solution.py:34
  56.6 26.4 %collective-permute-start.22 = (f32[8,320,128]{2,1,0:T(8,128)S(1)}, f32[8,320,128]{2,1,0:T(8,128)S(1)}, u32[]{:S(2)}, u32[]{:S(2)}) collective-permute-start(f32[8,320,128]{2,1,0:T(8,128)S(1)} %pad_maximum_fusion.1.refs_8_), channel_id=1, source_target_pairs={{0,8},{8,16},{16,24},{24,0},{32,56},{40,32},{48,40},{56,48},{1,9},... | collective-permute-start | bytes 3932168 | tf_op jit(solution)/shard_map/ppermute | solution.py:34
  59.3 1.7 %copy-start.1 = (s32[2048,8]{0,1:T(8,128)S(1)}, s32[2048,8]{0,1:T(8,128)}, u32[]{:S(2)}) copy-start(s32[2048,8]{0,1:T(8,128)} %param.7) | copy-start | bytes 196612
  59.3 1.7 %copy-start.2 = (s32[2048,8]{0,1:T(8,128)S(1)}, s32[2048,8]{0,1:T(8,128)}, u32[]{:S(2)}) copy-start(s32[2048,8]{0,1:T(8,128)} %param.8) | copy-start | bytes 196612
  59.3 1.7 %copy-start.3 = (s32[2048,8]{0,1:T(8,128)S(1)}, s32[2048,8]{0,1:T(8,128)}, u32[]{:S(2)}) copy-start(s32[2048,8]{0,1:T(8,128)} %param.9) | copy-start | bytes 196612
  59.4 1.7 %copy-start.4 = (s32[2048]{0:T(1024)S(1)}, s32[2048]{0:T(1024)}, u32[]{:S(2)}) copy-start(s32[2048]{0:T(1024)} %param.11) | copy-start | bytes 24580
  59.5 23.7 %copy-start.7 = (f32[4,8,80,128]{3,2,1,0:T(8,128)}, f32[4,8,80,128]{3,2,1,0:T(8,128)S(1)}, u32[]{:S(2)}) copy-start(f32[4,8,80,128]{3,2,1,0:T(8,128)S(1)} %pad_maximum_fusion.refs_3_) | copy-start | bytes 3932164
  59.5 23.6 %collective-permute-start.21 = (f32[4,8,80,128]{3,2,1,0:T(8,128)S(1)}, f32[4,8,80,128]{3,2,1,0:T(8,128)S(1)}, u32[]{:S(2)}, u32[]{:S(2)}) collective-permute-start(f32[4,8,80,128]{3,2,1,0:T(8,128)S(1)} %pad_maximum_fusion.refs_3_), channel_id=1, source_target_pairs={{0,192},{64,0},{128,64},{192,128},{1,193},{65,1},{129,65},{193,129... | collective-permute-start | bytes 3932168 | tf_op jit(solution)/shard_map/ppermute | solution.py:24
  60.5 22.6 %collective-permute-start.20 = (f32[4,8,80,128]{3,2,1,0:T(8,128)S(1)}, f32[4,8,80,128]{3,2,1,0:T(8,128)S(1)}, u32[]{:S(2)}, u32[]{:S(2)}) collective-permute-start(f32[4,8,80,128]{3,2,1,0:T(8,128)S(1)} %pad_maximum_fusion.refs_3_), channel_id=1, source_target_pairs={{0,64},{64,128},{128,192},{192,0},{1,65},{65,129},{129,193},{193,1... | collective-permute-start | bytes 3932168 | tf_op jit(solution)/shard_map/ppermute | solution.py:24
  62.0 21.2 %copy-start = (f32[128,512]{1,0:T(8,128)}, f32[128,512]{1,0:T(8,128)S(1)}, u32[]{:S(2)}) copy-start(f32[128,512]{1,0:T(8,128)S(1)} %shard_map.64.refs_0_) | copy-start | bytes 786436
  62.0 14.4 %collective-permute-start.24 = (f32[128,512]{1,0:T(8,128)S(1)}, f32[128,512]{1,0:T(8,128)S(1)}, u32[]{:S(2)}, u32[]{:S(2)}) collective-permute-start(f32[128,512]{1,0:T(8,128)S(1)} %shard_map.64.refs_0_), channel_id=1, source_target_pairs={{0,32},{32,0},{1,33},{33,1},{2,34},{34,2},{3,35},{35,3},{4,36},{36... | collective-permute-start | bytes 786440 | tf_op jit(solution)/shard_map/ppermute | solution.py:317
  76.4 27.8 %copy-start.16 = (f32[128,512]{1,0:T(8,128)}, f32[128,512]{1,0:T(8,128)S(1)}, u32[]{:S(2)}) copy-start(f32[128,512]{1,0:T(8,128)S(1)} %collective-permute-done.24.refs_1_) | copy-start | bytes 786436
  81.3 1.9 %copy-start.8 = (f32[8,320,128]{2,1,0:T(8,128)}, f32[8,320,128]{2,1,0:T(8,128)S(1)}, u32[]{:S(2)}) copy-start(f32[8,320,128]{2,1,0:T(8,128)S(1)} %collective-permute-done.23.refs_12_) | copy-start | bytes 3932164
  83.1 4.9 %copy-start.11 = (f32[4,8,80,128]{3,2,1,0:T(8,128)}, f32[4,8,80,128]{3,2,1,0:T(8,128)S(1)}, u32[]{:S(2)}) copy-start(f32[4,8,80,128]{3,2,1,0:T(8,128)S(1)} %collective-permute-done.20.refs_4_) | copy-start | bytes 3932164
  84.2 15.1 %collective-permute-start.28 = (f32[4,320,128]{2,1,0:T(8,128)S(1)}, f32[4,320,128]{2,1,0:T(8,128)S(1)}, u32[]{:S(2)}, u32[]{:S(2)}) collective-permute-start(f32[4,320,128]{2,1,0:T(8,128)S(1)} %slice.47), channel_id=1, source_target_pairs={{0,24},{8,0},{16,8},{24,16},{32,40},{40,48},{48,56},{56,32},{1,25}... | collective-permute-start | bytes 1966088 | tf_op jit(solution)/shard_map/ppermute | solution.py:34
  84.6 14.7 %collective-permute-start.27 = (f32[4,320,128]{2,1,0:T(8,128)S(1)}, f32[4,320,128]{2,1,0:T(8,128)S(1)}, u32[]{:S(2)}, u32[]{:S(2)}) collective-permute-start(f32[4,320,128]{2,1,0:T(8,128)S(1)} %slice.46), channel_id=1, source_target_pairs={{0,8},{8,16},{16,24},{24,0},{32,56},{40,32},{48,40},{56,48},{1,9},... | collective-permute-start | bytes 1966088 | tf_op jit(solution)/shard_map/ppermute | solution.py:34
  88.0 11.3 %collective-permute-start.26 = (f32[2,8,80,128]{3,2,1,0:T(8,128)S(1)}, f32[2,8,80,128]{3,2,1,0:T(8,128)S(1)}, u32[]{:S(2)}, u32[]{:S(2)}) collective-permute-start(f32[2,8,80,128]{3,2,1,0:T(8,128)S(1)} %slice.45), channel_id=1, source_target_pairs={{0,192},{64,0},{128,64},{192,128},{1,193},{65,1},{129,65},{193,129... | collective-permute-start | bytes 1966088 | tf_op jit(solution)/shard_map/ppermute | solution.py:24
  88.0 12.5 %collective-permute-start.25 = (f32[2,8,80,128]{3,2,1,0:T(8,128)S(1)}, f32[2,8,80,128]{3,2,1,0:T(8,128)S(1)}, u32[]{:S(2)}, u32[]{:S(2)}) collective-permute-start(f32[2,8,80,128]{3,2,1,0:T(8,128)S(1)} %slice.44), channel_id=1, source_target_pairs={{0,64},{64,128},{128,192},{192,0},{1,65},{65,129},{129,193},{193,1... | collective-permute-start | bytes 1966088 | tf_op jit(solution)/shard_map/ppermute | solution.py:24
  99.3 4.9 %copy-start.12 = (f32[4,320,128]{2,1,0:T(8,128)}, f32[4,320,128]{2,1,0:T(8,128)S(1)}, u32[]{:S(2)}) copy-start(f32[4,320,128]{2,1,0:T(8,128)S(1)} %collective-permute-done.28.refs_11_) | copy-start | bytes 1966084
  99.3 4.9 %copy-start.13 = (f32[4,320,128]{2,1,0:T(8,128)}, f32[4,320,128]{2,1,0:T(8,128)S(1)}, u32[]{:S(2)}) copy-start(f32[4,320,128]{2,1,0:T(8,128)S(1)} %collective-permute-done.27.refs_10_) | copy-start | bytes 1966084
  99.3 4.9 %copy-start.14 = (f32[2,8,80,128]{3,2,1,0:T(8,128)}, f32[2,8,80,128]{3,2,1,0:T(8,128)S(1)}, u32[]{:S(2)}) copy-start(f32[2,8,80,128]{3,2,1,0:T(8,128)S(1)} %collective-permute-done.26.refs_6_) | copy-start | bytes 1966084
  100.5 3.6 %copy-start.15 = (f32[2,8,80,128]{3,2,1,0:T(8,128)}, f32[2,8,80,128]{3,2,1,0:T(8,128)S(1)}, u32[]{:S(2)}) copy-start(f32[2,8,80,128]{3,2,1,0:T(8,128)S(1)} %collective-permute-done.25.refs_5_) | copy-start | bytes 1966084
  115.1 16.9 %collective-permute-start.30 = (f32[2,1024,128]{2,1,0:T(8,128)}, f32[2,1024,128]{2,1,0:T(8,128)S(1)}, u32[]{:S(2)}, u32[]{:S(2)}) collective-permute-start(f32[2,1024,128]{2,1,0:T(8,128)} %get-tuple-element.61), channel_id=1, source_target_pairs={{0,32},{32,0},{1,33},{33,1},{2,34},{34,2},{3,35},{35,3},{4,36},{36... | collective-permute-start | bytes 3145736 | tf_op jit(solution)/shard_map/ppermute | solution.py:326
  125.2 6.8 %collective-permute-start.31 = (f32[2,1024,128]{2,1,0:T(8,128)}, f32[2,1024,128]{2,1,0:T(8,128)S(1)}, u32[]{:S(2)}, u32[]{:S(2)}) collective-permute-start(f32[2,1024,128]{2,1,0:T(8,128)} %get-tuple-element.62), channel_id=1, source_target_pairs={{0,32},{32,0},{1,33},{33,1},{2,34},{34,2},{3,35},{35,3},{4,36},{36... | collective-permute-start | bytes 3145736 | tf_op jit(solution)/shard_map/ppermute | solution.py:326
  125.3 6.7 %collective-permute-start.32 = (f32[2,1024,128]{2,1,0:T(8,128)}, f32[2,1024,128]{2,1,0:T(8,128)S(1)}, u32[]{:S(2)}, u32[]{:S(2)}) collective-permute-start(f32[2,1024,128]{2,1,0:T(8,128)} %get-tuple-element.63), channel_id=1, source_target_pairs={{0,32},{32,0},{1,33},{33,1},{2,34},{34,2},{3,35},{35,3},{4,36},{36... | collective-permute-start | bytes 3145736 | tf_op jit(solution)/shard_map/ppermute | solution.py:326
  131.8 3.0 %collective-permute-start.29 = (f32[2,1024,128]{2,1,0:T(8,128)}, f32[2,1024,128]{2,1,0:T(8,128)S(1)}, u32[]{:S(2)}, u32[]{:S(2)}) collective-permute-start(f32[2,1024,128]{2,1,0:T(8,128)} %get-tuple-element.60), channel_id=1, source_target_pairs={{0,32},{32,0},{1,33},{33,1},{2,34},{34,2},{3,35},{35,3},{4,36},{36... | collective-permute-start | bytes 3145736 | tf_op jit(solution)/shard_map/ppermute | solution.py:326
  (3 other events, 4.3 us)
Sparse Core Ops, SparseCore 0:
  56.6 47.5 all-gather.2
where the time goes:
time: 143 us
  starting transfers between devices  64.1 us (45%)
  waiting for transfers between devices  41.5 us (29%)
  Pallas kernels  20.6 us (14%)
  between operations  13.8 us (10%)
  local copies, waits for them, and re-layouts  1.68 us (1%)
    ppermute x8, waiting for transfers between devices, turn(): lax.ppermute(value, ('y', 'core') if axis == 'y' else ('core', axis), pairs)  18.7 us
    pallas_call x2, Pallas kernels, product(): pl.pallas_call(functools.partial(product_kernel, steps, fresh), out_shape...  17 us
    ppermute x15, starting transfers between devices, shift(): return lax.ppermute(value, axis, [(i, (i + step) % n) for i in range(n)])  16.5 us
    ppermute x1, starting transfers between devices, body(): other = lax.ppermute(own, 'core', [(0, 1), (1, 0)])  13.3 us
    ppermute x8, starting transfers between devices, turn(): lax.ppermute(value, ('y', 'core') if axis == 'y' else ('core', axis), pairs)  11.4 us
    ppermute x4, starting transfers between devices, body(): lax.ppermute(block, 'core', [(0, 1), (1, 0)])  10.8 us
    ppermute x15, waiting for transfers between devices, shift(): return lax.ppermute(value, axis, [(i, (i + step) % n) for i in range(n)])  9.68 us
    ppermute x1, starting transfers between devices, swap_halves(): return lax.ppermute(flat, ('core', 'z'), pairs)  6.28 us
  transfers between devices with their start and end apart: 34, of which 15 were waited for; matrix products, arithmetic and copies ran while one was open for 1% of the time, Pallas kernels for 6%

commit v1 on v0

--- a/solution.py
+++ b/solution.py
@@ -133,11 +133,11 @@
 
 def product_kernel(steps, fresh, *refs):
     count = len(steps)
-    own_ref, other_ref = refs[:2]
-    a_ref, b_refs, c_refs = refs[2], refs[3:8], refs[8:13]
-    refs = refs[13 + (0 if fresh else 1) :]
-    out_ref, send_refs = refs[0], refs[1 : 1 + count]
-    a_all, b_all, c_all, left_all, kept, given, sems, out_sems = refs[1 + count :]
+    mix_refs = refs[:2]
+    parts = 2 if steps == (2,) else count
+    a_ref, b_refs, c_refs = refs[2], refs[3:8], refs[8 : 8 + parts]
+    refs = refs[8 + parts + (0 if fresh else 1) :]
+    out_ref, send_ref, a_all, b_all, c_all, mix_all, left_all, kept, given, sems, out_sems = refs
     core, x, z = (lax.axis_index(name) for name in ("core", "x", "z"))
 
     def arrive(n):
@@ -154,9 +154,9 @@
         add(b_refs[4].at[step], b_all.at[n, 3])
         if step == 2:
             for half in range(2):
-                add(c_refs[2 + half], c_all.at[n, pl.ds(4 * half, 4)])
+                add(c_refs[half], c_all.at[n, pl.ds(4 * half, 4)])
         else:
-            add(c_refs[(0, 1, None, 4)[step]], c_all.at[n])
+            add(c_refs[n], c_all.at[n])
         return copies
 
     def leave(n, q):
@@ -165,12 +165,17 @@
             pltpu.make_async_copy(
                 kept.at[n, q].reshape(SLOTS, 8, NS), out_ref.at[:, rows, :], out_sems.at[n, q]
             ),
-            pltpu.make_async_copy(given.at[n, q], send_refs[n].at[q], out_sems.at[n, 2 + q]),
+            pltpu.make_async_copy(given.at[n, q], send_ref.at[n, q], out_sems.at[n, 2 + q]),
         )
 
-    for copy in arrive(0):
+    mixes = [
+        pltpu.make_async_copy(mix_refs[m], mix_all.at[pl.ds(m * SLOTS, SLOTS)], out_sems.at[0, m]) for m in range(2)
+    ]
+    for copy in mixes + arrive(0):
         copy.start()
-    mix = jnp.concatenate([own_ref[...], other_ref[...]], axis=0)
+    for copy in mixes:
+        copy.wait()
+    mix = mix_all[...]
     mix_high = mix.astype(BF16)
     left_all[: 2 * SLOTS, :] = mix_high
     left_all[2 * SLOTS :, :] = (mix - mix_high.astype(F32)).astype(BF16)
@@ -222,9 +227,7 @@
 
 
 def product(steps, own, other, a_part, b_parts, c_parts, out):
-    vmem = pl.BlockSpec(memory_space=pltpu.VMEM)
     anywhere = pl.BlockSpec(memory_space=pl.ANY)
-    hbm = pl.BlockSpec(memory_space=pltpu.HBM)
     fresh, count = out is None, len(steps)
     operands = [own, other, a_part, *b_parts, *c_parts] + ([] if fresh else [out])
     flops = 2 * 8 * 768 * 512 * 256
@@ -232,14 +235,15 @@
         functools.partial(product_kernel, steps, fresh),
         out_shape=(
             jax.ShapeDtypeStruct((SLOTS, NS, NS), F32),
-            *[jax.ShapeDtypeStruct((2, SLOTS * 8, NS), F32)] * count,
+            jax.ShapeDtypeStruct((count, 2, SLOTS * 8, NS), F32),
         ),
-        in_specs=[vmem, vmem, hbm] + [anywhere] * (len(operands) - 3),
-        out_specs=(anywhere,) * (1 + count),
+        in_specs=[anywhere] * len(operands),
+        out_specs=(anywhere, anywhere),
         scratch_shapes=[
             pltpu.VMEM((count, NZ, NY * FLAT[0], NS), F32),
             pltpu.VMEM((count, NY, NZ, FLAT[1], NS), F32),
             pltpu.VMEM((count, NZ, NY * FLAT[2], NS), F32),
+            pltpu.VMEM((2 * SLOTS, 512), F32),
             pltpu.VMEM((4 * SLOTS, 512), BF16),
             pltpu.VMEM((count, 2, SLOTS * 8, NS), F32),
             pltpu.VMEM((count, 2, SLOTS * 8, NS), F32),
@@ -252,17 +256,15 @@
     )(*operands)
 
 
-def place_kernel(steps, *refs):
-    count = len(steps)
-    blocks, out_ref, sems = refs[:count], refs[-2], refs[-1]
+def place_kernel(steps, blocks_ref, _, out_ref, sems):
     core, x = lax.axis_index("core"), lax.axis_index("x")
     copies = []
     for n, step in enumerate(steps):
         tile = 4 * before(x, 1 - core, step) + 1 - core
         for q in range(2):
             rows = pl.ds(pl.multiple_of(8 * (tile + 2 * q), 8), 8)
-            source = blocks[n].at[q].reshape(SLOTS, 8, NS)
-            copies.append(pltpu.make_async_copy(source, out_ref.at[:, rows, :], sems.at[2 * n + q]))
+            source = blocks_ref.at[n, q].reshape(SLOTS, 8, NS)
+            copies.append(pltpu.make_async_copy(source, out_ref.at[:, rows, :], sems.at[n, q]))
     for copy in copies:
         copy.start()
     for copy in copies:
@@ -272,17 +274,17 @@
 def place(steps, blocks, out):
     anywhere = pl.BlockSpec(memory_space=pl.ANY)
     vmem = pl.BlockSpec(memory_space=pltpu.VMEM)
-    count = len(blocks)
+    count = len(steps)
     return pl.pallas_call(
         functools.partial(place_kernel, steps),
         out_shape=jax.ShapeDtypeStruct(out.shape, F32),
-        in_specs=[vmem] * count + [anywhere],
+        in_specs=[vmem, anywhere],
         out_specs=anywhere,
-        scratch_shapes=[pltpu.SemaphoreType.DMA((2 * count,))],
-        input_output_aliases={count: 0},
+        scratch_shapes=[pltpu.SemaphoreType.DMA((count, 2))],
+        input_output_aliases={1: 0},
         compiler_params=pltpu.CompilerParams(vmem_limit_bytes=8 << 20),
         cost_estimate=pl.CostEstimate(flops=0, bytes_accessed=count << 21, transcendentals=0),
-    )(*blocks, out)
+    )(blocks, out)
 
 
 def body(slater, couple_type, couple_multipole, couple_angle, angular, owner_map):
@@ -318,14 +320,17 @@
     y_1, y_3, x_1, x_3, other = together(y_1, y_3, x_1, x_3, other)
     y_2 = shift(y_1[:2], "y", 1), shift(y_3[2:], "y", -1)
     x_2 = turn(x_1[:4], "x", 1), turn(x_3[4:], "x", -1)
-
-    b_parts, c_parts = [b_x, y_1, *y_2, y_3], [c_y, x_1, *x_2, x_3]
-    out, received = None, []
-    for steps in ((0, 1, 2), (3,)):
-        out, *given = product(steps, own, other, a_z, b_parts, c_parts, out)
-        received += [lax.ppermute(block, "core", [(0, 1), (1, 0)]) for block in given]
-    out = place((0, 1, 2), received[:3], out)
-    return place((3,), received[3:], out)
+    *y_2, x_20, x_21 = together(*y_2, *x_2)
+    x_2 = x_20, x_21
+
+    b_parts = [b_x, y_1, *y_2, y_3]
+    out = None
+    received = []
+    for steps, c_parts in (((0, 1, 3), (c_y, x_1, x_3)), ((2,), x_2)):
+        out, given = product(steps, own, other, a_z, b_parts, c_parts, out)
+        received.append(lax.ppermute(given, "core", [(0, 1), (1, 0)]))
+    out = place((0, 1, 3), received[0], out)
+    return place((2,), received[1], out)
 
 
 def solution(mesh):

time: 143 us -> 141 us (0.986)
  Pallas kernels: 20.6 us -> 18.8 us
    ppermute x8, waiting for transfers between devices: 18.7 us -> 8.88 us  [turn(): lax.ppermute(value, ('y', 'core') if axis == 'y' else ('core', axis), pairs)]
    ppermute x15, waiting for transfers between devices: 9.68 us -> 19.4 us  [shift(): return lax.ppermute(value, axis, [(i, (i + step) % n) for i in range(n)])]
    pallas_call x2, Pallas kernels: 17 us -> 15.2 us  [product(): pl.pallas_call(functools.partial(product_kernel, steps, fresh), out_shape...]
    ppermute x4 -> x2, starting transfers between devices: 10.8 us -> 10.6 us  [body(): received.append(lax.ppermute(given, 'core', [(0, 1), (1, 0)]))]
  transfers between devices with their start and end apart: 34 -> 32, of which waited for: 15 -> 16; matrix products, arithmetic and copies ran while one was open for 1% -> 1% of each run, Pallas kernels for 6% -> 5%
where the time goes in v1:
time: 141 us
  starting transfers between devices  63.9 us (45%)
  waiting for transfers between devices  41.4 us (29%)
  Pallas kernels  18.8 us (13%)
  between operations  13.8 us (10%)
  local copies, waits for them, and re-layouts  1.8 us (1%)
    ppermute x15, waiting for transfers between devices, shift(): return lax.ppermute(value, axis, [(i, (i + step) % n) for i in range(n)])  19.4 us
    ppermute x15, starting transfers between devices, shift(): return lax.ppermute(value, axis, [(i, (i + step) % n) for i in range(n)])  16.5 us
    pallas_call x2, Pallas kernels, product(): pl.pallas_call(functools.partial(product_kernel, steps, fresh), out_shape...  15.2 us
    ppermute x1, starting transfers between devices, body(): other = lax.ppermute(own, 'core', [(0, 1), (1, 0)])  13.3 us
    ppermute x8, starting transfers between devices, turn(): lax.ppermute(value, ('y', 'core') if axis == 'y' else ('core', axis), pairs)  11.4 us
    ppermute x2, starting transfers between devices, body(): received.append(lax.ppermute(given, 'core', [(0, 1), (1, 0)]))  10.6 us
    ppermute x8, waiting for transfers between devices, turn(): lax.ppermute(value, ('y', 'core') if axis == 'y' else ('core', axis), pairs)  8.88 us
    ppermute x1, starting transfers between devices, swap_halves(): return lax.ppermute(flat, ('core', 'z'), pairs)  6.28 us
  transfers between devices with their start and end apart: 32, of which 16 were waited for; matrix products, arithmetic and copies ran while one was open for 1% of the time, Pallas kernels for 5%

profile of v1, /device:TPU:1, one launch (start us, length us, event | category | flops | bytes accessed | tf_op | source)
XLA Modules:
  0.0 140.7 jit_solution(5253067489915611912)
XLA Ops:
  6.5 6.3 %collective-permute-start = (f32[200,128]{1,0:T(8,128)}, f32[200,128]{1,0:T(8,128)S(1)}, u32[]{:S(2)}, u32[]{:S(2)}) collective-permute-start(f32[200,128]{1,0:T(8,128)} %bitcast.42), channel_id=1, source_target_pairs={{0,0},{1,1},{2,32},{3,33},{4,4},{5,5},{6,36},{7,37},{32,2},{33,3},... | collective-permute-start | bytes 307208 | tf_op jit(solution)/shard_map/ppermute | solution.py:51
  12.8 2.5 %collective-permute-done = f32[200,128]{1,0:T(8,128)S(1)} collective-permute-done((f32[200,128]{1,0:T(8,128)}, f32[200,128]{1,0:T(8,128)S(1)}, u32[]{:S(2)}, u32[]{:S(2)}) %collective-permute-start) | collective-permute-done | bytes 102432 | tf_op jit(solution)/shard_map/ppermute | solution.py:51
  15.4 1.3 collective-permute-start.5
  16.7 2.4 %collective-permute-start.3 = (f32[160,128]{1,0:T(8,128)S(1)}, f32[160,128]{1,0:T(8,128)S(1)}, u32[]{:S(2)}, u32[]{:S(2)}) collective-permute-start(f32[160,128]{1,0:T(8,128)S(1)} %slice.48), channel_id=1, source_target_pairs={{0,2},{1,3},{2,4},{3,5},{4,6},{5,7},{6,0},{7,1},{8,10},{9,11},{10,... | collective-permute-start | bytes 245768 | tf_op jit(solution)/shard_map/ppermute | solution.py:24
  19.0 3.6 %collective-permute-start.2 = (f32[160,128]{1,0:T(8,128)S(1)}, f32[160,128]{1,0:T(8,128)S(1)}, u32[]{:S(2)}, u32[]{:S(2)}) collective-permute-start(f32[160,128]{1,0:T(8,128)S(1)} %slice.48), channel_id=1, source_target_pairs={{0,7},{1,0},{2,1},{3,2},{4,3},{5,4},{6,5},{7,6},{8,15},{9,8},{10,9... | collective-permute-start | bytes 245768 | tf_op jit(solution)/shard_map/ppermute | solution.py:24
  22.6 4.2 %collective-permute-done.3 = f32[160,128]{1,0:T(8,128)S(1)} collective-permute-done((f32[160,128]{1,0:T(8,128)S(1)}, f32[160,128]{1,0:T(8,128)S(1)}, u32[]{:S(2)}, u32[]{:S(2)}) %collective-permute-start.3) | collective-permute-done | bytes 81952 | tf_op jit(solution)/shard_map/ppermute | solution.py:24
  26.9 0.4 collective-permute-done.1
  27.2 2.6 %collective-permute-start.9 = (f32[80,128]{1,0:T(8,128)S(1)}, f32[80,128]{1,0:T(8,128)S(1)}, u32[]{:S(2)}, u32[]{:S(2)}) collective-permute-start(f32[80,128]{1,0:T(8,128)S(1)} %pad_maximum_fusion.5), channel_id=1, source_target_pairs={{0,128},{64,192},{128,0},{192,64},{1,129},{65,193},{129,1},{193,65... | collective-permute-start | bytes 122888 | tf_op jit(solution)/shard_map/ppermute | solution.py:39
  29.9 1.9 %collective-permute-start.8 = (f32[160,128]{1,0:T(8,128)S(1)}, f32[160,128]{1,0:T(8,128)S(1)}, u32[]{:S(2)}, u32[]{:S(2)}) collective-permute-start(f32[160,128]{1,0:T(8,128)S(1)} %collective-permute-done.3), channel_id=1, source_target_pairs={{0,2},{1,3},{2,4},{3,5},{4,6},{5,7},{6,0},{7,1},{8,10},{9,11},{10,... | collective-permute-start | bytes 245768 | tf_op jit(solution)/shard_map/ppermute | solution.py:24
  31.8 0.9 collective-permute-start.6
  32.7 1.8 %collective-permute-start.7 = (f32[160,128]{1,0:T(8,128)S(1)}, f32[160,128]{1,0:T(8,128)S(1)}, u32[]{:S(2)}, u32[]{:S(2)}) collective-permute-start(f32[160,128]{1,0:T(8,128)S(1)} %collective-permute-done.4), channel_id=1, source_target_pairs={{0,7},{1,0},{2,1},{3,2},{4,3},{5,4},{6,5},{7,6},{8,15},{9,8},{10,9... | collective-permute-start | bytes 245768 | tf_op jit(solution)/shard_map/ppermute | solution.py:24
  34.4 2.4 %collective-permute-done.7 = f32[160,128]{1,0:T(8,128)S(1)} collective-permute-done((f32[160,128]{1,0:T(8,128)S(1)}, f32[160,128]{1,0:T(8,128)S(1)}, u32[]{:S(2)}, u32[]{:S(2)}) %collective-permute-start.7) | collective-permute-done | bytes 81952 | tf_op jit(solution)/shard_map/ppermute | solution.py:24
  37.1 2.6 %collective-permute-start.10 = (f32[8,80,128]{2,1,0:T(8,128)S(1)}, f32[8,80,128]{2,1,0:T(8,128)S(1)}, u32[]{:S(2)}, u32[]{:S(2)}) collective-permute-start(f32[8,80,128]{2,1,0:T(8,128)S(1)} %get-tuple-element.71), channel_id=1, source_target_pairs={{0,8},{8,16},{16,24},{24,0},{32,56},{40,32},{48,40},{56,48},{1,9},... | collective-permute-start | bytes 983048 | tf_op jit(solution)/shard_map/ppermute | solution.py:34
  39.6 1.5 %collective-permute-start.12 = (f32[8,80,128]{2,1,0:T(8,128)S(1)}, f32[8,80,128]{2,1,0:T(8,128)S(1)}, u32[]{:S(2)}, u32[]{:S(2)}) collective-permute-start(f32[8,80,128]{2,1,0:T(8,128)S(1)} %get-tuple-element.70), channel_id=1, source_target_pairs={{0,64},{64,128},{128,192},{192,0},{1,65},{65,129},{129,193},{193,1... | collective-permute-start | bytes 983048 | tf_op jit(solution)/shard_map/ppermute | solution.py:24
  41.1 0.2 collective-permute-start.14
  41.3 3.2 %collective-permute-done.14 = f32[160,128]{1,0:T(8,128)S(1)} collective-permute-done((f32[160,128]{1,0:T(8,128)S(1)}, f32[160,128]{1,0:T(8,128)S(1)}, u32[]{:S(2)}, u32[]{:S(2)}) %collective-permute-start.14) | collective-permute-done | bytes 81952 | tf_op jit(solution)/shard_map/ppermute | solution.py:39
  44.5 2.2 %collective-permute-done.11 = f32[8,80,128]{2,1,0:T(8,128)S(1)} collective-permute-done((f32[8,80,128]{2,1,0:T(8,128)S(1)}, f32[8,80,128]{2,1,0:T(8,128)S(1)}, u32[]{:S(2)}, u32[]{:S(2)}) %collective-permute-start.11) | collective-permute-done | bytes 327712 | tf_op jit(solution)/shard_map/ppermute | solution.py:34
  46.8 1.7 %collective-permute-start.19 = (f32[2,160,128]{2,1,0:T(8,128)S(1)}, f32[2,160,128]{2,1,0:T(8,128)S(1)}, u32[]{:S(2)}, u32[]{:S(2)}) collective-permute-start(f32[2,160,128]{2,1,0:T(8,128)S(1)} %pad_maximum_fusion.3), channel_id=1, source_target_pairs={{0,16},{8,24},{16,0},{24,8},{1,17},{9,25},{17,1},{25,9},{2,18},{10... | collective-permute-start | bytes 491528 | tf_op jit(solution)/shard_map/ppermute | solution.py:39
  48.7 1.5 %collective-permute-start.17 = (f32[4,80,128]{2,1,0:T(8,128)S(1)}, f32[4,80,128]{2,1,0:T(8,128)S(1)}, u32[]{:S(2)}, u32[]{:S(2)}) collective-permute-start(f32[4,80,128]{2,1,0:T(8,128)S(1)} %slice.42), channel_id=1, source_target_pairs={{0,64},{64,128},{128,192},{192,0},{1,65},{65,129},{129,193},{193,1... | collective-permute-start | bytes 491528 | tf_op jit(solution)/shard_map/ppermute | solution.py:24
  50.1 1.5 %collective-permute-start.16 = (f32[4,80,128]{2,1,0:T(8,128)S(1)}, f32[4,80,128]{2,1,0:T(8,128)S(1)}, u32[]{:S(2)}, u32[]{:S(2)}) collective-permute-start(f32[4,80,128]{2,1,0:T(8,128)S(1)} %slice.41), channel_id=1, source_target_pairs={{0,24},{8,0},{16,8},{24,16},{32,40},{40,48},{48,56},{56,32},{1,25}... | collective-permute-start | bytes 491528 | tf_op jit(solution)/shard_map/ppermute | solution.py:34
  51.6 1.2 collective-permute-start.15
  52.8 1.5 %collective-permute-done.19 = f32[2,160,128]{2,1,0:T(8,128)S(1)} collective-permute-done((f32[2,160,128]{2,1,0:T(8,128)S(1)}, f32[2,160,128]{2,1,0:T(8,128)S(1)}, u32[]{:S(2)}, u32[]{:S(2)}) %collective-permute-start.19) | collective-permute-done | bytes 163872 | tf_op jit(solution)/shard_map/ppermute | solution.py:39
  54.2 0.7 pad_maximum_fusion.2
  55.0 1.4 collective-permute-done.17
  56.6 2.7 %collective-permute-start.22 = (f32[8,320,128]{2,1,0:T(8,128)S(1)}, f32[8,320,128]{2,1,0:T(8,128)S(1)}, u32[]{:S(2)}, u32[]{:S(2)}) collective-permute-start(f32[8,320,128]{2,1,0:T(8,128)S(1)} %pad_maximum_fusion.1.refs_8_), channel_id=1, source_target_pairs={{0,8},{8,16},{16,24},{24,0},{32,56},{40,32},{48,40},{56,48},{1,9},... | collective-permute-start | bytes 3932168 | tf_op jit(solution)/shard_map/ppermute | solution.py:34
  59.4 0.1 pad_maximum_fusion.refs_3_
  59.5 0.9 collective-permute-start.21
  60.5 0.6 collective-permute-start.20
  61.1 0.9 shard_map.64.refs_0_
  62.0 13.3 %collective-permute-start.24 = (f32[128,512]{1,0:T(8,128)S(1)}, f32[128,512]{1,0:T(8,128)S(1)}, u32[]{:S(2)}, u32[]{:S(2)}) collective-permute-start(f32[128,512]{1,0:T(8,128)S(1)} %shard_map.64.refs_0_), channel_id=1, source_target_pairs={{0,32},{32,0},{1,33},{33,1},{2,34},{34,2},{3,35},{35,3},{4,36},{36... | collective-permute-start | bytes 786440 | tf_op jit(solution)/shard_map/ppermute | solution.py:319
  75.2 1.2 collective-permute-done.24.refs_1_
  76.4 4.9 %collective-permute-done.23.refs_10_ = f32[8,320,128]{2,1,0:T(8,128)S(1)} collective-permute-done((f32[8,320,128]{2,1,0:T(8,128)S(1)}, f32[8,320,128]{2,1,0:T(8,128)S(1)}, u32[]{:S(2)}, u32[]{:S(2)}) %collective-permute-start.23) | collective-permute-done | bytes 1310752 | tf_op jit(solution)/shard_map/ppermute | solution.py:34
  81.3 1.7 %collective-permute-done.22.refs_9_ = f32[8,320,128]{2,1,0:T(8,128)S(1)} collective-permute-done((f32[8,320,128]{2,1,0:T(8,128)S(1)}, f32[8,320,128]{2,1,0:T(8,128)S(1)}, u32[]{:S(2)}, u32[]{:S(2)}) %collective-permute-start.22) | collective-permute-done | bytes 1310752 | tf_op jit(solution)/shard_map/ppermute | solution.py:34
  83.3 0.9 copy-done.7
  84.2 0.5 copy-done.8
  84.7 1.5 %collective-permute-start.25 = (f32[2,8,80,128]{3,2,1,0:T(8,128)S(1)}, f32[2,8,80,128]{3,2,1,0:T(8,128)S(1)}, u32[]{:S(2)}, u32[]{:S(2)}) collective-permute-start(f32[2,8,80,128]{3,2,1,0:T(8,128)S(1)} %slice.44), channel_id=1, source_target_pairs={{0,64},{64,128},{128,192},{192,0},{1,65},{65,129},{129,193},{193,1... | collective-permute-start | bytes 1966088 | tf_op jit(solution)/shard_map/ppermute | solution.py:24
  86.1 3.4 %collective-permute-start.27 = (f32[4,320,128]{2,1,0:T(8,128)S(1)}, f32[4,320,128]{2,1,0:T(8,128)S(1)}, u32[]{:S(2)}, u32[]{:S(2)}) collective-permute-start(f32[4,320,128]{2,1,0:T(8,128)S(1)} %slice.46), channel_id=1, source_target_pairs={{0,8},{8,16},{16,24},{24,0},{32,56},{40,32},{48,40},{56,48},{1,9},... | collective-permute-start | bytes 1966088 | tf_op jit(solution)/shard_map/ppermute | solution.py:34
  89.6 9.7 %collective-permute-done.26.refs_6_ = f32[2,8,80,128]{3,2,1,0:T(8,128)S(1)} collective-permute-done((f32[2,8,80,128]{3,2,1,0:T(8,128)S(1)}, f32[2,8,80,128]{3,2,1,0:T(8,128)S(1)}, u32[]{:S(2)}, u32[]{:S(2)}) %collective-permute-start.26) | collective-permute-done | bytes 655392 | tf_op jit(solution)/shard_map/ppermute | solution.py:24
  99.3 1.3 collective-permute-done.25.refs_5_
  100.6 3.6 %all-gather.3.cloned.1.call-done = f32[32,160,128]{2,1,0:T(8,128)} async-done(((f32[4,160,128]{2,1,0:T(8,128)}), f32[32,160,128]{2,1,0:T(8,128)}) %all-gather.3.cloned.1.call-update) | async-done | bytes 2621456 | tf_op jit(solution)/shard_map/all_gather | solution.py:316
  104.2 10.0 %shard_map.65 = (f32[128,128,128]{2,1,0:T(8,128)}, f32[3,2,1024,128]{3,2,1,0:T(8,128)}) custom-call(f32[128,512]{1,0:T(8,128)} %copy-done, f32[128,512]{1,0:T(8,128)} %copy-done.16, f32[8,4,160,128]{3,2,1,0:T(8,128)} %bitcast.36, f32[4,8,80,128]{3,2,1,0:T(8,128)} %copy-done.6, f32[4,8,80,128]{3,2,1,0:T(8,128)} %copy-done.8, f32[2,8,80,128]{3,2,1,0:T(8,128)} %copy-done.11, ...), custom_call_target="tpu_custom_call" | custom-call | flops 4831838208 | bytes 25165824 | tf_op jit(solution)/shard_map/pallas_call | solution.py:234
  114.2 10.5 %collective-permute-start.30 = (f32[3,2,1024,128]{3,2,1,0:T(8,128)}, f32[3,2,1024,128]{3,2,1,0:T(8,128)S(1)}, u32[]{:S(2)}, u32[]{:S(2)}) collective-permute-start(f32[3,2,1024,128]{3,2,1,0:T(8,128)} %get-tuple-element.67), channel_id=1, source_target_pairs={{0,32},{32,0},{1,33},{33,1},{2,34},{34,2},{3,35},{35,3},{4,36},{36... | collective-permute-start | bytes 9437192 | tf_op jit(solution)/shard_map/ppermute | solution.py:331
  124.7 5.1 %shard_map.66 = (f32[128,128,128]{2,1,0:T(8,128)}, f32[1,2,1024,128]{3,2,1,0:T(8,128)}) custom-call(f32[128,512]{1,0:T(8,128)} %copy-done, f32[128,512]{1,0:T(8,128)} %copy-done.16, f32[8,4,160,128]{3,2,1,0:T(8,128)} %bitcast.37, f32[4,8,80,128]{3,2,1,0:T(8,128)} %copy-done.6, f32[4,8,80,128]{3,2,1,0:T(8,128)} %copy-done.8, ...), custom_call_target="tpu_custom_call", output_to_operand_aliasing={{0}: (10, {})} | custom-call | flops 1610612736 | bytes 8388608 | tf_op jit(solution)/shard_map/pallas_call | solution.py:234
  129.9 0.1 collective-permute-start.29
  130.0 0.2 collective-permute-done.30.blocks_ref
  130.2 1.7 %shard_map.67._ = f32[128,128,128]{2,1,0:T(8,128)} custom-call(f32[3,2,1024,128]{3,2,1,0:T(8,128)S(1)} %collective-permute-done.30.blocks_ref, f32[128,128,128]{2,1,0:T(8,128)} %get-tuple-element.68._), custom_call_target="tpu_custom_call", output_to_operand_aliasing={{}: (1, {})} | custom-call | bytes 6291456 | tf_op jit(solution)/shard_map/pallas_call | solution.py:278
  131.9 0.9 collective-permute-done.29.blocks_ref
  132.8 1.0 shard_map.68
  (82 shorter events, 0.8 us)
Async XLA Ops:
  6.5 97.6 %all-gather.3.cloned.1.call-start = ((), (), s32[]{:S(2)}) async-start(), calls=%async_computation | async-start | bytes 2949120 | tf_op jit(solution)/shard_map/all_gather | solution.py:316
  6.5 8.8 %collective-permute-start = (f32[200,128]{1,0:T(8,128)}, f32[200,128]{1,0:T(8,128)S(1)}, u32[]{:S(2)}, u32[]{:S(2)}) collective-permute-start(f32[200,128]{1,0:T(8,128)} %bitcast.42), channel_id=1, source_target_pairs={{0,0},{1,1},{2,32},{3,33},{4,4},{5,5},{6,36},{7,37},{32,2},{33,3},... | collective-permute-start | bytes 307208 | tf_op jit(solution)/shard_map/ppermute | solution.py:51
  15.4 7.2 %collective-permute-start.5 = (f32[40,128]{1,0:T(8,128)S(1)}, f32[40,128]{1,0:T(8,128)S(1)}, u32[]{:S(2)}, u32[]{:S(2)}) collective-permute-start(f32[40,128]{1,0:T(8,128)S(1)} %slice.49), channel_id=1, source_target_pairs={{0,64},{64,0},{128,192},{192,128},{1,65},{65,1},{129,193},{193,129... | collective-permute-start | bytes 61448 | tf_op jit(solution)/shard_map/ppermute | solution.py:39
  16.7 5.9 %collective-permute-start.4 = (f32[160,128]{1,0:T(8,128)S(1)}, f32[160,128]{1,0:T(8,128)S(1)}, u32[]{:S(2)}, u32[]{:S(2)}) collective-permute-start(f32[160,128]{1,0:T(8,128)S(1)} %slice.48), channel_id=1, source_target_pairs={{0,6},{1,7},{2,0},{3,1},{4,2},{5,3},{6,4},{7,5},{8,14},{9,15},{10,... | collective-permute-start | bytes 245768 | tf_op jit(solution)/shard_map/ppermute | solution.py:24
  16.7 10.2 %collective-permute-start.3 = (f32[160,128]{1,0:T(8,128)S(1)}, f32[160,128]{1,0:T(8,128)S(1)}, u32[]{:S(2)}, u32[]{:S(2)}) collective-permute-start(f32[160,128]{1,0:T(8,128)S(1)} %slice.48), channel_id=1, source_target_pairs={{0,2},{1,3},{2,4},{3,5},{4,6},{5,7},{6,0},{7,1},{8,10},{9,11},{10,... | collective-permute-start | bytes 245768 | tf_op jit(solution)/shard_map/ppermute | solution.py:24
  19.0 7.8 %collective-permute-start.2 = (f32[160,128]{1,0:T(8,128)S(1)}, f32[160,128]{1,0:T(8,128)S(1)}, u32[]{:S(2)}, u32[]{:S(2)}) collective-permute-start(f32[160,128]{1,0:T(8,128)S(1)} %slice.48), channel_id=1, source_target_pairs={{0,7},{1,0},{2,1},{3,2},{4,3},{5,4},{6,5},{7,6},{8,15},{9,8},{10,9... | collective-permute-start | bytes 245768 | tf_op jit(solution)/shard_map/ppermute | solution.py:24
  22.6 4.6 %collective-permute-start.1 = (f32[160,128]{1,0:T(8,128)S(1)}, f32[160,128]{1,0:T(8,128)S(1)}, u32[]{:S(2)}, u32[]{:S(2)}) collective-permute-start(f32[160,128]{1,0:T(8,128)S(1)} %slice.48), channel_id=1, source_target_pairs={{0,1},{1,2},{2,3},{3,4},{4,5},{5,6},{6,7},{7,0},{8,9},{9,10},{10,1... | collective-permute-start | bytes 245768 | tf_op jit(solution)/shard_map/ppermute | solution.py:24
  27.2 7.2 %collective-permute-start.9 = (f32[80,128]{1,0:T(8,128)S(1)}, f32[80,128]{1,0:T(8,128)S(1)}, u32[]{:S(2)}, u32[]{:S(2)}) collective-permute-start(f32[80,128]{1,0:T(8,128)S(1)} %pad_maximum_fusion.5), channel_id=1, source_target_pairs={{0,128},{64,192},{128,0},{192,64},{1,129},{65,193},{129,1},{193,65... | collective-permute-start | bytes 122888 | tf_op jit(solution)/shard_map/ppermute | solution.py:39
  29.9 7.0 %collective-permute-start.8 = (f32[160,128]{1,0:T(8,128)S(1)}, f32[160,128]{1,0:T(8,128)S(1)}, u32[]{:S(2)}, u32[]{:S(2)}) collective-permute-start(f32[160,128]{1,0:T(8,128)S(1)} %collective-permute-done.3), channel_id=1, source_target_pairs={{0,2},{1,3},{2,4},{3,5},{4,6},{5,7},{6,0},{7,1},{8,10},{9,11},{10,... | collective-permute-start | bytes 245768 | tf_op jit(solution)/shard_map/ppermute | solution.py:24
  31.8 5.1 %collective-permute-start.6 = (f32[160,128]{1,0:T(8,128)S(1)}, f32[160,128]{1,0:T(8,128)S(1)}, u32[]{:S(2)}, u32[]{:S(2)}) collective-permute-start(f32[160,128]{1,0:T(8,128)S(1)} %collective-permute-done.3), channel_id=1, source_target_pairs={{0,1},{1,2},{2,3},{3,4},{4,5},{5,6},{6,7},{7,0},{8,9},{9,10},{10,1... | collective-permute-start | bytes 245768 | tf_op jit(solution)/shard_map/ppermute | solution.py:24
  32.7 4.2 %collective-permute-start.7 = (f32[160,128]{1,0:T(8,128)S(1)}, f32[160,128]{1,0:T(8,128)S(1)}, u32[]{:S(2)}, u32[]{:S(2)}) collective-permute-start(f32[160,128]{1,0:T(8,128)S(1)} %collective-permute-done.4), channel_id=1, source_target_pairs={{0,7},{1,0},{2,1},{3,2},{4,3},{5,4},{6,5},{7,6},{8,15},{9,8},{10,9... | collective-permute-start | bytes 245768 | tf_op jit(solution)/shard_map/ppermute | solution.py:24
  37.1 7.5 %collective-permute-start.10 = (f32[8,80,128]{2,1,0:T(8,128)S(1)}, f32[8,80,128]{2,1,0:T(8,128)S(1)}, u32[]{:S(2)}, u32[]{:S(2)}) collective-permute-start(f32[8,80,128]{2,1,0:T(8,128)S(1)} %get-tuple-element.71), channel_id=1, source_target_pairs={{0,8},{8,16},{16,24},{24,0},{32,56},{40,32},{48,40},{56,48},{1,9},... | collective-permute-start | bytes 983048 | tf_op jit(solution)/shard_map/ppermute | solution.py:34
  39.6 7.1 %collective-permute-start.11 = (f32[8,80,128]{2,1,0:T(8,128)S(1)}, f32[8,80,128]{2,1,0:T(8,128)S(1)}, u32[]{:S(2)}, u32[]{:S(2)}) collective-permute-start(f32[8,80,128]{2,1,0:T(8,128)S(1)} %get-tuple-element.71), channel_id=1, source_target_pairs={{0,24},{8,0},{16,8},{24,16},{32,40},{40,48},{48,56},{56,32},{1,25}... | collective-permute-start | bytes 983048 | tf_op jit(solution)/shard_map/ppermute | solution.py:34
  39.6 7.1 %collective-permute-start.13 = (f32[8,80,128]{2,1,0:T(8,128)S(1)}, f32[8,80,128]{2,1,0:T(8,128)S(1)}, u32[]{:S(2)}, u32[]{:S(2)}) collective-permute-start(f32[8,80,128]{2,1,0:T(8,128)S(1)} %get-tuple-element.70), channel_id=1, source_target_pairs={{0,192},{64,0},{128,64},{192,128},{1,193},{65,1},{129,65},{193,129... | collective-permute-start | bytes 983048 | tf_op jit(solution)/shard_map/ppermute | solution.py:24
  39.6 7.1 %collective-permute-start.12 = (f32[8,80,128]{2,1,0:T(8,128)S(1)}, f32[8,80,128]{2,1,0:T(8,128)S(1)}, u32[]{:S(2)}, u32[]{:S(2)}) collective-permute-start(f32[8,80,128]{2,1,0:T(8,128)S(1)} %get-tuple-element.70), channel_id=1, source_target_pairs={{0,64},{64,128},{128,192},{192,0},{1,65},{65,129},{129,193},{193,1... | collective-permute-start | bytes 983048 | tf_op jit(solution)/shard_map/ppermute | solution.py:24
  41.1 3.4 %collective-permute-start.14 = (f32[160,128]{1,0:T(8,128)S(1)}, f32[160,128]{1,0:T(8,128)S(1)}, u32[]{:S(2)}, u32[]{:S(2)}) collective-permute-start(f32[160,128]{1,0:T(8,128)S(1)} %pad_maximum_fusion.4), channel_id=1, source_target_pairs={{0,8},{8,0},{16,24},{24,16},{1,9},{9,1},{17,25},{25,17},{2,10},{10... | collective-permute-start | bytes 245768 | tf_op jit(solution)/shard_map/ppermute | solution.py:39
  46.8 7.5 %collective-permute-start.19 = (f32[2,160,128]{2,1,0:T(8,128)S(1)}, f32[2,160,128]{2,1,0:T(8,128)S(1)}, u32[]{:S(2)}, u32[]{:S(2)}) collective-permute-start(f32[2,160,128]{2,1,0:T(8,128)S(1)} %pad_maximum_fusion.3), channel_id=1, source_target_pairs={{0,16},{8,24},{16,0},{24,8},{1,17},{9,25},{17,1},{25,9},{2,18},{10... | collective-permute-start | bytes 491528 | tf_op jit(solution)/shard_map/ppermute | solution.py:39
  48.6 6.4 %collective-permute-start.18 = (f32[4,80,128]{2,1,0:T(8,128)S(1)}, f32[4,80,128]{2,1,0:T(8,128)S(1)}, u32[]{:S(2)}, u32[]{:S(2)}) collective-permute-start(f32[4,80,128]{2,1,0:T(8,128)S(1)} %slice.43), channel_id=1, source_target_pairs={{0,192},{64,0},{128,64},{192,128},{1,193},{65,1},{129,65},{193,129... | collective-permute-start | bytes 491528 | tf_op jit(solution)/shard_map/ppermute | solution.py:24
  48.7 7.8 %collective-permute-start.17 = (f32[4,80,128]{2,1,0:T(8,128)S(1)}, f32[4,80,128]{2,1,0:T(8,128)S(1)}, u32[]{:S(2)}, u32[]{:S(2)}) collective-permute-start(f32[4,80,128]{2,1,0:T(8,128)S(1)} %slice.42), channel_id=1, source_target_pairs={{0,64},{64,128},{128,192},{192,0},{1,65},{65,129},{129,193},{193,1... | collective-permute-start | bytes 491528 | tf_op jit(solution)/shard_map/ppermute | solution.py:24
  50.1 6.3 %collective-permute-start.16 = (f32[4,80,128]{2,1,0:T(8,128)S(1)}, f32[4,80,128]{2,1,0:T(8,128)S(1)}, u32[]{:S(2)}, u32[]{:S(2)}) collective-permute-start(f32[4,80,128]{2,1,0:T(8,128)S(1)} %slice.41), channel_id=1, source_target_pairs={{0,24},{8,0},{16,8},{24,16},{32,40},{40,48},{48,56},{56,32},{1,25}... | collective-permute-start | bytes 491528 | tf_op jit(solution)/shard_map/ppermute | solution.py:34
  51.6 4.8 %collective-permute-start.15 = (f32[4,80,128]{2,1,0:T(8,128)S(1)}, f32[4,80,128]{2,1,0:T(8,128)S(1)}, u32[]{:S(2)}, u32[]{:S(2)}) collective-permute-start(f32[4,80,128]{2,1,0:T(8,128)S(1)} %slice.40), channel_id=1, source_target_pairs={{0,8},{8,16},{16,24},{24,0},{32,56},{40,32},{48,40},{56,48},{1,9},... | collective-permute-start | bytes 491528 | tf_op jit(solution)/shard_map/ppermute | solution.py:34
  56.5 3.0 %copy-start.9 = (f32[8,320,128]{2,1,0:T(8,128)}, f32[8,320,128]{2,1,0:T(8,128)S(1)}, u32[]{:S(2)}) copy-start(f32[8,320,128]{2,1,0:T(8,128)S(1)} %pad_maximum_fusion.1.refs_8_) | copy-start | bytes 3932164
  56.5 24.8 %collective-permute-start.23 = (f32[8,320,128]{2,1,0:T(8,128)S(1)}, f32[8,320,128]{2,1,0:T(8,128)S(1)}, u32[]{:S(2)}, u32[]{:S(2)}) collective-permute-start(f32[8,320,128]{2,1,0:T(8,128)S(1)} %pad_maximum_fusion.1.refs_8_), channel_id=1, source_target_pairs={{0,24},{8,0},{16,8},{24,16},{32,40},{40,48},{48,56},{56,32},{1,25}... | collective-permute-start | bytes 3932168 | tf_op jit(solution)/shard_map/ppermute | solution.py:34
  56.6 26.4 %collective-permute-start.22 = (f32[8,320,128]{2,1,0:T(8,128)S(1)}, f32[8,320,128]{2,1,0:T(8,128)S(1)}, u32[]{:S(2)}, u32[]{:S(2)}) collective-permute-start(f32[8,320,128]{2,1,0:T(8,128)S(1)} %pad_maximum_fusion.1.refs_8_), channel_id=1, source_target_pairs={{0,8},{8,16},{16,24},{24,0},{32,56},{40,32},{48,40},{56,48},{1,9},... | collective-permute-start | bytes 3932168 | tf_op jit(solution)/shard_map/ppermute | solution.py:34
  59.3 1.7 %copy-start.1 = (s32[2048,8]{0,1:T(8,128)S(1)}, s32[2048,8]{0,1:T(8,128)}, u32[]{:S(2)}) copy-start(s32[2048,8]{0,1:T(8,128)} %param.7) | copy-start | bytes 196612
  59.3 1.7 %copy-start.2 = (s32[2048,8]{0,1:T(8,128)S(1)}, s32[2048,8]{0,1:T(8,128)}, u32[]{:S(2)}) copy-start(s32[2048,8]{0,1:T(8,128)} %param.8) | copy-start | bytes 196612
  59.3 1.7 %copy-start.3 = (s32[2048,8]{0,1:T(8,128)S(1)}, s32[2048,8]{0,1:T(8,128)}, u32[]{:S(2)}) copy-start(s32[2048,8]{0,1:T(8,128)} %param.9) | copy-start | bytes 196612
  59.4 1.7 %copy-start.4 = (s32[2048]{0:T(1024)S(1)}, s32[2048]{0:T(1024)}, u32[]{:S(2)}) copy-start(s32[2048]{0:T(1024)} %param.11) | copy-start | bytes 24580
  59.4 1.7 %copy-start.5 = (f32[64]{0:T(128)S(1)}, f32[64]{0:T(128)}, u32[]{:S(2)}) copy-start(f32[64]{0:T(128)} %param.10) | copy-start | bytes 772
  59.5 23.7 %copy-start.6 = (f32[4,8,80,128]{3,2,1,0:T(8,128)}, f32[4,8,80,128]{3,2,1,0:T(8,128)S(1)}, u32[]{:S(2)}) copy-start(f32[4,8,80,128]{3,2,1,0:T(8,128)S(1)} %pad_maximum_fusion.refs_3_) | copy-start | bytes 3932164
  59.5 23.6 %collective-permute-start.21 = (f32[4,8,80,128]{3,2,1,0:T(8,128)S(1)}, f32[4,8,80,128]{3,2,1,0:T(8,128)S(1)}, u32[]{:S(2)}, u32[]{:S(2)}) collective-permute-start(f32[4,8,80,128]{3,2,1,0:T(8,128)S(1)} %pad_maximum_fusion.refs_3_), channel_id=1, source_target_pairs={{0,192},{64,0},{128,64},{192,128},{1,193},{65,1},{129,65},{193,129... | collective-permute-start | bytes 3932168 | tf_op jit(solution)/shard_map/ppermute | solution.py:24
  60.5 22.6 %collective-permute-start.20 = (f32[4,8,80,128]{3,2,1,0:T(8,128)S(1)}, f32[4,8,80,128]{3,2,1,0:T(8,128)S(1)}, u32[]{:S(2)}, u32[]{:S(2)}) collective-permute-start(f32[4,8,80,128]{3,2,1,0:T(8,128)S(1)} %pad_maximum_fusion.refs_3_), channel_id=1, source_target_pairs={{0,64},{64,128},{128,192},{192,0},{1,65},{65,129},{129,193},{193,1... | collective-permute-start | bytes 3932168 | tf_op jit(solution)/shard_map/ppermute | solution.py:24
  62.0 21.2 %copy-start = (f32[128,512]{1,0:T(8,128)}, f32[128,512]{1,0:T(8,128)S(1)}, u32[]{:S(2)}) copy-start(f32[128,512]{1,0:T(8,128)S(1)} %shard_map.64.refs_0_) | copy-start | bytes 786436
  62.0 14.4 %collective-permute-start.24 = (f32[128,512]{1,0:T(8,128)S(1)}, f32[128,512]{1,0:T(8,128)S(1)}, u32[]{:S(2)}, u32[]{:S(2)}) collective-permute-start(f32[128,512]{1,0:T(8,128)S(1)} %shard_map.64.refs_0_), channel_id=1, source_target_pairs={{0,32},{32,0},{1,33},{33,1},{2,34},{34,2},{3,35},{35,3},{4,36},{36... | collective-permute-start | bytes 786440 | tf_op jit(solution)/shard_map/ppermute | solution.py:319
  76.4 27.8 %copy-start.16 = (f32[128,512]{1,0:T(8,128)}, f32[128,512]{1,0:T(8,128)S(1)}, u32[]{:S(2)}) copy-start(f32[128,512]{1,0:T(8,128)S(1)} %collective-permute-done.24.refs_1_) | copy-start | bytes 786436
  81.3 1.9 %copy-start.14 = (f32[8,320,128]{2,1,0:T(8,128)}, f32[8,320,128]{2,1,0:T(8,128)S(1)}, u32[]{:S(2)}) copy-start(f32[8,320,128]{2,1,0:T(8,128)S(1)} %collective-permute-done.23.refs_10_) | copy-start | bytes 3932164
  83.1 17.5 %copy-start.15 = (f32[8,320,128]{2,1,0:T(8,128)}, f32[8,320,128]{2,1,0:T(8,128)S(1)}, u32[]{:S(2)}) copy-start(f32[8,320,128]{2,1,0:T(8,128)S(1)} %collective-permute-done.22.refs_9_) | copy-start | bytes 3932164
  83.1 1.6 %copy-start.8 = (f32[4,8,80,128]{3,2,1,0:T(8,128)}, f32[4,8,80,128]{3,2,1,0:T(8,128)S(1)}, u32[]{:S(2)}) copy-start(f32[4,8,80,128]{3,2,1,0:T(8,128)S(1)} %collective-permute-done.20.refs_4_) | copy-start | bytes 3932164
  84.7 14.6 %collective-permute-start.26 = (f32[2,8,80,128]{3,2,1,0:T(8,128)S(1)}, f32[2,8,80,128]{3,2,1,0:T(8,128)S(1)}, u32[]{:S(2)}, u32[]{:S(2)}) collective-permute-start(f32[2,8,80,128]{3,2,1,0:T(8,128)S(1)} %slice.45), channel_id=1, source_target_pairs={{0,192},{64,0},{128,64},{192,128},{1,193},{65,1},{129,65},{193,129... | collective-permute-start | bytes 1966088 | tf_op jit(solution)/shard_map/ppermute | solution.py:24
  84.7 15.8 %collective-permute-start.25 = (f32[2,8,80,128]{3,2,1,0:T(8,128)S(1)}, f32[2,8,80,128]{3,2,1,0:T(8,128)S(1)}, u32[]{:S(2)}, u32[]{:S(2)}) collective-permute-start(f32[2,8,80,128]{3,2,1,0:T(8,128)S(1)} %slice.44), channel_id=1, source_target_pairs={{0,64},{64,128},{128,192},{192,0},{1,65},{65,129},{129,193},{193,1... | collective-permute-start | bytes 1966088 | tf_op jit(solution)/shard_map/ppermute | solution.py:24
  86.1 14.4 %collective-permute-start.28 = (f32[4,320,128]{2,1,0:T(8,128)S(1)}, f32[4,320,128]{2,1,0:T(8,128)S(1)}, u32[]{:S(2)}, u32[]{:S(2)}) collective-permute-start(f32[4,320,128]{2,1,0:T(8,128)S(1)} %slice.47), channel_id=1, source_target_pairs={{0,24},{8,0},{16,8},{24,16},{32,40},{40,48},{48,56},{56,32},{1,25}... | collective-permute-start | bytes 1966088 | tf_op jit(solution)/shard_map/ppermute | solution.py:34
  86.1 14.4 %collective-permute-start.27 = (f32[4,320,128]{2,1,0:T(8,128)S(1)}, f32[4,320,128]{2,1,0:T(8,128)S(1)}, u32[]{:S(2)}, u32[]{:S(2)}) collective-permute-start(f32[4,320,128]{2,1,0:T(8,128)S(1)} %slice.46), channel_id=1, source_target_pairs={{0,8},{8,16},{16,24},{24,0},{32,56},{40,32},{48,40},{56,48},{1,9},... | collective-permute-start | bytes 1966088 | tf_op jit(solution)/shard_map/ppermute | solution.py:34
  99.3 4.9 %copy-start.10 = (f32[2,8,80,128]{3,2,1,0:T(8,128)}, f32[2,8,80,128]{3,2,1,0:T(8,128)S(1)}, u32[]{:S(2)}) copy-start(f32[2,8,80,128]{3,2,1,0:T(8,128)S(1)} %collective-permute-done.26.refs_6_) | copy-start | bytes 1966084
  100.5 3.6 %copy-start.11 = (f32[2,8,80,128]{3,2,1,0:T(8,128)}, f32[2,8,80,128]{3,2,1,0:T(8,128)S(1)}, u32[]{:S(2)}) copy-start(f32[2,8,80,128]{3,2,1,0:T(8,128)S(1)} %collective-permute-done.25.refs_5_) | copy-start | bytes 1966084
  100.5 13.7 %copy-start.12 = (f32[4,320,128]{2,1,0:T(8,128)}, f32[4,320,128]{2,1,0:T(8,128)S(1)}, u32[]{:S(2)}) copy-start(f32[4,320,128]{2,1,0:T(8,128)S(1)} %collective-permute-done.28.refs_9_) | copy-start | bytes 1966084
  100.6 13.7 %copy-start.13 = (f32[4,320,128]{2,1,0:T(8,128)}, f32[4,320,128]{2,1,0:T(8,128)S(1)}, u32[]{:S(2)}) copy-start(f32[4,320,128]{2,1,0:T(8,128)S(1)} %collective-permute-done.27.refs_8_) | copy-start | bytes 1966084
  114.2 16.0 %collective-permute-start.30 = (f32[3,2,1024,128]{3,2,1,0:T(8,128)}, f32[3,2,1024,128]{3,2,1,0:T(8,128)S(1)}, u32[]{:S(2)}, u32[]{:S(2)}) collective-permute-start(f32[3,2,1024,128]{3,2,1,0:T(8,128)} %get-tuple-element.67), channel_id=1, source_target_pairs={{0,32},{32,0},{1,33},{33,1},{2,34},{34,2},{3,35},{35,3},{4,36},{36... | collective-permute-start | bytes 9437192 | tf_op jit(solution)/shard_map/ppermute | solution.py:331
  129.9 3.0 %collective-permute-start.29 = (f32[1,2,1024,128]{3,2,1,0:T(8,128)}, f32[1,2,1024,128]{3,2,1,0:T(8,128)S(1)}, u32[]{:S(2)}, u32[]{:S(2)}) collective-permute-start(f32[1,2,1024,128]{3,2,1,0:T(8,128)} %get-tuple-element.66), channel_id=1, source_target_pairs={{0,32},{32,0},{1,33},{33,1},{2,34},{34,2},{3,35},{35,3},{4,36},{36... | collective-permute-start | bytes 3145736 | tf_op jit(solution)/shard_map/ppermute | solution.py:331
  (1 other events, 1.1 us)
Sparse Core Ops, SparseCore 0:
  56.6 47.5 all-gather.2

commit v2 on v1

--- a/solution.py
+++ b/solution.py
@@ -241,7 +241,7 @@
         out_specs=(anywhere, anywhere),
         scratch_shapes=[
             pltpu.VMEM((count, NZ, NY * FLAT[0], NS), F32),
-            pltpu.VMEM((count, NY, NZ, FLAT[1], NS), F32),
+            pltpu.VMEM((count + 1, NY, NZ, FLAT[1], NS), F32),
             pltpu.VMEM((count, NZ, NY * FLAT[2], NS), F32),
             pltpu.VMEM((2 * SLOTS, 512), F32),
             pltpu.VMEM((4 * SLOTS, 512), BF16),

time: 141 us -> 141 us (level)
  no operation moved by 1% of the time
where the time goes in v2:
time: 141 us
  starting transfers between devices  63.9 us (45%)
  waiting for transfers between devices  41.4 us (29%)
  Pallas kernels  18.8 us (13%)
  between operations  13.8 us (10%)
  local copies, waits for them, and re-layouts  1.8 us (1%)
    ppermute x15, waiting for transfers between devices, shift(): return lax.ppermute(value, axis, [(i, (i + step) % n) for i in range(n)])  19.4 us
    ppermute x15, starting transfers between devices, shift(): return lax.ppermute(value, axis, [(i, (i + step) % n) for i in range(n)])  16.5 us
    pallas_call x2, Pallas kernels, product(): pl.pallas_call(functools.partial(product_kernel, steps, fresh), out_shape...  15.2 us
    ppermute x1, starting transfers between devices, body(): other = lax.ppermute(own, 'core', [(0, 1), (1, 0)])  13.3 us
    ppermute x8, starting transfers between devices, turn(): lax.ppermute(value, ('y', 'core') if axis == 'y' else ('core', axis), pairs)  11.4 us
    ppermute x2, starting transfers between devices, body(): received.append(lax.ppermute(given, 'core', [(0, 1), (1, 0)]))  10.6 us
    ppermute x8, waiting for transfers between devices, turn(): lax.ppermute(value, ('y', 'core') if axis == 'y' else ('core', axis), pairs)  8.88 us
    ppermute x1, starting transfers between devices, swap_halves(): return lax.ppermute(flat, ('core', 'z'), pairs)  6.28 us
  transfers between devices with their start and end apart: 32, of which 16 were waited for; matrix products, arithmetic and copies ran while one was open for 1% of the time, Pallas kernels for 5%

profile of v2, /device:TPU:1, one launch (start us, length us, event | category | flops | bytes accessed | tf_op | source)
XLA Modules:
  0.0 140.7 jit_solution(1517121660459360590)
XLA Ops:
  6.5 6.3 %collective-permute-start = (f32[200,128]{1,0:T(8,128)}, f32[200,128]{1,0:T(8,128)S(1)}, u32[]{:S(2)}, u32[]{:S(2)}) collective-permute-start(f32[200,128]{1,0:T(8,128)} %bitcast.42), channel_id=1, source_target_pairs={{0,0},{1,1},{2,32},{3,33},{4,4},{5,5},{6,36},{7,37},{32,2},{33,3},... | collective-permute-start | bytes 307208 | tf_op jit(solution)/shard_map/ppermute | solution.py:51
  12.8 2.5 %collective-permute-done = f32[200,128]{1,0:T(8,128)S(1)} collective-permute-done((f32[200,128]{1,0:T(8,128)}, f32[200,128]{1,0:T(8,128)S(1)}, u32[]{:S(2)}, u32[]{:S(2)}) %collective-permute-start) | collective-permute-done | bytes 102432 | tf_op jit(solution)/shard_map/ppermute | solution.py:51
  15.4 1.3 collective-permute-start.5
  16.7 2.4 %collective-permute-start.3 = (f32[160,128]{1,0:T(8,128)S(1)}, f32[160,128]{1,0:T(8,128)S(1)}, u32[]{:S(2)}, u32[]{:S(2)}) collective-permute-start(f32[160,128]{1,0:T(8,128)S(1)} %slice.48), channel_id=1, source_target_pairs={{0,2},{1,3},{2,4},{3,5},{4,6},{5,7},{6,0},{7,1},{8,10},{9,11},{10,... | collective-permute-start | bytes 245768 | tf_op jit(solution)/shard_map/ppermute | solution.py:24
  19.0 3.6 %collective-permute-start.2 = (f32[160,128]{1,0:T(8,128)S(1)}, f32[160,128]{1,0:T(8,128)S(1)}, u32[]{:S(2)}, u32[]{:S(2)}) collective-permute-start(f32[160,128]{1,0:T(8,128)S(1)} %slice.48), channel_id=1, source_target_pairs={{0,7},{1,0},{2,1},{3,2},{4,3},{5,4},{6,5},{7,6},{8,15},{9,8},{10,9... | collective-permute-start | bytes 245768 | tf_op jit(solution)/shard_map/ppermute | solution.py:24
  22.6 4.2 %collective-permute-done.3 = f32[160,128]{1,0:T(8,128)S(1)} collective-permute-done((f32[160,128]{1,0:T(8,128)S(1)}, f32[160,128]{1,0:T(8,128)S(1)}, u32[]{:S(2)}, u32[]{:S(2)}) %collective-permute-start.3) | collective-permute-done | bytes 81952 | tf_op jit(solution)/shard_map/ppermute | solution.py:24
  26.9 0.4 collective-permute-done.1
  27.2 2.6 %collective-permute-start.9 = (f32[80,128]{1,0:T(8,128)S(1)}, f32[80,128]{1,0:T(8,128)S(1)}, u32[]{:S(2)}, u32[]{:S(2)}) collective-permute-start(f32[80,128]{1,0:T(8,128)S(1)} %pad_maximum_fusion.5), channel_id=1, source_target_pairs={{0,128},{64,192},{128,0},{192,64},{1,129},{65,193},{129,1},{193,65... | collective-permute-start | bytes 122888 | tf_op jit(solution)/shard_map/ppermute | solution.py:39
  29.9 1.9 %collective-permute-start.8 = (f32[160,128]{1,0:T(8,128)S(1)}, f32[160,128]{1,0:T(8,128)S(1)}, u32[]{:S(2)}, u32[]{:S(2)}) collective-permute-start(f32[160,128]{1,0:T(8,128)S(1)} %collective-permute-done.3), channel_id=1, source_target_pairs={{0,2},{1,3},{2,4},{3,5},{4,6},{5,7},{6,0},{7,1},{8,10},{9,11},{10,... | collective-permute-start | bytes 245768 | tf_op jit(solution)/shard_map/ppermute | solution.py:24
  31.8 0.9 collective-permute-start.6
  32.7 1.8 %collective-permute-start.7 = (f32[160,128]{1,0:T(8,128)S(1)}, f32[160,128]{1,0:T(8,128)S(1)}, u32[]{:S(2)}, u32[]{:S(2)}) collective-permute-start(f32[160,128]{1,0:T(8,128)S(1)} %collective-permute-done.4), channel_id=1, source_target_pairs={{0,7},{1,0},{2,1},{3,2},{4,3},{5,4},{6,5},{7,6},{8,15},{9,8},{10,9... | collective-permute-start | bytes 245768 | tf_op jit(solution)/shard_map/ppermute | solution.py:24
  34.4 2.4 %collective-permute-done.7 = f32[160,128]{1,0:T(8,128)S(1)} collective-permute-done((f32[160,128]{1,0:T(8,128)S(1)}, f32[160,128]{1,0:T(8,128)S(1)}, u32[]{:S(2)}, u32[]{:S(2)}) %collective-permute-start.7) | collective-permute-done | bytes 81952 | tf_op jit(solution)/shard_map/ppermute | solution.py:24
  37.1 2.6 %collective-permute-start.10 = (f32[8,80,128]{2,1,0:T(8,128)S(1)}, f32[8,80,128]{2,1,0:T(8,128)S(1)}, u32[]{:S(2)}, u32[]{:S(2)}) collective-permute-start(f32[8,80,128]{2,1,0:T(8,128)S(1)} %get-tuple-element.71), channel_id=1, source_target_pairs={{0,8},{8,16},{16,24},{24,0},{32,56},{40,32},{48,40},{56,48},{1,9},... | collective-permute-start | bytes 983048 | tf_op jit(solution)/shard_map/ppermute | solution.py:34
  39.6 1.5 %collective-permute-start.12 = (f32[8,80,128]{2,1,0:T(8,128)S(1)}, f32[8,80,128]{2,1,0:T(8,128)S(1)}, u32[]{:S(2)}, u32[]{:S(2)}) collective-permute-start(f32[8,80,128]{2,1,0:T(8,128)S(1)} %get-tuple-element.70), channel_id=1, source_target_pairs={{0,64},{64,128},{128,192},{192,0},{1,65},{65,129},{129,193},{193,1... | collective-permute-start | bytes 983048 | tf_op jit(solution)/shard_map/ppermute | solution.py:24
  41.1 0.2 collective-permute-start.14
  41.3 3.2 %collective-permute-done.14 = f32[160,128]{1,0:T(8,128)S(1)} collective-permute-done((f32[160,128]{1,0:T(8,128)S(1)}, f32[160,128]{1,0:T(8,128)S(1)}, u32[]{:S(2)}, u32[]{:S(2)}) %collective-permute-start.14) | collective-permute-done | bytes 81952 | tf_op jit(solution)/shard_map/ppermute | solution.py:39
  44.5 2.2 %collective-permute-done.11 = f32[8,80,128]{2,1,0:T(8,128)S(1)} collective-permute-done((f32[8,80,128]{2,1,0:T(8,128)S(1)}, f32[8,80,128]{2,1,0:T(8,128)S(1)}, u32[]{:S(2)}, u32[]{:S(2)}) %collective-permute-start.11) | collective-permute-done | bytes 327712 | tf_op jit(solution)/shard_map/ppermute | solution.py:34
  46.8 1.7 %collective-permute-start.19 = (f32[2,160,128]{2,1,0:T(8,128)S(1)}, f32[2,160,128]{2,1,0:T(8,128)S(1)}, u32[]{:S(2)}, u32[]{:S(2)}) collective-permute-start(f32[2,160,128]{2,1,0:T(8,128)S(1)} %pad_maximum_fusion.3), channel_id=1, source_target_pairs={{0,16},{8,24},{16,0},{24,8},{1,17},{9,25},{17,1},{25,9},{2,18},{10... | collective-permute-start | bytes 491528 | tf_op jit(solution)/shard_map/ppermute | solution.py:39
  48.7 1.5 %collective-permute-start.17 = (f32[4,80,128]{2,1,0:T(8,128)S(1)}, f32[4,80,128]{2,1,0:T(8,128)S(1)}, u32[]{:S(2)}, u32[]{:S(2)}) collective-permute-start(f32[4,80,128]{2,1,0:T(8,128)S(1)} %slice.42), channel_id=1, source_target_pairs={{0,64},{64,128},{128,192},{192,0},{1,65},{65,129},{129,193},{193,1... | collective-permute-start | bytes 491528 | tf_op jit(solution)/shard_map/ppermute | solution.py:24
  50.1 1.5 %collective-permute-start.16 = (f32[4,80,128]{2,1,0:T(8,128)S(1)}, f32[4,80,128]{2,1,0:T(8,128)S(1)}, u32[]{:S(2)}, u32[]{:S(2)}) collective-permute-start(f32[4,80,128]{2,1,0:T(8,128)S(1)} %slice.41), channel_id=1, source_target_pairs={{0,24},{8,0},{16,8},{24,16},{32,40},{40,48},{48,56},{56,32},{1,25}... | collective-permute-start | bytes 491528 | tf_op jit(solution)/shard_map/ppermute | solution.py:34
  51.6 1.2 collective-permute-start.15
  52.8 1.5 %collective-permute-done.19 = f32[2,160,128]{2,1,0:T(8,128)S(1)} collective-permute-done((f32[2,160,128]{2,1,0:T(8,128)S(1)}, f32[2,160,128]{2,1,0:T(8,128)S(1)}, u32[]{:S(2)}, u32[]{:S(2)}) %collective-permute-start.19) | collective-permute-done | bytes 163872 | tf_op jit(solution)/shard_map/ppermute | solution.py:39
  54.2 0.7 pad_maximum_fusion.2
  55.0 1.4 collective-permute-done.17
  56.6 2.7 %collective-permute-start.22 = (f32[8,320,128]{2,1,0:T(8,128)S(1)}, f32[8,320,128]{2,1,0:T(8,128)S(1)}, u32[]{:S(2)}, u32[]{:S(2)}) collective-permute-start(f32[8,320,128]{2,1,0:T(8,128)S(1)} %pad_maximum_fusion.1.refs_8_), channel_id=1, source_target_pairs={{0,8},{8,16},{16,24},{24,0},{32,56},{40,32},{48,40},{56,48},{1,9},... | collective-permute-start | bytes 3932168 | tf_op jit(solution)/shard_map/ppermute | solution.py:34
  59.4 0.1 pad_maximum_fusion.refs_3_
  59.5 0.9 collective-permute-start.21
  60.5 0.6 collective-permute-start.20
  61.1 0.9 shard_map.64.refs_0_
  62.0 13.3 %collective-permute-start.24 = (f32[128,512]{1,0:T(8,128)S(1)}, f32[128,512]{1,0:T(8,128)S(1)}, u32[]{:S(2)}, u32[]{:S(2)}) collective-permute-start(f32[128,512]{1,0:T(8,128)S(1)} %shard_map.64.refs_0_), channel_id=1, source_target_pairs={{0,32},{32,0},{1,33},{33,1},{2,34},{34,2},{3,35},{35,3},{4,36},{36... | collective-permute-start | bytes 786440 | tf_op jit(solution)/shard_map/ppermute | solution.py:319
  75.2 1.2 collective-permute-done.24.refs_1_
  76.4 4.9 %collective-permute-done.23.refs_10_ = f32[8,320,128]{2,1,0:T(8,128)S(1)} collective-permute-done((f32[8,320,128]{2,1,0:T(8,128)S(1)}, f32[8,320,128]{2,1,0:T(8,128)S(1)}, u32[]{:S(2)}, u32[]{:S(2)}) %collective-permute-start.23) | collective-permute-done | bytes 1310752 | tf_op jit(solution)/shard_map/ppermute | solution.py:34
  81.3 1.7 %collective-permute-done.22.refs_9_ = f32[8,320,128]{2,1,0:T(8,128)S(1)} collective-permute-done((f32[8,320,128]{2,1,0:T(8,128)S(1)}, f32[8,320,128]{2,1,0:T(8,128)S(1)}, u32[]{:S(2)}, u32[]{:S(2)}) %collective-permute-start.22) | collective-permute-done | bytes 1310752 | tf_op jit(solution)/shard_map/ppermute | solution.py:34
  83.3 0.9 copy-done.7
  84.2 0.5 copy-done.8
  84.7 1.5 %collective-permute-start.25 = (f32[2,8,80,128]{3,2,1,0:T(8,128)S(1)}, f32[2,8,80,128]{3,2,1,0:T(8,128)S(1)}, u32[]{:S(2)}, u32[]{:S(2)}) collective-permute-start(f32[2,8,80,128]{3,2,1,0:T(8,128)S(1)} %slice.44), channel_id=1, source_target_pairs={{0,64},{64,128},{128,192},{192,0},{1,65},{65,129},{129,193},{193,1... | collective-permute-start | bytes 1966088 | tf_op jit(solution)/shard_map/ppermute | solution.py:24
  86.1 3.4 %collective-permute-start.27 = (f32[4,320,128]{2,1,0:T(8,128)S(1)}, f32[4,320,128]{2,1,0:T(8,128)S(1)}, u32[]{:S(2)}, u32[]{:S(2)}) collective-permute-start(f32[4,320,128]{2,1,0:T(8,128)S(1)} %slice.46), channel_id=1, source_target_pairs={{0,8},{8,16},{16,24},{24,0},{32,56},{40,32},{48,40},{56,48},{1,9},... | collective-permute-start | bytes 1966088 | tf_op jit(solution)/shard_map/ppermute | solution.py:34
  89.6 9.7 %collective-permute-done.26.refs_6_ = f32[2,8,80,128]{3,2,1,0:T(8,128)S(1)} collective-permute-done((f32[2,8,80,128]{3,2,1,0:T(8,128)S(1)}, f32[2,8,80,128]{3,2,1,0:T(8,128)S(1)}, u32[]{:S(2)}, u32[]{:S(2)}) %collective-permute-start.26) | collective-permute-done | bytes 655392 | tf_op jit(solution)/shard_map/ppermute | solution.py:24
  99.3 1.3 collective-permute-done.25.refs_5_
  100.6 3.6 %all-gather.3.cloned.1.call-done = f32[32,160,128]{2,1,0:T(8,128)} async-done(((f32[4,160,128]{2,1,0:T(8,128)}), f32[32,160,128]{2,1,0:T(8,128)}) %all-gather.3.cloned.1.call-update) | async-done | bytes 2621456 | tf_op jit(solution)/shard_map/all_gather | solution.py:316
  104.2 10.0 %shard_map.65 = (f32[128,128,128]{2,1,0:T(8,128)}, f32[3,2,1024,128]{3,2,1,0:T(8,128)}) custom-call(f32[128,512]{1,0:T(8,128)} %copy-done, f32[128,512]{1,0:T(8,128)} %copy-done.16, f32[8,4,160,128]{3,2,1,0:T(8,128)} %bitcast.36, f32[4,8,80,128]{3,2,1,0:T(8,128)} %copy-done.6, f32[4,8,80,128]{3,2,1,0:T(8,128)} %copy-done.8, f32[2,8,80,128]{3,2,1,0:T(8,128)} %copy-done.11, ...), custom_call_target="tpu_custom_call" | custom-call | flops 4831838208 | bytes 25165824 | tf_op jit(solution)/shard_map/pallas_call | solution.py:234
  114.2 10.5 %collective-permute-start.30 = (f32[3,2,1024,128]{3,2,1,0:T(8,128)}, f32[3,2,1024,128]{3,2,1,0:T(8,128)S(1)}, u32[]{:S(2)}, u32[]{:S(2)}) collective-permute-start(f32[3,2,1024,128]{3,2,1,0:T(8,128)} %get-tuple-element.67), channel_id=1, source_target_pairs={{0,32},{32,0},{1,33},{33,1},{2,34},{34,2},{3,35},{35,3},{4,36},{36... | collective-permute-start | bytes 9437192 | tf_op jit(solution)/shard_map/ppermute | solution.py:331
  124.7 5.1 %shard_map.66 = (f32[128,128,128]{2,1,0:T(8,128)}, f32[1,2,1024,128]{3,2,1,0:T(8,128)}) custom-call(f32[128,512]{1,0:T(8,128)} %copy-done, f32[128,512]{1,0:T(8,128)} %copy-done.16, f32[8,4,160,128]{3,2,1,0:T(8,128)} %bitcast.37, f32[4,8,80,128]{3,2,1,0:T(8,128)} %copy-done.6, f32[4,8,80,128]{3,2,1,0:T(8,128)} %copy-done.8, ...), custom_call_target="tpu_custom_call", output_to_operand_aliasing={{0}: (10, {})} | custom-call | flops 1610612736 | bytes 8388608 | tf_op jit(solution)/shard_map/pallas_call | solution.py:234
  129.9 0.1 collective-permute-start.29
  130.0 0.2 collective-permute-done.30.blocks_ref
  130.2 1.7 %shard_map.67._ = f32[128,128,128]{2,1,0:T(8,128)} custom-call(f32[3,2,1024,128]{3,2,1,0:T(8,128)S(1)} %collective-permute-done.30.blocks_ref, f32[128,128,128]{2,1,0:T(8,128)} %get-tuple-element.68._), custom_call_target="tpu_custom_call", output_to_operand_aliasing={{}: (1, {})} | custom-call | bytes 6291456 | tf_op jit(solution)/shard_map/pallas_call | solution.py:278
  131.9 0.9 collective-permute-done.29.blocks_ref
  132.8 1.0 shard_map.68
  (82 shorter events, 0.8 us)
Async XLA Ops:
  6.5 97.6 %all-gather.3.cloned.1.call-start = ((), (), s32[]{:S(2)}) async-start(), calls=%async_computation | async-start | bytes 2949120 | tf_op jit(solution)/shard_map/all_gather | solution.py:316
  6.5 8.8 %collective-permute-start = (f32[200,128]{1,0:T(8,128)}, f32[200,128]{1,0:T(8,128)S(1)}, u32[]{:S(2)}, u32[]{:S(2)}) collective-permute-start(f32[200,128]{1,0:T(8,128)} %bitcast.42), channel_id=1, source_target_pairs={{0,0},{1,1},{2,32},{3,33},{4,4},{5,5},{6,36},{7,37},{32,2},{33,3},... | collective-permute-start | bytes 307208 | tf_op jit(solution)/shard_map/ppermute | solution.py:51
  15.4 7.2 %collective-permute-start.5 = (f32[40,128]{1,0:T(8,128)S(1)}, f32[40,128]{1,0:T(8,128)S(1)}, u32[]{:S(2)}, u32[]{:S(2)}) collective-permute-start(f32[40,128]{1,0:T(8,128)S(1)} %slice.49), channel_id=1, source_target_pairs={{0,64},{64,0},{128,192},{192,128},{1,65},{65,1},{129,193},{193,129... | collective-permute-start | bytes 61448 | tf_op jit(solution)/shard_map/ppermute | solution.py:39
  16.7 5.9 %collective-permute-start.4 = (f32[160,128]{1,0:T(8,128)S(1)}, f32[160,128]{1,0:T(8,128)S(1)}, u32[]{:S(2)}, u32[]{:S(2)}) collective-permute-start(f32[160,128]{1,0:T(8,128)S(1)} %slice.48), channel_id=1, source_target_pairs={{0,6},{1,7},{2,0},{3,1},{4,2},{5,3},{6,4},{7,5},{8,14},{9,15},{10,... | collective-permute-start | bytes 245768 | tf_op jit(solution)/shard_map/ppermute | solution.py:24
  16.7 10.2 %collective-permute-start.3 = (f32[160,128]{1,0:T(8,128)S(1)}, f32[160,128]{1,0:T(8,128)S(1)}, u32[]{:S(2)}, u32[]{:S(2)}) collective-permute-start(f32[160,128]{1,0:T(8,128)S(1)} %slice.48), channel_id=1, source_target_pairs={{0,2},{1,3},{2,4},{3,5},{4,6},{5,7},{6,0},{7,1},{8,10},{9,11},{10,... | collective-permute-start | bytes 245768 | tf_op jit(solution)/shard_map/ppermute | solution.py:24
  19.0 7.8 %collective-permute-start.2 = (f32[160,128]{1,0:T(8,128)S(1)}, f32[160,128]{1,0:T(8,128)S(1)}, u32[]{:S(2)}, u32[]{:S(2)}) collective-permute-start(f32[160,128]{1,0:T(8,128)S(1)} %slice.48), channel_id=1, source_target_pairs={{0,7},{1,0},{2,1},{3,2},{4,3},{5,4},{6,5},{7,6},{8,15},{9,8},{10,9... | collective-permute-start | bytes 245768 | tf_op jit(solution)/shard_map/ppermute | solution.py:24
  22.6 4.6 %collective-permute-start.1 = (f32[160,128]{1,0:T(8,128)S(1)}, f32[160,128]{1,0:T(8,128)S(1)}, u32[]{:S(2)}, u32[]{:S(2)}) collective-permute-start(f32[160,128]{1,0:T(8,128)S(1)} %slice.48), channel_id=1, source_target_pairs={{0,1},{1,2},{2,3},{3,4},{4,5},{5,6},{6,7},{7,0},{8,9},{9,10},{10,1... | collective-permute-start | bytes 245768 | tf_op jit(solution)/shard_map/ppermute | solution.py:24
  27.2 7.2 %collective-permute-start.9 = (f32[80,128]{1,0:T(8,128)S(1)}, f32[80,128]{1,0:T(8,128)S(1)}, u32[]{:S(2)}, u32[]{:S(2)}) collective-permute-start(f32[80,128]{1,0:T(8,128)S(1)} %pad_maximum_fusion.5), channel_id=1, source_target_pairs={{0,128},{64,192},{128,0},{192,64},{1,129},{65,193},{129,1},{193,65... | collective-permute-start | bytes 122888 | tf_op jit(solution)/shard_map/ppermute | solution.py:39
  29.9 7.0 %collective-permute-start.8 = (f32[160,128]{1,0:T(8,128)S(1)}, f32[160,128]{1,0:T(8,128)S(1)}, u32[]{:S(2)}, u32[]{:S(2)}) collective-permute-start(f32[160,128]{1,0:T(8,128)S(1)} %collective-permute-done.3), channel_id=1, source_target_pairs={{0,2},{1,3},{2,4},{3,5},{4,6},{5,7},{6,0},{7,1},{8,10},{9,11},{10,... | collective-permute-start | bytes 245768 | tf_op jit(solution)/shard_map/ppermute | solution.py:24
  31.8 5.1 %collective-permute-start.6 = (f32[160,128]{1,0:T(8,128)S(1)}, f32[160,128]{1,0:T(8,128)S(1)}, u32[]{:S(2)}, u32[]{:S(2)}) collective-permute-start(f32[160,128]{1,0:T(8,128)S(1)} %collective-permute-done.3), channel_id=1, source_target_pairs={{0,1},{1,2},{2,3},{3,4},{4,5},{5,6},{6,7},{7,0},{8,9},{9,10},{10,1... | collective-permute-start | bytes 245768 | tf_op jit(solution)/shard_map/ppermute | solution.py:24
  32.7 4.2 %collective-permute-start.7 = (f32[160,128]{1,0:T(8,128)S(1)}, f32[160,128]{1,0:T(8,128)S(1)}, u32[]{:S(2)}, u32[]{:S(2)}) collective-permute-start(f32[160,128]{1,0:T(8,128)S(1)} %collective-permute-done.4), channel_id=1, source_target_pairs={{0,7},{1,0},{2,1},{3,2},{4,3},{5,4},{6,5},{7,6},{8,15},{9,8},{10,9... | collective-permute-start | bytes 245768 | tf_op jit(solution)/shard_map/ppermute | solution.py:24
  37.1 7.5 %collective-permute-start.10 = (f32[8,80,128]{2,1,0:T(8,128)S(1)}, f32[8,80,128]{2,1,0:T(8,128)S(1)}, u32[]{:S(2)}, u32[]{:S(2)}) collective-permute-start(f32[8,80,128]{2,1,0:T(8,128)S(1)} %get-tuple-element.71), channel_id=1, source_target_pairs={{0,8},{8,16},{16,24},{24,0},{32,56},{40,32},{48,40},{56,48},{1,9},... | collective-permute-start | bytes 983048 | tf_op jit(solution)/shard_map/ppermute | solution.py:34
  39.6 7.1 %collective-permute-start.11 = (f32[8,80,128]{2,1,0:T(8,128)S(1)}, f32[8,80,128]{2,1,0:T(8,128)S(1)}, u32[]{:S(2)}, u32[]{:S(2)}) collective-permute-start(f32[8,80,128]{2,1,0:T(8,128)S(1)} %get-tuple-element.71), channel_id=1, source_target_pairs={{0,24},{8,0},{16,8},{24,16},{32,40},{40,48},{48,56},{56,32},{1,25}... | collective-permute-start | bytes 983048 | tf_op jit(solution)/shard_map/ppermute | solution.py:34
  39.6 7.1 %collective-permute-start.13 = (f32[8,80,128]{2,1,0:T(8,128)S(1)}, f32[8,80,128]{2,1,0:T(8,128)S(1)}, u32[]{:S(2)}, u32[]{:S(2)}) collective-permute-start(f32[8,80,128]{2,1,0:T(8,128)S(1)} %get-tuple-element.70), channel_id=1, source_target_pairs={{0,192},{64,0},{128,64},{192,128},{1,193},{65,1},{129,65},{193,129... | collective-permute-start | bytes 983048 | tf_op jit(solution)/shard_map/ppermute | solution.py:24
  39.6 7.1 %collective-permute-start.12 = (f32[8,80,128]{2,1,0:T(8,128)S(1)}, f32[8,80,128]{2,1,0:T(8,128)S(1)}, u32[]{:S(2)}, u32[]{:S(2)}) collective-permute-start(f32[8,80,128]{2,1,0:T(8,128)S(1)} %get-tuple-element.70), channel_id=1, source_target_pairs={{0,64},{64,128},{128,192},{192,0},{1,65},{65,129},{129,193},{193,1... | collective-permute-start | bytes 983048 | tf_op jit(solution)/shard_map/ppermute | solution.py:24
  41.1 3.4 %collective-permute-start.14 = (f32[160,128]{1,0:T(8,128)S(1)}, f32[160,128]{1,0:T(8,128)S(1)}, u32[]{:S(2)}, u32[]{:S(2)}) collective-permute-start(f32[160,128]{1,0:T(8,128)S(1)} %pad_maximum_fusion.4), channel_id=1, source_target_pairs={{0,8},{8,0},{16,24},{24,16},{1,9},{9,1},{17,25},{25,17},{2,10},{10... | collective-permute-start | bytes 245768 | tf_op jit(solution)/shard_map/ppermute | solution.py:39
  46.8 7.5 %collective-permute-start.19 = (f32[2,160,128]{2,1,0:T(8,128)S(1)}, f32[2,160,128]{2,1,0:T(8,128)S(1)}, u32[]{:S(2)}, u32[]{:S(2)}) collective-permute-start(f32[2,160,128]{2,1,0:T(8,128)S(1)} %pad_maximum_fusion.3), channel_id=1, source_target_pairs={{0,16},{8,24},{16,0},{24,8},{1,17},{9,25},{17,1},{25,9},{2,18},{10... | collective-permute-start | bytes 491528 | tf_op jit(solution)/shard_map/ppermute | solution.py:39
  48.6 6.4 %collective-permute-start.18 = (f32[4,80,128]{2,1,0:T(8,128)S(1)}, f32[4,80,128]{2,1,0:T(8,128)S(1)}, u32[]{:S(2)}, u32[]{:S(2)}) collective-permute-start(f32[4,80,128]{2,1,0:T(8,128)S(1)} %slice.43), channel_id=1, source_target_pairs={{0,192},{64,0},{128,64},{192,128},{1,193},{65,1},{129,65},{193,129... | collective-permute-start | bytes 491528 | tf_op jit(solution)/shard_map/ppermute | solution.py:24
  48.7 7.8 %collective-permute-start.17 = (f32[4,80,128]{2,1,0:T(8,128)S(1)}, f32[4,80,128]{2,1,0:T(8,128)S(1)}, u32[]{:S(2)}, u32[]{:S(2)}) collective-permute-start(f32[4,80,128]{2,1,0:T(8,128)S(1)} %slice.42), channel_id=1, source_target_pairs={{0,64},{64,128},{128,192},{192,0},{1,65},{65,129},{129,193},{193,1... | collective-permute-start | bytes 491528 | tf_op jit(solution)/shard_map/ppermute | solution.py:24
  50.1 6.3 %collective-permute-start.16 = (f32[4,80,128]{2,1,0:T(8,128)S(1)}, f32[4,80,128]{2,1,0:T(8,128)S(1)}, u32[]{:S(2)}, u32[]{:S(2)}) collective-permute-start(f32[4,80,128]{2,1,0:T(8,128)S(1)} %slice.41), channel_id=1, source_target_pairs={{0,24},{8,0},{16,8},{24,16},{32,40},{40,48},{48,56},{56,32},{1,25}... | collective-permute-start | bytes 491528 | tf_op jit(solution)/shard_map/ppermute | solution.py:34
  51.6 4.8 %collective-permute-start.15 = (f32[4,80,128]{2,1,0:T(8,128)S(1)}, f32[4,80,128]{2,1,0:T(8,128)S(1)}, u32[]{:S(2)}, u32[]{:S(2)}) collective-permute-start(f32[4,80,128]{2,1,0:T(8,128)S(1)} %slice.40), channel_id=1, source_target_pairs={{0,8},{8,16},{16,24},{24,0},{32,56},{40,32},{48,40},{56,48},{1,9},... | collective-permute-start | bytes 491528 | tf_op jit(solution)/shard_map/ppermute | solution.py:34
  56.5 3.0 %copy-start.9 = (f32[8,320,128]{2,1,0:T(8,128)}, f32[8,320,128]{2,1,0:T(8,128)S(1)}, u32[]{:S(2)}) copy-start(f32[8,320,128]{2,1,0:T(8,128)S(1)} %pad_maximum_fusion.1.refs_8_) | copy-start | bytes 3932164
  56.5 24.8 %collective-permute-start.23 = (f32[8,320,128]{2,1,0:T(8,128)S(1)}, f32[8,320,128]{2,1,0:T(8,128)S(1)}, u32[]{:S(2)}, u32[]{:S(2)}) collective-permute-start(f32[8,320,128]{2,1,0:T(8,128)S(1)} %pad_maximum_fusion.1.refs_8_), channel_id=1, source_target_pairs={{0,24},{8,0},{16,8},{24,16},{32,40},{40,48},{48,56},{56,32},{1,25}... | collective-permute-start | bytes 3932168 | tf_op jit(solution)/shard_map/ppermute | solution.py:34
  56.6 26.4 %collective-permute-start.22 = (f32[8,320,128]{2,1,0:T(8,128)S(1)}, f32[8,320,128]{2,1,0:T(8,128)S(1)}, u32[]{:S(2)}, u32[]{:S(2)}) collective-permute-start(f32[8,320,128]{2,1,0:T(8,128)S(1)} %pad_maximum_fusion.1.refs_8_), channel_id=1, source_target_pairs={{0,8},{8,16},{16,24},{24,0},{32,56},{40,32},{48,40},{56,48},{1,9},... | collective-permute-start | bytes 3932168 | tf_op jit(solution)/shard_map/ppermute | solution.py:34
  59.3 1.7 %copy-start.1 = (s32[2048,8]{0,1:T(8,128)S(1)}, s32[2048,8]{0,1:T(8,128)}, u32[]{:S(2)}) copy-start(s32[2048,8]{0,1:T(8,128)} %param.7) | copy-start | bytes 196612
  59.3 1.7 %copy-start.2 = (s32[2048,8]{0,1:T(8,128)S(1)}, s32[2048,8]{0,1:T(8,128)}, u32[]{:S(2)}) copy-start(s32[2048,8]{0,1:T(8,128)} %param.8) | copy-start | bytes 196612
  59.3 1.7 %copy-start.3 = (s32[2048,8]{0,1:T(8,128)S(1)}, s32[2048,8]{0,1:T(8,128)}, u32[]{:S(2)}) copy-start(s32[2048,8]{0,1:T(8,128)} %param.9) | copy-start | bytes 196612
  59.4 1.7 %copy-start.4 = (s32[2048]{0:T(1024)S(1)}, s32[2048]{0:T(1024)}, u32[]{:S(2)}) copy-start(s32[2048]{0:T(1024)} %param.11) | copy-start | bytes 24580
  59.4 1.7 %copy-start.5 = (f32[64]{0:T(128)S(1)}, f32[64]{0:T(128)}, u32[]{:S(2)}) copy-start(f32[64]{0:T(128)} %param.10) | copy-start | bytes 772
  59.5 23.7 %copy-start.6 = (f32[4,8,80,128]{3,2,1,0:T(8,128)}, f32[4,8,80,128]{3,2,1,0:T(8,128)S(1)}, u32[]{:S(2)}) copy-start(f32[4,8,80,128]{3,2,1,0:T(8,128)S(1)} %pad_maximum_fusion.refs_3_) | copy-start | bytes 3932164
  59.5 23.6 %collective-permute-start.21 = (f32[4,8,80,128]{3,2,1,0:T(8,128)S(1)}, f32[4,8,80,128]{3,2,1,0:T(8,128)S(1)}, u32[]{:S(2)}, u32[]{:S(2)}) collective-permute-start(f32[4,8,80,128]{3,2,1,0:T(8,128)S(1)} %pad_maximum_fusion.refs_3_), channel_id=1, source_target_pairs={{0,192},{64,0},{128,64},{192,128},{1,193},{65,1},{129,65},{193,129... | collective-permute-start | bytes 3932168 | tf_op jit(solution)/shard_map/ppermute | solution.py:24
  60.5 22.6 %collective-permute-start.20 = (f32[4,8,80,128]{3,2,1,0:T(8,128)S(1)}, f32[4,8,80,128]{3,2,1,0:T(8,128)S(1)}, u32[]{:S(2)}, u32[]{:S(2)}) collective-permute-start(f32[4,8,80,128]{3,2,1,0:T(8,128)S(1)} %pad_maximum_fusion.refs_3_), channel_id=1, source_target_pairs={{0,64},{64,128},{128,192},{192,0},{1,65},{65,129},{129,193},{193,1... | collective-permute-start | bytes 3932168 | tf_op jit(solution)/shard_map/ppermute | solution.py:24
  62.0 21.2 %copy-start = (f32[128,512]{1,0:T(8,128)}, f32[128,512]{1,0:T(8,128)S(1)}, u32[]{:S(2)}) copy-start(f32[128,512]{1,0:T(8,128)S(1)} %shard_map.64.refs_0_) | copy-start | bytes 786436
  62.0 14.4 %collective-permute-start.24 = (f32[128,512]{1,0:T(8,128)S(1)}, f32[128,512]{1,0:T(8,128)S(1)}, u32[]{:S(2)}, u32[]{:S(2)}) collective-permute-start(f32[128,512]{1,0:T(8,128)S(1)} %shard_map.64.refs_0_), channel_id=1, source_target_pairs={{0,32},{32,0},{1,33},{33,1},{2,34},{34,2},{3,35},{35,3},{4,36},{36... | collective-permute-start | bytes 786440 | tf_op jit(solution)/shard_map/ppermute | solution.py:319
  76.4 27.8 %copy-start.16 = (f32[128,512]{1,0:T(8,128)}, f32[128,512]{1,0:T(8,128)S(1)}, u32[]{:S(2)}) copy-start(f32[128,512]{1,0:T(8,128)S(1)} %collective-permute-done.24.refs_1_) | copy-start | bytes 786436
  81.3 1.9 %copy-start.14 = (f32[8,320,128]{2,1,0:T(8,128)}, f32[8,320,128]{2,1,0:T(8,128)S(1)}, u32[]{:S(2)}) copy-start(f32[8,320,128]{2,1,0:T(8,128)S(1)} %collective-permute-done.23.refs_10_) | copy-start | bytes 3932164
  83.1 17.5 %copy-start.15 = (f32[8,320,128]{2,1,0:T(8,128)}, f32[8,320,128]{2,1,0:T(8,128)S(1)}, u32[]{:S(2)}) copy-start(f32[8,320,128]{2,1,0:T(8,128)S(1)} %collective-permute-done.22.refs_9_) | copy-start | bytes 3932164
  83.1 1.6 %copy-start.8 = (f32[4,8,80,128]{3,2,1,0:T(8,128)}, f32[4,8,80,128]{3,2,1,0:T(8,128)S(1)}, u32[]{:S(2)}) copy-start(f32[4,8,80,128]{3,2,1,0:T(8,128)S(1)} %collective-permute-done.20.refs_4_) | copy-start | bytes 3932164
  84.7 14.6 %collective-permute-start.26 = (f32[2,8,80,128]{3,2,1,0:T(8,128)S(1)}, f32[2,8,80,128]{3,2,1,0:T(8,128)S(1)}, u32[]{:S(2)}, u32[]{:S(2)}) collective-permute-start(f32[2,8,80,128]{3,2,1,0:T(8,128)S(1)} %slice.45), channel_id=1, source_target_pairs={{0,192},{64,0},{128,64},{192,128},{1,193},{65,1},{129,65},{193,129... | collective-permute-start | bytes 1966088 | tf_op jit(solution)/shard_map/ppermute | solution.py:24
  84.7 15.8 %collective-permute-start.25 = (f32[2,8,80,128]{3,2,1,0:T(8,128)S(1)}, f32[2,8,80,128]{3,2,1,0:T(8,128)S(1)}, u32[]{:S(2)}, u32[]{:S(2)}) collective-permute-start(f32[2,8,80,128]{3,2,1,0:T(8,128)S(1)} %slice.44), channel_id=1, source_target_pairs={{0,64},{64,128},{128,192},{192,0},{1,65},{65,129},{129,193},{193,1... | collective-permute-start | bytes 1966088 | tf_op jit(solution)/shard_map/ppermute | solution.py:24
  86.1 14.4 %collective-permute-start.28 = (f32[4,320,128]{2,1,0:T(8,128)S(1)}, f32[4,320,128]{2,1,0:T(8,128)S(1)}, u32[]{:S(2)}, u32[]{:S(2)}) collective-permute-start(f32[4,320,128]{2,1,0:T(8,128)S(1)} %slice.47), channel_id=1, source_target_pairs={{0,24},{8,0},{16,8},{24,16},{32,40},{40,48},{48,56},{56,32},{1,25}... | collective-permute-start | bytes 1966088 | tf_op jit(solution)/shard_map/ppermute | solution.py:34
  86.1 14.4 %collective-permute-start.27 = (f32[4,320,128]{2,1,0:T(8,128)S(1)}, f32[4,320,128]{2,1,0:T(8,128)S(1)}, u32[]{:S(2)}, u32[]{:S(2)}) collective-permute-start(f32[4,320,128]{2,1,0:T(8,128)S(1)} %slice.46), channel_id=1, source_target_pairs={{0,8},{8,16},{16,24},{24,0},{32,56},{40,32},{48,40},{56,48},{1,9},... | collective-permute-start | bytes 1966088 | tf_op jit(solution)/shard_map/ppermute | solution.py:34
  99.3 4.9 %copy-start.10 = (f32[2,8,80,128]{3,2,1,0:T(8,128)}, f32[2,8,80,128]{3,2,1,0:T(8,128)S(1)}, u32[]{:S(2)}) copy-start(f32[2,8,80,128]{3,2,1,0:T(8,128)S(1)} %collective-permute-done.26.refs_6_) | copy-start | bytes 1966084
  100.5 3.6 %copy-start.11 = (f32[2,8,80,128]{3,2,1,0:T(8,128)}, f32[2,8,80,128]{3,2,1,0:T(8,128)S(1)}, u32[]{:S(2)}) copy-start(f32[2,8,80,128]{3,2,1,0:T(8,128)S(1)} %collective-permute-done.25.refs_5_) | copy-start | bytes 1966084
  100.5 13.7 %copy-start.12 = (f32[4,320,128]{2,1,0:T(8,128)}, f32[4,320,128]{2,1,0:T(8,128)S(1)}, u32[]{:S(2)}) copy-start(f32[4,320,128]{2,1,0:T(8,128)S(1)} %collective-permute-done.28.refs_9_) | copy-start | bytes 1966084
  100.6 13.7 %copy-start.13 = (f32[4,320,128]{2,1,0:T(8,128)}, f32[4,320,128]{2,1,0:T(8,128)S(1)}, u32[]{:S(2)}) copy-start(f32[4,320,128]{2,1,0:T(8,128)S(1)} %collective-permute-done.27.refs_8_) | copy-start | bytes 1966084
  114.2 16.0 %collective-permute-start.30 = (f32[3,2,1024,128]{3,2,1,0:T(8,128)}, f32[3,2,1024,128]{3,2,1,0:T(8,128)S(1)}, u32[]{:S(2)}, u32[]{:S(2)}) collective-permute-start(f32[3,2,1024,128]{3,2,1,0:T(8,128)} %get-tuple-element.67), channel_id=1, source_target_pairs={{0,32},{32,0},{1,33},{33,1},{2,34},{34,2},{3,35},{35,3},{4,36},{36... | collective-permute-start | bytes 9437192 | tf_op jit(solution)/shard_map/ppermute | solution.py:331
  129.9 3.0 %collective-permute-start.29 = (f32[1,2,1024,128]{3,2,1,0:T(8,128)}, f32[1,2,1024,128]{3,2,1,0:T(8,128)S(1)}, u32[]{:S(2)}, u32[]{:S(2)}) collective-permute-start(f32[1,2,1024,128]{3,2,1,0:T(8,128)} %get-tuple-element.66), channel_id=1, source_target_pairs={{0,32},{32,0},{1,33},{33,1},{2,34},{34,2},{3,35},{35,3},{4,36},{36... | collective-permute-start | bytes 3145736 | tf_op jit(solution)/shard_map/ppermute | solution.py:331
  (1 other events, 1.1 us)
Sparse Core Ops, SparseCore 0:
  56.6 47.5 all-gather.2

commit v3 on v2

--- a/solution.py
+++ b/solution.py
@@ -177,10 +177,11 @@
         copy.wait()
     mix = mix_all[...]
     mix_high = mix.astype(BF16)
-    left_all[: 2 * SLOTS, :] = mix_high
-    left_all[2 * SLOTS :, :] = (mix - mix_high.astype(F32)).astype(BF16)
+    mix_low = (mix - mix_high.astype(F32)).astype(BF16)
+    tail = jnp.zeros((2 * SLOTS, 1280 - 3 * K), BF16)
+    left_all[...] = jnp.concatenate([mix_high[:, :K], mix_low[:, :K], mix_high[:, :K], tail], axis=1)
     a_run, b_run, c_run = NY * CUTS[0], CUTS[1], NY * CUTS[2]
-    pad = jnp.zeros((512 - K, NS), F32)
+    pad = jnp.zeros((1280 - 3 * K, 2 * NS), BF16)
 
     for n in range(count):
         for copy in arrive(n):
@@ -201,15 +202,14 @@
                             b_all[n, y, s, pl.ds(r, b_run, stride=ROWS), :] for s in spots for y in range(NY)
                         ]
                         pieces += [c_all[n, s, pl.ds(r, c_run, stride=ROWS), :] for s in spots]
-                        value = jnp.concatenate(pieces + [pad], axis=0)
+                        value = jnp.concatenate(pieces, axis=0)
                         high = value.astype(BF16)
                         highs.append(high)
                         lows.append((value - high.astype(F32)).astype(BF16))
                     right_high = jnp.concatenate(highs, axis=1)
                     right_low = jnp.concatenate(lows, axis=1)
-                    full = jnp.dot(left_all[...], right_high, preferred_element_type=F32)
-                    rest = jnp.dot(left_all[: 2 * SLOTS, :], right_low, preferred_element_type=F32)
-                    total = full[: 2 * SLOTS] + (full[2 * SLOTS :] + rest)
+                    right = jnp.concatenate([right_high, right_high, right_low, pad], axis=0)
+                    total = jnp.dot(left_all[...], right, preferred_element_type=F32)
                     for m in range(2):
                         lanes = slice(m * NS, (m + 1) * NS)
                         row = pl.ds(4 * b + first + m, SLOTS, stride=8)
@@ -244,7 +244,7 @@
             pltpu.VMEM((count + 1, NY, NZ, FLAT[1], NS), F32),
             pltpu.VMEM((count, NZ, NY * FLAT[2], NS), F32),
             pltpu.VMEM((2 * SLOTS, 512), F32),
-            pltpu.VMEM((4 * SLOTS, 512), BF16),
+            pltpu.VMEM((2 * SLOTS, 1280), BF16),
             pltpu.VMEM((count, 2, SLOTS * 8, NS), F32),
             pltpu.VMEM((count, 2, SLOTS * 8, NS), F32),
             pltpu.SemaphoreType.DMA((count, 7)),

time: 141 us -> 140 us (level)
  no operation moved by 1% of the time
where the time goes in v3:
time: 140 us
  starting transfers between devices  63.9 us (46%)
  waiting for transfers between devices  41.4 us (30%)
  Pallas kernels  17.9 us (13%)
  between operations  13.8 us (10%)
  local copies, waits for them, and re-layouts  1.8 us (1%)
    ppermute x15, waiting for transfers between devices, shift(): return lax.ppermute(value, axis, [(i, (i + step) % n) for i in range(n)])  19.4 us
    ppermute x15, starting transfers between devices, shift(): return lax.ppermute(value, axis, [(i, (i + step) % n) for i in range(n)])  16.5 us
    pallas_call x2, Pallas kernels, product(): pl.pallas_call(functools.partial(product_kernel, steps, fresh), out_shape...  14.3 us
    ppermute x1, starting transfers between devices, body(): other = lax.ppermute(own, 'core', [(0, 1), (1, 0)])  13.3 us
    ppermute x8, starting transfers between devices, turn(): lax.ppermute(value, ('y', 'core') if axis == 'y' else ('core', axis), pairs)  11.4 us
    ppermute x2, starting transfers between devices, body(): received.append(lax.ppermute(given, 'core', [(0, 1), (1, 0)]))  10.6 us
    ppermute x8, waiting for transfers between devices, turn(): lax.ppermute(value, ('y', 'core') if axis == 'y' else ('core', axis), pairs)  8.88 us
    ppermute x1, starting transfers between devices, swap_halves(): return lax.ppermute(flat, ('core', 'z'), pairs)  6.28 us
  transfers between devices with their start and end apart: 32, of which 16 were waited for; matrix products, arithmetic and copies ran while one was open for 1% of the time, Pallas kernels for 5%

profile of v3, /device:TPU:1, one launch (start us, length us, event | category | flops | bytes accessed | tf_op | source)
XLA Modules:
  0.0 139.8 jit_solution(6948233944794635510)
XLA Ops:
  6.5 6.3 %collective-permute-start = (f32[200,128]{1,0:T(8,128)}, f32[200,128]{1,0:T(8,128)S(1)}, u32[]{:S(2)}, u32[]{:S(2)}) collective-permute-start(f32[200,128]{1,0:T(8,128)} %bitcast.42), channel_id=1, source_target_pairs={{0,0},{1,1},{2,32},{3,33},{4,4},{5,5},{6,36},{7,37},{32,2},{33,3},... | collective-permute-start | bytes 307208 | tf_op jit(solution)/shard_map/ppermute | solution.py:51
  12.8 2.5 %collective-permute-done = f32[200,128]{1,0:T(8,128)S(1)} collective-permute-done((f32[200,128]{1,0:T(8,128)}, f32[200,128]{1,0:T(8,128)S(1)}, u32[]{:S(2)}, u32[]{:S(2)}) %collective-permute-start) | collective-permute-done | bytes 102432 | tf_op jit(solution)/shard_map/ppermute | solution.py:51
  15.4 1.3 collective-permute-start.5
  16.7 2.4 %collective-permute-start.3 = (f32[160,128]{1,0:T(8,128)S(1)}, f32[160,128]{1,0:T(8,128)S(1)}, u32[]{:S(2)}, u32[]{:S(2)}) collective-permute-start(f32[160,128]{1,0:T(8,128)S(1)} %slice.48), channel_id=1, source_target_pairs={{0,2},{1,3},{2,4},{3,5},{4,6},{5,7},{6,0},{7,1},{8,10},{9,11},{10,... | collective-permute-start | bytes 245768 | tf_op jit(solution)/shard_map/ppermute | solution.py:24
  19.0 3.6 %collective-permute-start.2 = (f32[160,128]{1,0:T(8,128)S(1)}, f32[160,128]{1,0:T(8,128)S(1)}, u32[]{:S(2)}, u32[]{:S(2)}) collective-permute-start(f32[160,128]{1,0:T(8,128)S(1)} %slice.48), channel_id=1, source_target_pairs={{0,7},{1,0},{2,1},{3,2},{4,3},{5,4},{6,5},{7,6},{8,15},{9,8},{10,9... | collective-permute-start | bytes 245768 | tf_op jit(solution)/shard_map/ppermute | solution.py:24
  22.6 4.2 %collective-permute-done.3 = f32[160,128]{1,0:T(8,128)S(1)} collective-permute-done((f32[160,128]{1,0:T(8,128)S(1)}, f32[160,128]{1,0:T(8,128)S(1)}, u32[]{:S(2)}, u32[]{:S(2)}) %collective-permute-start.3) | collective-permute-done | bytes 81952 | tf_op jit(solution)/shard_map/ppermute | solution.py:24
  26.9 0.4 collective-permute-done.1
  27.2 2.6 %collective-permute-start.9 = (f32[80,128]{1,0:T(8,128)S(1)}, f32[80,128]{1,0:T(8,128)S(1)}, u32[]{:S(2)}, u32[]{:S(2)}) collective-permute-start(f32[80,128]{1,0:T(8,128)S(1)} %pad_maximum_fusion.5), channel_id=1, source_target_pairs={{0,128},{64,192},{128,0},{192,64},{1,129},{65,193},{129,1},{193,65... | collective-permute-start | bytes 122888 | tf_op jit(solution)/shard_map/ppermute | solution.py:39
  29.9 1.9 %collective-permute-start.8 = (f32[160,128]{1,0:T(8,128)S(1)}, f32[160,128]{1,0:T(8,128)S(1)}, u32[]{:S(2)}, u32[]{:S(2)}) collective-permute-start(f32[160,128]{1,0:T(8,128)S(1)} %collective-permute-done.3), channel_id=1, source_target_pairs={{0,2},{1,3},{2,4},{3,5},{4,6},{5,7},{6,0},{7,1},{8,10},{9,11},{10,... | collective-permute-start | bytes 245768 | tf_op jit(solution)/shard_map/ppermute | solution.py:24
  31.8 0.9 collective-permute-start.6
  32.7 1.8 %collective-permute-start.7 = (f32[160,128]{1,0:T(8,128)S(1)}, f32[160,128]{1,0:T(8,128)S(1)}, u32[]{:S(2)}, u32[]{:S(2)}) collective-permute-start(f32[160,128]{1,0:T(8,128)S(1)} %collective-permute-done.4), channel_id=1, source_target_pairs={{0,7},{1,0},{2,1},{3,2},{4,3},{5,4},{6,5},{7,6},{8,15},{9,8},{10,9... | collective-permute-start | bytes 245768 | tf_op jit(solution)/shard_map/ppermute | solution.py:24
  34.4 2.4 %collective-permute-done.7 = f32[160,128]{1,0:T(8,128)S(1)} collective-permute-done((f32[160,128]{1,0:T(8,128)S(1)}, f32[160,128]{1,0:T(8,128)S(1)}, u32[]{:S(2)}, u32[]{:S(2)}) %collective-permute-start.7) | collective-permute-done | bytes 81952 | tf_op jit(solution)/shard_map/ppermute | solution.py:24
  37.1 2.6 %collective-permute-start.10 = (f32[8,80,128]{2,1,0:T(8,128)S(1)}, f32[8,80,128]{2,1,0:T(8,128)S(1)}, u32[]{:S(2)}, u32[]{:S(2)}) collective-permute-start(f32[8,80,128]{2,1,0:T(8,128)S(1)} %get-tuple-element.71), channel_id=1, source_target_pairs={{0,8},{8,16},{16,24},{24,0},{32,56},{40,32},{48,40},{56,48},{1,9},... | collective-permute-start | bytes 983048 | tf_op jit(solution)/shard_map/ppermute | solution.py:34
  39.6 1.5 %collective-permute-start.12 = (f32[8,80,128]{2,1,0:T(8,128)S(1)}, f32[8,80,128]{2,1,0:T(8,128)S(1)}, u32[]{:S(2)}, u32[]{:S(2)}) collective-permute-start(f32[8,80,128]{2,1,0:T(8,128)S(1)} %get-tuple-element.70), channel_id=1, source_target_pairs={{0,64},{64,128},{128,192},{192,0},{1,65},{65,129},{129,193},{193,1... | collective-permute-start | bytes 983048 | tf_op jit(solution)/shard_map/ppermute | solution.py:24
  41.1 0.2 collective-permute-start.14
  41.3 3.2 %collective-permute-done.14 = f32[160,128]{1,0:T(8,128)S(1)} collective-permute-done((f32[160,128]{1,0:T(8,128)S(1)}, f32[160,128]{1,0:T(8,128)S(1)}, u32[]{:S(2)}, u32[]{:S(2)}) %collective-permute-start.14) | collective-permute-done | bytes 81952 | tf_op jit(solution)/shard_map/ppermute | solution.py:39
  44.5 2.2 %collective-permute-done.11 = f32[8,80,128]{2,1,0:T(8,128)S(1)} collective-permute-done((f32[8,80,128]{2,1,0:T(8,128)S(1)}, f32[8,80,128]{2,1,0:T(8,128)S(1)}, u32[]{:S(2)}, u32[]{:S(2)}) %collective-permute-start.11) | collective-permute-done | bytes 327712 | tf_op jit(solution)/shard_map/ppermute | solution.py:34
  46.8 1.7 %collective-permute-start.19 = (f32[2,160,128]{2,1,0:T(8,128)S(1)}, f32[2,160,128]{2,1,0:T(8,128)S(1)}, u32[]{:S(2)}, u32[]{:S(2)}) collective-permute-start(f32[2,160,128]{2,1,0:T(8,128)S(1)} %pad_maximum_fusion.3), channel_id=1, source_target_pairs={{0,16},{8,24},{16,0},{24,8},{1,17},{9,25},{17,1},{25,9},{2,18},{10... | collective-permute-start | bytes 491528 | tf_op jit(solution)/shard_map/ppermute | solution.py:39
  48.7 1.5 %collective-permute-start.17 = (f32[4,80,128]{2,1,0:T(8,128)S(1)}, f32[4,80,128]{2,1,0:T(8,128)S(1)}, u32[]{:S(2)}, u32[]{:S(2)}) collective-permute-start(f32[4,80,128]{2,1,0:T(8,128)S(1)} %slice.42), channel_id=1, source_target_pairs={{0,64},{64,128},{128,192},{192,0},{1,65},{65,129},{129,193},{193,1... | collective-permute-start | bytes 491528 | tf_op jit(solution)/shard_map/ppermute | solution.py:24
  50.1 1.5 %collective-permute-start.16 = (f32[4,80,128]{2,1,0:T(8,128)S(1)}, f32[4,80,128]{2,1,0:T(8,128)S(1)}, u32[]{:S(2)}, u32[]{:S(2)}) collective-permute-start(f32[4,80,128]{2,1,0:T(8,128)S(1)} %slice.41), channel_id=1, source_target_pairs={{0,24},{8,0},{16,8},{24,16},{32,40},{40,48},{48,56},{56,32},{1,25}... | collective-permute-start | bytes 491528 | tf_op jit(solution)/shard_map/ppermute | solution.py:34
  51.6 1.2 collective-permute-start.15
  52.8 1.5 %collective-permute-done.19 = f32[2,160,128]{2,1,0:T(8,128)S(1)} collective-permute-done((f32[2,160,128]{2,1,0:T(8,128)S(1)}, f32[2,160,128]{2,1,0:T(8,128)S(1)}, u32[]{:S(2)}, u32[]{:S(2)}) %collective-permute-start.19) | collective-permute-done | bytes 163872 | tf_op jit(solution)/shard_map/ppermute | solution.py:39
  54.2 0.7 pad_maximum_fusion.2
  55.0 1.4 %collective-permute-done.17 = f32[4,80,128]{2,1,0:T(8,128)S(1)} collective-permute-done((f32[4,80,128]{2,1,0:T(8,128)S(1)}, f32[4,80,128]{2,1,0:T(8,128)S(1)}, u32[]{:S(2)}, u32[]{:S(2)}) %collective-permute-start.17) | collective-permute-done | bytes 163872 | tf_op jit(solution)/shard_map/ppermute | solution.py:24
  56.6 2.7 %collective-permute-start.22 = (f32[8,320,128]{2,1,0:T(8,128)S(1)}, f32[8,320,128]{2,1,0:T(8,128)S(1)}, u32[]{:S(2)}, u32[]{:S(2)}) collective-permute-start(f32[8,320,128]{2,1,0:T(8,128)S(1)} %pad_maximum_fusion.1.refs_8_), channel_id=1, source_target_pairs={{0,8},{8,16},{16,24},{24,0},{32,56},{40,32},{48,40},{56,48},{1,9},... | collective-permute-start | bytes 3932168 | tf_op jit(solution)/shard_map/ppermute | solution.py:34
  59.4 0.1 pad_maximum_fusion.refs_3_
  59.5 0.9 collective-permute-start.21
  60.5 0.6 collective-permute-start.20
  61.1 0.9 shard_map.64.refs_0_
  62.0 13.3 %collective-permute-start.24 = (f32[128,512]{1,0:T(8,128)S(1)}, f32[128,512]{1,0:T(8,128)S(1)}, u32[]{:S(2)}, u32[]{:S(2)}) collective-permute-start(f32[128,512]{1,0:T(8,128)S(1)} %shard_map.64.refs_0_), channel_id=1, source_target_pairs={{0,32},{32,0},{1,33},{33,1},{2,34},{34,2},{3,35},{35,3},{4,36},{36... | collective-permute-start | bytes 786440 | tf_op jit(solution)/shard_map/ppermute | solution.py:319
  75.2 1.2 collective-permute-done.24.refs_1_
  76.4 4.9 %collective-permute-done.23.refs_10_ = f32[8,320,128]{2,1,0:T(8,128)S(1)} collective-permute-done((f32[8,320,128]{2,1,0:T(8,128)S(1)}, f32[8,320,128]{2,1,0:T(8,128)S(1)}, u32[]{:S(2)}, u32[]{:S(2)}) %collective-permute-start.23) | collective-permute-done | bytes 1310752 | tf_op jit(solution)/shard_map/ppermute | solution.py:34
  81.3 1.7 %collective-permute-done.22.refs_9_ = f32[8,320,128]{2,1,0:T(8,128)S(1)} collective-permute-done((f32[8,320,128]{2,1,0:T(8,128)S(1)}, f32[8,320,128]{2,1,0:T(8,128)S(1)}, u32[]{:S(2)}, u32[]{:S(2)}) %collective-permute-start.22) | collective-permute-done | bytes 1310752 | tf_op jit(solution)/shard_map/ppermute | solution.py:34
  83.3 0.9 copy-done.7
  84.2 0.5 copy-done.8
  84.7 1.5 %collective-permute-start.25 = (f32[2,8,80,128]{3,2,1,0:T(8,128)S(1)}, f32[2,8,80,128]{3,2,1,0:T(8,128)S(1)}, u32[]{:S(2)}, u32[]{:S(2)}) collective-permute-start(f32[2,8,80,128]{3,2,1,0:T(8,128)S(1)} %slice.44), channel_id=1, source_target_pairs={{0,64},{64,128},{128,192},{192,0},{1,65},{65,129},{129,193},{193,1... | collective-permute-start | bytes 1966088 | tf_op jit(solution)/shard_map/ppermute | solution.py:24
  86.1 3.4 %collective-permute-start.27 = (f32[4,320,128]{2,1,0:T(8,128)S(1)}, f32[4,320,128]{2,1,0:T(8,128)S(1)}, u32[]{:S(2)}, u32[]{:S(2)}) collective-permute-start(f32[4,320,128]{2,1,0:T(8,128)S(1)} %slice.46), channel_id=1, source_target_pairs={{0,8},{8,16},{16,24},{24,0},{32,56},{40,32},{48,40},{56,48},{1,9},... | collective-permute-start | bytes 1966088 | tf_op jit(solution)/shard_map/ppermute | solution.py:34
  89.6 9.7 %collective-permute-done.26.refs_6_ = f32[2,8,80,128]{3,2,1,0:T(8,128)S(1)} collective-permute-done((f32[2,8,80,128]{3,2,1,0:T(8,128)S(1)}, f32[2,8,80,128]{3,2,1,0:T(8,128)S(1)}, u32[]{:S(2)}, u32[]{:S(2)}) %collective-permute-start.26) | collective-permute-done | bytes 655392 | tf_op jit(solution)/shard_map/ppermute | solution.py:24
  99.3 1.3 collective-permute-done.25.refs_5_
  100.6 3.6 %all-gather.3.cloned.1.call-done = f32[32,160,128]{2,1,0:T(8,128)} async-done(((f32[4,160,128]{2,1,0:T(8,128)}), f32[32,160,128]{2,1,0:T(8,128)}) %all-gather.3.cloned.1.call-update) | async-done | bytes 2621456 | tf_op jit(solution)/shard_map/all_gather | solution.py:316
  104.2 9.5 %shard_map.65 = (f32[128,128,128]{2,1,0:T(8,128)}, f32[3,2,1024,128]{3,2,1,0:T(8,128)}) custom-call(f32[128,512]{1,0:T(8,128)} %copy-done, f32[128,512]{1,0:T(8,128)} %copy-done.16, f32[8,4,160,128]{3,2,1,0:T(8,128)} %bitcast.36, f32[4,8,80,128]{3,2,1,0:T(8,128)} %copy-done.6, f32[4,8,80,128]{3,2,1,0:T(8,128)} %copy-done.8, f32[2,8,80,128]{3,2,1,0:T(8,128)} %copy-done.11, ...), custom_call_target="tpu_custom_call" | custom-call | flops 4831838208 | bytes 25165824 | tf_op jit(solution)/shard_map/pallas_call | solution.py:234
  113.6 10.5 %collective-permute-start.30 = (f32[3,2,1024,128]{3,2,1,0:T(8,128)}, f32[3,2,1024,128]{3,2,1,0:T(8,128)S(1)}, u32[]{:S(2)}, u32[]{:S(2)}) collective-permute-start(f32[3,2,1024,128]{3,2,1,0:T(8,128)} %get-tuple-element.67), channel_id=1, source_target_pairs={{0,32},{32,0},{1,33},{33,1},{2,34},{34,2},{3,35},{35,3},{4,36},{36... | collective-permute-start | bytes 9437192 | tf_op jit(solution)/shard_map/ppermute | solution.py:331
  124.1 4.9 %shard_map.66 = (f32[128,128,128]{2,1,0:T(8,128)}, f32[1,2,1024,128]{3,2,1,0:T(8,128)}) custom-call(f32[128,512]{1,0:T(8,128)} %copy-done, f32[128,512]{1,0:T(8,128)} %copy-done.16, f32[8,4,160,128]{3,2,1,0:T(8,128)} %bitcast.37, f32[4,8,80,128]{3,2,1,0:T(8,128)} %copy-done.6, f32[4,8,80,128]{3,2,1,0:T(8,128)} %copy-done.8, ...), custom_call_target="tpu_custom_call", output_to_operand_aliasing={{0}: (10, {})} | custom-call | flops 1610612736 | bytes 8388608 | tf_op jit(solution)/shard_map/pallas_call | solution.py:234
  129.0 0.1 collective-permute-start.29
  129.1 0.5 collective-permute-done.30.blocks_ref
  129.6 1.7 %shard_map.67._ = f32[128,128,128]{2,1,0:T(8,128)} custom-call(f32[3,2,1024,128]{3,2,1,0:T(8,128)S(1)} %collective-permute-done.30.blocks_ref, f32[128,128,128]{2,1,0:T(8,128)} %get-tuple-element.68._), custom_call_target="tpu_custom_call", output_to_operand_aliasing={{}: (1, {})} | custom-call | bytes 6291456 | tf_op jit(solution)/shard_map/pallas_call | solution.py:278
  131.3 0.6 collective-permute-done.29.blocks_ref
  132.0 1.0 shard_map.68
  (82 shorter events, 0.8 us)
Async XLA Ops:
  6.5 97.6 %all-gather.3.cloned.1.call-start = ((), (), s32[]{:S(2)}) async-start(), calls=%async_computation | async-start | bytes 2949120 | tf_op jit(solution)/shard_map/all_gather | solution.py:316
  6.5 8.8 %collective-permute-start = (f32[200,128]{1,0:T(8,128)}, f32[200,128]{1,0:T(8,128)S(1)}, u32[]{:S(2)}, u32[]{:S(2)}) collective-permute-start(f32[200,128]{1,0:T(8,128)} %bitcast.42), channel_id=1, source_target_pairs={{0,0},{1,1},{2,32},{3,33},{4,4},{5,5},{6,36},{7,37},{32,2},{33,3},... | collective-permute-start | bytes 307208 | tf_op jit(solution)/shard_map/ppermute | solution.py:51
  15.4 7.2 %collective-permute-start.5 = (f32[40,128]{1,0:T(8,128)S(1)}, f32[40,128]{1,0:T(8,128)S(1)}, u32[]{:S(2)}, u32[]{:S(2)}) collective-permute-start(f32[40,128]{1,0:T(8,128)S(1)} %slice.49), channel_id=1, source_target_pairs={{0,64},{64,0},{128,192},{192,128},{1,65},{65,1},{129,193},{193,129... | collective-permute-start | bytes 61448 | tf_op jit(solution)/shard_map/ppermute | solution.py:39
  16.7 5.9 %collective-permute-start.4 = (f32[160,128]{1,0:T(8,128)S(1)}, f32[160,128]{1,0:T(8,128)S(1)}, u32[]{:S(2)}, u32[]{:S(2)}) collective-permute-start(f32[160,128]{1,0:T(8,128)S(1)} %slice.48), channel_id=1, source_target_pairs={{0,6},{1,7},{2,0},{3,1},{4,2},{5,3},{6,4},{7,5},{8,14},{9,15},{10,... | collective-permute-start | bytes 245768 | tf_op jit(solution)/shard_map/ppermute | solution.py:24
  16.7 10.2 %collective-permute-start.3 = (f32[160,128]{1,0:T(8,128)S(1)}, f32[160,128]{1,0:T(8,128)S(1)}, u32[]{:S(2)}, u32[]{:S(2)}) collective-permute-start(f32[160,128]{1,0:T(8,128)S(1)} %slice.48), channel_id=1, source_target_pairs={{0,2},{1,3},{2,4},{3,5},{4,6},{5,7},{6,0},{7,1},{8,10},{9,11},{10,... | collective-permute-start | bytes 245768 | tf_op jit(solution)/shard_map/ppermute | solution.py:24
  19.0 7.8 %collective-permute-start.2 = (f32[160,128]{1,0:T(8,128)S(1)}, f32[160,128]{1,0:T(8,128)S(1)}, u32[]{:S(2)}, u32[]{:S(2)}) collective-permute-start(f32[160,128]{1,0:T(8,128)S(1)} %slice.48), channel_id=1, source_target_pairs={{0,7},{1,0},{2,1},{3,2},{4,3},{5,4},{6,5},{7,6},{8,15},{9,8},{10,9... | collective-permute-start | bytes 245768 | tf_op jit(solution)/shard_map/ppermute | solution.py:24
  22.6 4.6 %collective-permute-start.1 = (f32[160,128]{1,0:T(8,128)S(1)}, f32[160,128]{1,0:T(8,128)S(1)}, u32[]{:S(2)}, u32[]{:S(2)}) collective-permute-start(f32[160,128]{1,0:T(8,128)S(1)} %slice.48), channel_id=1, source_target_pairs={{0,1},{1,2},{2,3},{3,4},{4,5},{5,6},{6,7},{7,0},{8,9},{9,10},{10,1... | collective-permute-start | bytes 245768 | tf_op jit(solution)/shard_map/ppermute | solution.py:24
  27.2 7.2 %collective-permute-start.9 = (f32[80,128]{1,0:T(8,128)S(1)}, f32[80,128]{1,0:T(8,128)S(1)}, u32[]{:S(2)}, u32[]{:S(2)}) collective-permute-start(f32[80,128]{1,0:T(8,128)S(1)} %pad_maximum_fusion.5), channel_id=1, source_target_pairs={{0,128},{64,192},{128,0},{192,64},{1,129},{65,193},{129,1},{193,65... | collective-permute-start | bytes 122888 | tf_op jit(solution)/shard_map/ppermute | solution.py:39
  29.9 7.0 %collective-permute-start.8 = (f32[160,128]{1,0:T(8,128)S(1)}, f32[160,128]{1,0:T(8,128)S(1)}, u32[]{:S(2)}, u32[]{:S(2)}) collective-permute-start(f32[160,128]{1,0:T(8,128)S(1)} %collective-permute-done.3), channel_id=1, source_target_pairs={{0,2},{1,3},{2,4},{3,5},{4,6},{5,7},{6,0},{7,1},{8,10},{9,11},{10,... | collective-permute-start | bytes 245768 | tf_op jit(solution)/shard_map/ppermute | solution.py:24
  31.8 5.1 %collective-permute-start.6 = (f32[160,128]{1,0:T(8,128)S(1)}, f32[160,128]{1,0:T(8,128)S(1)}, u32[]{:S(2)}, u32[]{:S(2)}) collective-permute-start(f32[160,128]{1,0:T(8,128)S(1)} %collective-permute-done.3), channel_id=1, source_target_pairs={{0,1},{1,2},{2,3},{3,4},{4,5},{5,6},{6,7},{7,0},{8,9},{9,10},{10,1... | collective-permute-start | bytes 245768 | tf_op jit(solution)/shard_map/ppermute | solution.py:24
  32.7 4.2 %collective-permute-start.7 = (f32[160,128]{1,0:T(8,128)S(1)}, f32[160,128]{1,0:T(8,128)S(1)}, u32[]{:S(2)}, u32[]{:S(2)}) collective-permute-start(f32[160,128]{1,0:T(8,128)S(1)} %collective-permute-done.4), channel_id=1, source_target_pairs={{0,7},{1,0},{2,1},{3,2},{4,3},{5,4},{6,5},{7,6},{8,15},{9,8},{10,9... | collective-permute-start | bytes 245768 | tf_op jit(solution)/shard_map/ppermute | solution.py:24
  37.1 7.5 %collective-permute-start.10 = (f32[8,80,128]{2,1,0:T(8,128)S(1)}, f32[8,80,128]{2,1,0:T(8,128)S(1)}, u32[]{:S(2)}, u32[]{:S(2)}) collective-permute-start(f32[8,80,128]{2,1,0:T(8,128)S(1)} %get-tuple-element.71), channel_id=1, source_target_pairs={{0,8},{8,16},{16,24},{24,0},{32,56},{40,32},{48,40},{56,48},{1,9},... | collective-permute-start | bytes 983048 | tf_op jit(solution)/shard_map/ppermute | solution.py:34
  39.6 7.1 %collective-permute-start.11 = (f32[8,80,128]{2,1,0:T(8,128)S(1)}, f32[8,80,128]{2,1,0:T(8,128)S(1)}, u32[]{:S(2)}, u32[]{:S(2)}) collective-permute-start(f32[8,80,128]{2,1,0:T(8,128)S(1)} %get-tuple-element.71), channel_id=1, source_target_pairs={{0,24},{8,0},{16,8},{24,16},{32,40},{40,48},{48,56},{56,32},{1,25}... | collective-permute-start | bytes 983048 | tf_op jit(solution)/shard_map/ppermute | solution.py:34
  39.6 7.1 %collective-permute-start.13 = (f32[8,80,128]{2,1,0:T(8,128)S(1)}, f32[8,80,128]{2,1,0:T(8,128)S(1)}, u32[]{:S(2)}, u32[]{:S(2)}) collective-permute-start(f32[8,80,128]{2,1,0:T(8,128)S(1)} %get-tuple-element.70), channel_id=1, source_target_pairs={{0,192},{64,0},{128,64},{192,128},{1,193},{65,1},{129,65},{193,129... | collective-permute-start | bytes 983048 | tf_op jit(solution)/shard_map/ppermute | solution.py:24
  39.6 7.1 %collective-permute-start.12 = (f32[8,80,128]{2,1,0:T(8,128)S(1)}, f32[8,80,128]{2,1,0:T(8,128)S(1)}, u32[]{:S(2)}, u32[]{:S(2)}) collective-permute-start(f32[8,80,128]{2,1,0:T(8,128)S(1)} %get-tuple-element.70), channel_id=1, source_target_pairs={{0,64},{64,128},{128,192},{192,0},{1,65},{65,129},{129,193},{193,1... | collective-permute-start | bytes 983048 | tf_op jit(solution)/shard_map/ppermute | solution.py:24
  41.1 3.4 %collective-permute-start.14 = (f32[160,128]{1,0:T(8,128)S(1)}, f32[160,128]{1,0:T(8,128)S(1)}, u32[]{:S(2)}, u32[]{:S(2)}) collective-permute-start(f32[160,128]{1,0:T(8,128)S(1)} %pad_maximum_fusion.4), channel_id=1, source_target_pairs={{0,8},{8,0},{16,24},{24,16},{1,9},{9,1},{17,25},{25,17},{2,10},{10... | collective-permute-start | bytes 245768 | tf_op jit(solution)/shard_map/ppermute | solution.py:39
  46.8 7.5 %collective-permute-start.19 = (f32[2,160,128]{2,1,0:T(8,128)S(1)}, f32[2,160,128]{2,1,0:T(8,128)S(1)}, u32[]{:S(2)}, u32[]{:S(2)}) collective-permute-start(f32[2,160,128]{2,1,0:T(8,128)S(1)} %pad_maximum_fusion.3), channel_id=1, source_target_pairs={{0,16},{8,24},{16,0},{24,8},{1,17},{9,25},{17,1},{25,9},{2,18},{10... | collective-permute-start | bytes 491528 | tf_op jit(solution)/shard_map/ppermute | solution.py:39
  48.6 6.4 %collective-permute-start.18 = (f32[4,80,128]{2,1,0:T(8,128)S(1)}, f32[4,80,128]{2,1,0:T(8,128)S(1)}, u32[]{:S(2)}, u32[]{:S(2)}) collective-permute-start(f32[4,80,128]{2,1,0:T(8,128)S(1)} %slice.43), channel_id=1, source_target_pairs={{0,192},{64,0},{128,64},{192,128},{1,193},{65,1},{129,65},{193,129... | collective-permute-start | bytes 491528 | tf_op jit(solution)/shard_map/ppermute | solution.py:24
  48.7 7.8 %collective-permute-start.17 = (f32[4,80,128]{2,1,0:T(8,128)S(1)}, f32[4,80,128]{2,1,0:T(8,128)S(1)}, u32[]{:S(2)}, u32[]{:S(2)}) collective-permute-start(f32[4,80,128]{2,1,0:T(8,128)S(1)} %slice.42), channel_id=1, source_target_pairs={{0,64},{64,128},{128,192},{192,0},{1,65},{65,129},{129,193},{193,1... | collective-permute-start | bytes 491528 | tf_op jit(solution)/shard_map/ppermute | solution.py:24
  50.1 6.3 %collective-permute-start.16 = (f32[4,80,128]{2,1,0:T(8,128)S(1)}, f32[4,80,128]{2,1,0:T(8,128)S(1)}, u32[]{:S(2)}, u32[]{:S(2)}) collective-permute-start(f32[4,80,128]{2,1,0:T(8,128)S(1)} %slice.41), channel_id=1, source_target_pairs={{0,24},{8,0},{16,8},{24,16},{32,40},{40,48},{48,56},{56,32},{1,25}... | collective-permute-start | bytes 491528 | tf_op jit(solution)/shard_map/ppermute | solution.py:34
  51.6 4.8 %collective-permute-start.15 = (f32[4,80,128]{2,1,0:T(8,128)S(1)}, f32[4,80,128]{2,1,0:T(8,128)S(1)}, u32[]{:S(2)}, u32[]{:S(2)}) collective-permute-start(f32[4,80,128]{2,1,0:T(8,128)S(1)} %slice.40), channel_id=1, source_target_pairs={{0,8},{8,16},{16,24},{24,0},{32,56},{40,32},{48,40},{56,48},{1,9},... | collective-permute-start | bytes 491528 | tf_op jit(solution)/shard_map/ppermute | solution.py:34
  56.5 3.0 %copy-start.9 = (f32[8,320,128]{2,1,0:T(8,128)}, f32[8,320,128]{2,1,0:T(8,128)S(1)}, u32[]{:S(2)}) copy-start(f32[8,320,128]{2,1,0:T(8,128)S(1)} %pad_maximum_fusion.1.refs_8_) | copy-start | bytes 3932164
  56.5 24.8 %collective-permute-start.23 = (f32[8,320,128]{2,1,0:T(8,128)S(1)}, f32[8,320,128]{2,1,0:T(8,128)S(1)}, u32[]{:S(2)}, u32[]{:S(2)}) collective-permute-start(f32[8,320,128]{2,1,0:T(8,128)S(1)} %pad_maximum_fusion.1.refs_8_), channel_id=1, source_target_pairs={{0,24},{8,0},{16,8},{24,16},{32,40},{40,48},{48,56},{56,32},{1,25}... | collective-permute-start | bytes 3932168 | tf_op jit(solution)/shard_map/ppermute | solution.py:34
  56.6 26.4 %collective-permute-start.22 = (f32[8,320,128]{2,1,0:T(8,128)S(1)}, f32[8,320,128]{2,1,0:T(8,128)S(1)}, u32[]{:S(2)}, u32[]{:S(2)}) collective-permute-start(f32[8,320,128]{2,1,0:T(8,128)S(1)} %pad_maximum_fusion.1.refs_8_), channel_id=1, source_target_pairs={{0,8},{8,16},{16,24},{24,0},{32,56},{40,32},{48,40},{56,48},{1,9},... | collective-permute-start | bytes 3932168 | tf_op jit(solution)/shard_map/ppermute | solution.py:34
  59.3 1.7 %copy-start.1 = (s32[2048,8]{0,1:T(8,128)S(1)}, s32[2048,8]{0,1:T(8,128)}, u32[]{:S(2)}) copy-start(s32[2048,8]{0,1:T(8,128)} %param.7) | copy-start | bytes 196612
  59.3 1.7 %copy-start.2 = (s32[2048,8]{0,1:T(8,128)S(1)}, s32[2048,8]{0,1:T(8,128)}, u32[]{:S(2)}) copy-start(s32[2048,8]{0,1:T(8,128)} %param.8) | copy-start | bytes 196612
  59.3 1.7 %copy-start.3 = (s32[2048,8]{0,1:T(8,128)S(1)}, s32[2048,8]{0,1:T(8,128)}, u32[]{:S(2)}) copy-start(s32[2048,8]{0,1:T(8,128)} %param.9) | copy-start | bytes 196612
  59.4 1.7 %copy-start.4 = (s32[2048]{0:T(1024)S(1)}, s32[2048]{0:T(1024)}, u32[]{:S(2)}) copy-start(s32[2048]{0:T(1024)} %param.11) | copy-start | bytes 24580
  59.4 1.7 %copy-start.5 = (f32[64]{0:T(128)S(1)}, f32[64]{0:T(128)}, u32[]{:S(2)}) copy-start(f32[64]{0:T(128)} %param.10) | copy-start | bytes 772
  59.5 23.7 %copy-start.6 = (f32[4,8,80,128]{3,2,1,0:T(8,128)}, f32[4,8,80,128]{3,2,1,0:T(8,128)S(1)}, u32[]{:S(2)}) copy-start(f32[4,8,80,128]{3,2,1,0:T(8,128)S(1)} %pad_maximum_fusion.refs_3_) | copy-start | bytes 3932164
  59.5 23.6 %collective-permute-start.21 = (f32[4,8,80,128]{3,2,1,0:T(8,128)S(1)}, f32[4,8,80,128]{3,2,1,0:T(8,128)S(1)}, u32[]{:S(2)}, u32[]{:S(2)}) collective-permute-start(f32[4,8,80,128]{3,2,1,0:T(8,128)S(1)} %pad_maximum_fusion.refs_3_), channel_id=1, source_target_pairs={{0,192},{64,0},{128,64},{192,128},{1,193},{65,1},{129,65},{193,129... | collective-permute-start | bytes 3932168 | tf_op jit(solution)/shard_map/ppermute | solution.py:24
  60.5 22.6 %collective-permute-start.20 = (f32[4,8,80,128]{3,2,1,0:T(8,128)S(1)}, f32[4,8,80,128]{3,2,1,0:T(8,128)S(1)}, u32[]{:S(2)}, u32[]{:S(2)}) collective-permute-start(f32[4,8,80,128]{3,2,1,0:T(8,128)S(1)} %pad_maximum_fusion.refs_3_), channel_id=1, source_target_pairs={{0,64},{64,128},{128,192},{192,0},{1,65},{65,129},{129,193},{193,1... | collective-permute-start | bytes 3932168 | tf_op jit(solution)/shard_map/ppermute | solution.py:24
  62.0 21.2 %copy-start = (f32[128,512]{1,0:T(8,128)}, f32[128,512]{1,0:T(8,128)S(1)}, u32[]{:S(2)}) copy-start(f32[128,512]{1,0:T(8,128)S(1)} %shard_map.64.refs_0_) | copy-start | bytes 786436
  62.0 14.4 %collective-permute-start.24 = (f32[128,512]{1,0:T(8,128)S(1)}, f32[128,512]{1,0:T(8,128)S(1)}, u32[]{:S(2)}, u32[]{:S(2)}) collective-permute-start(f32[128,512]{1,0:T(8,128)S(1)} %shard_map.64.refs_0_), channel_id=1, source_target_pairs={{0,32},{32,0},{1,33},{33,1},{2,34},{34,2},{3,35},{35,3},{4,36},{36... | collective-permute-start | bytes 786440 | tf_op jit(solution)/shard_map/ppermute | solution.py:319
  76.4 27.8 %copy-start.16 = (f32[128,512]{1,0:T(8,128)}, f32[128,512]{1,0:T(8,128)S(1)}, u32[]{:S(2)}) copy-start(f32[128,512]{1,0:T(8,128)S(1)} %collective-permute-done.24.refs_1_) | copy-start | bytes 786436
  81.3 1.9 %copy-start.14 = (f32[8,320,128]{2,1,0:T(8,128)}, f32[8,320,128]{2,1,0:T(8,128)S(1)}, u32[]{:S(2)}) copy-start(f32[8,320,128]{2,1,0:T(8,128)S(1)} %collective-permute-done.23.refs_10_) | copy-start | bytes 3932164
  83.1 17.5 %copy-start.15 = (f32[8,320,128]{2,1,0:T(8,128)}, f32[8,320,128]{2,1,0:T(8,128)S(1)}, u32[]{:S(2)}) copy-start(f32[8,320,128]{2,1,0:T(8,128)S(1)} %collective-permute-done.22.refs_9_) | copy-start | bytes 3932164
  83.1 1.6 %copy-start.8 = (f32[4,8,80,128]{3,2,1,0:T(8,128)}, f32[4,8,80,128]{3,2,1,0:T(8,128)S(1)}, u32[]{:S(2)}) copy-start(f32[4,8,80,128]{3,2,1,0:T(8,128)S(1)} %collective-permute-done.20.refs_4_) | copy-start | bytes 3932164
  84.7 14.6 %collective-permute-start.26 = (f32[2,8,80,128]{3,2,1,0:T(8,128)S(1)}, f32[2,8,80,128]{3,2,1,0:T(8,128)S(1)}, u32[]{:S(2)}, u32[]{:S(2)}) collective-permute-start(f32[2,8,80,128]{3,2,1,0:T(8,128)S(1)} %slice.45), channel_id=1, source_target_pairs={{0,192},{64,0},{128,64},{192,128},{1,193},{65,1},{129,65},{193,129... | collective-permute-start | bytes 1966088 | tf_op jit(solution)/shard_map/ppermute | solution.py:24
  84.7 15.8 %collective-permute-start.25 = (f32[2,8,80,128]{3,2,1,0:T(8,128)S(1)}, f32[2,8,80,128]{3,2,1,0:T(8,128)S(1)}, u32[]{:S(2)}, u32[]{:S(2)}) collective-permute-start(f32[2,8,80,128]{3,2,1,0:T(8,128)S(1)} %slice.44), channel_id=1, source_target_pairs={{0,64},{64,128},{128,192},{192,0},{1,65},{65,129},{129,193},{193,1... | collective-permute-start | bytes 1966088 | tf_op jit(solution)/shard_map/ppermute | solution.py:24
  86.1 14.4 %collective-permute-start.28 = (f32[4,320,128]{2,1,0:T(8,128)S(1)}, f32[4,320,128]{2,1,0:T(8,128)S(1)}, u32[]{:S(2)}, u32[]{:S(2)}) collective-permute-start(f32[4,320,128]{2,1,0:T(8,128)S(1)} %slice.47), channel_id=1, source_target_pairs={{0,24},{8,0},{16,8},{24,16},{32,40},{40,48},{48,56},{56,32},{1,25}... | collective-permute-start | bytes 1966088 | tf_op jit(solution)/shard_map/ppermute | solution.py:34
  86.1 14.4 %collective-permute-start.27 = (f32[4,320,128]{2,1,0:T(8,128)S(1)}, f32[4,320,128]{2,1,0:T(8,128)S(1)}, u32[]{:S(2)}, u32[]{:S(2)}) collective-permute-start(f32[4,320,128]{2,1,0:T(8,128)S(1)} %slice.46), channel_id=1, source_target_pairs={{0,8},{8,16},{16,24},{24,0},{32,56},{40,32},{48,40},{56,48},{1,9},... | collective-permute-start | bytes 1966088 | tf_op jit(solution)/shard_map/ppermute | solution.py:34
  99.3 4.9 %copy-start.10 = (f32[2,8,80,128]{3,2,1,0:T(8,128)}, f32[2,8,80,128]{3,2,1,0:T(8,128)S(1)}, u32[]{:S(2)}) copy-start(f32[2,8,80,128]{3,2,1,0:T(8,128)S(1)} %collective-permute-done.26.refs_6_) | copy-start | bytes 1966084
  100.5 3.6 %copy-start.11 = (f32[2,8,80,128]{3,2,1,0:T(8,128)}, f32[2,8,80,128]{3,2,1,0:T(8,128)S(1)}, u32[]{:S(2)}) copy-start(f32[2,8,80,128]{3,2,1,0:T(8,128)S(1)} %collective-permute-done.25.refs_5_) | copy-start | bytes 1966084
  100.5 13.1 %copy-start.12 = (f32[4,320,128]{2,1,0:T(8,128)}, f32[4,320,128]{2,1,0:T(8,128)S(1)}, u32[]{:S(2)}) copy-start(f32[4,320,128]{2,1,0:T(8,128)S(1)} %collective-permute-done.28.refs_9_) | copy-start | bytes 1966084
  100.6 13.1 %copy-start.13 = (f32[4,320,128]{2,1,0:T(8,128)}, f32[4,320,128]{2,1,0:T(8,128)S(1)}, u32[]{:S(2)}) copy-start(f32[4,320,128]{2,1,0:T(8,128)S(1)} %collective-permute-done.27.refs_8_) | copy-start | bytes 1966084
  113.6 16.0 %collective-permute-start.30 = (f32[3,2,1024,128]{3,2,1,0:T(8,128)}, f32[3,2,1024,128]{3,2,1,0:T(8,128)S(1)}, u32[]{:S(2)}, u32[]{:S(2)}) collective-permute-start(f32[3,2,1024,128]{3,2,1,0:T(8,128)} %get-tuple-element.67), channel_id=1, source_target_pairs={{0,32},{32,0},{1,33},{33,1},{2,34},{34,2},{3,35},{35,3},{4,36},{36... | collective-permute-start | bytes 9437192 | tf_op jit(solution)/shard_map/ppermute | solution.py:331
  129.0 3.0 %collective-permute-start.29 = (f32[1,2,1024,128]{3,2,1,0:T(8,128)}, f32[1,2,1024,128]{3,2,1,0:T(8,128)S(1)}, u32[]{:S(2)}, u32[]{:S(2)}) collective-permute-start(f32[1,2,1024,128]{3,2,1,0:T(8,128)} %get-tuple-element.66), channel_id=1, source_target_pairs={{0,32},{32,0},{1,33},{33,1},{2,34},{34,2},{3,35},{35,3},{4,36},{36... | collective-permute-start | bytes 3145736 | tf_op jit(solution)/shard_map/ppermute | solution.py:331
  (1 other events, 1.1 us)
Sparse Core Ops, SparseCore 0:
  56.6 47.5 all-gather.2
